TPU v7x, 256 devices: a whole 4x4x8 slice. The times are simulated.
256 devices in a mesh: freq: 8 (over y, z_lo), brick: 32 (over x, z_hi, core).
Axes of the slice: x: 4, y: 4, z: 8 (z_hi: 4, z_lo: 2; z = z_hi * 2 + z_lo), core: 2. Of those that a mesh axis runs over, the one named last changes fastest.
Arguments:
- forward: bfloat16 [8, 4, 6, 64, 1024], P('freq', None, None, 'brick'), may hold values from -6 to 6
- adjoint: bfloat16 [8, 160, 6, 64, 1024], P('freq', None, None, 'brick'), may hold values from -8 to 8
- probes: bfloat16 [64, 1024, 128], P('brick'), may hold values from -0.0234375 to 0.0234375
- datum: int32 [8, 256], P('freq'), may hold values from 0 to 319, as said below
Outputs:
- cell_basis: float32 [128, 64, 1024], P('freq', 'brick')
Inputs may be any that keep to these rules, and one draw needn't show every extreme that they name: `datum`: the 256 codes of one group are distinct.
All inputs are finite; a program needn't handle non-finite values.
Results may differ from a plain program's by a relative error of at most 0.013.
Values may be sent and summed in bfloat16 or wider, within the bound.
No kernel may reach another device: no remote copies, remote signals or barrier semaphores. Data moves between devices by JAX's collectives and lax.ppermute only.
A program may use at most 128 MiB of HBM per device.

v0:
```python
import jax
import jax.numpy as jnp
from jax import lax
from jax.experimental import pallas as pl
from jax.experimental.pallas import tpu as pltpu
from jax.sharding import PartitionSpec as P

SITES = 40
NX = 64
ITERS = 4
PANEL = 256
PROBES = 128
SUB, LANES = 8, 128
BLOCK = 64

WHOLE = pl.BlockSpec(memory_space=pltpu.VMEM)
SCALARS = pl.BlockSpec(memory_space=pltpu.SMEM)
PARAMS = pltpu.CompilerParams(vmem_limit_bytes=40 * 1024 * 1024)


def cost(flops, size):
    return pl.CostEstimate(flops=flops, bytes_accessed=size, transcendentals=0)


def tiled(rows):
    lead = rows.shape[1:3]
    split = rows.reshape(lead + (2, SUB, LANES))
    return jnp.transpose(split, (0, 1, 3, 2, 4)).reshape(lead + (2 * SUB, LANES))


def decode(code):
    second = (code >= 4 * SITES).astype(jnp.int32)
    rest = code - second * (4 * SITES)
    fwd_row = second * 2 + (rest & 3) // 2
    adj_row = second * (2 * SITES) + rest // 4 * 2 + (rest & 1)
    return fwd_row, adj_row


def position(axis):
    return lax.broadcasted_iota(jnp.int32, (2 * SUB, LANES), axis)


def next_column(field):
    return jnp.where(position(1) % NX == NX - 1, 0.0, pltpu.roll(field, LANES - 1, 1))


def next_row(field):
    swapped = pltpu.roll(field, NX, 1)
    later = jnp.where(position(0) >= 2 * SUB - 2, 0.0, pltpu.roll(swapped, 2 * SUB - 2, 0))
    return jnp.where(position(1) < NX, swapped, later)


def edge_product(fwd, adj, fwd_row, adj_row, orientation):
    real, imag = 2 * orientation, 2 * orientation + 1

    def wide(ref, row, part):
        return ref[row, part].astype(jnp.float32)

    return wide(fwd, fwd_row, real) * wide(adj, adj_row, real) - wide(fwd, fwd_row, imag) * wide(
        adj, adj_row, imag
    )


def tile_rows(index, size):
    return pl.ds(pl.multiple_of(index * size, size), size)


def layer_rows(table, block, s, layer):
    return [
        table[pl.ds(block * 256 + half * 128 + 2 * s + layer, SUB, stride=2 * SUB), :]
        for half in range(2)
    ]


def upper_kernel(codes, fwd, adj, upper, lowest):
    def one(d, carry):
        rows = decode(codes[d])
        edge_x = edge_product(fwd, adj, *rows, 0)
        edge_y = edge_product(fwd, adj, *rows, 1)
        upper[tile_rows(d, 16), :] = edge_x + next_row(edge_x) + edge_y + next_column(edge_y)
        return carry

    lax.fori_loop(0, PANEL, one, 0, unroll=8)

    def block(i, carry):
        for s in range(SUB):
            low = jnp.concatenate(layer_rows(upper, i, s, 0), axis=0)
            lowest[s, tile_rows(i, 16), :] = low.astype(jnp.bfloat16)
        return carry

    lax.fori_loop(0, PANEL // 16, block, 0)


def side_kernel(codes, fwd, adj, upper, sens, rest, summed):
    def one(d, carry):
        edge_z = edge_product(fwd, adj, *decode(codes[d]), 0)
        paired = edge_z + next_column(edge_z)
        here = upper[tile_rows(d, 16), :]
        above = jnp.where(position(0) % 2 == 0, pltpu.roll(here, 2 * SUB - 1, 0), 0.0)
        summed[tile_rows(d, 16), :] = here + above + (paired + next_row(paired))
        return carry

    lax.fori_loop(0, PANEL, one, 0, unroll=8)

    def block(i, carry):
        for s in range(SUB):
            low = jnp.concatenate(layer_rows(summed, i, s, 0), axis=0)
            sens[s, tile_rows(i, 16), :] = (0.25 * low).astype(jnp.bfloat16)
            high = layer_rows(summed, i, s, 1)
            rest[s, tile_rows(2 * i, SUB), :] = high[0]
            rest[s, tile_rows(2 * i + 1, SUB), :] = high[1]
        return carry

    lax.fori_loop(0, PANEL // 16, block, 0)


def dot(left, right, left_dim, right_dim, precision=None):
    return lax.dot_general(
        left,
        right,
        (((left_dim,), (right_dim,)), ((), ())),
        precision=precision,
        preferred_element_type=jnp.float32,
    )


def layer_sums(sens, probes, layer):
    cross, sketch = 0.0, 0.0
    for s in range(0, SUB, 2):
        pair = jnp.concatenate([sens[s], sens[s + 1]], axis=1)
        cross = cross + dot(pair, pair, 1, 1)
        sketch = sketch + dot(probes[layer, 128 * s : 128 * s + 256, :], pair, 0, 1)
    return [cross[:128, :128], cross[:128, 128:], cross[128:, 128:], sketch[:, :128], sketch[:, 128:]]


def low_sums_kernel(sens, probes, table):
    for i, part in enumerate(layer_sums(sens, probes, 0)):
        table[128 * i : 128 * i + 128, :] = part


def high_sums_kernel(rest, above, probes, low_table, sens, table):
    def block(i, carry):
        for s in range(SUB):
            here = (s, tile_rows(i, 16), slice(None))
            sens[here] = (0.25 * (rest[here] + above[here].astype(jnp.float32))).astype(jnp.bfloat16)
        return carry

    lax.fori_loop(0, PANEL // 16, block, 0)
    for i, part in enumerate(layer_sums(sens, probes, 1)):
        at = slice(128 * i, 128 * i + 128)
        table[at, :] = low_table[at, :] + part


def spread(column):
    return jnp.broadcast_to(column, (SUB, LANES))


def eliminate(work):
    row = lax.broadcasted_iota(jnp.int32, (SUB, LANES), 0)
    groups = BLOCK // SUB
    for start in range(0, PROBES, BLOCK):
        m = [
            [work[start + SUB * g : start + SUB * g + SUB, h * 128 : h * 128 + 128] for h in range(2)]
            for g in range(groups)
        ]
        for g in range(groups):
            at = start + SUB * g
            column = {
                (q, k): spread(m[q][0][:, at + k : at + k + 1])
                for q in range(g, groups)
                for k in range(SUB)
            }
            u = {(i, k): spread(column[g, k][i : i + 1, :]) for k in range(SUB) for i in range(k + 1)}
            root = []
            for k in range(SUB):
                root.append(lax.rsqrt(u[k, k]))
                for j in range(k + 1, SUB):
                    u[k, j] = u[k, j] * root[k]
                for j in range(k + 1, SUB):
                    for i in range(k + 1, j + 1):
                        u[i, j] = u[i, j] - u[k, i] * u[k, j]
            lead = [[spread(m[g][h][k : k + 1, :]) for h in range(2)] for k in range(SUB)]
            for k in range(SUB):
                for h in range(2):
                    for j in range(k):
                        lead[k][h] = lead[k][h] - u[j, k] * lead[j][h]
                    lead[k][h] = lead[k][h] * root[k]
            for h in range(2):
                m[g][h] = lead[0][h]
                for k in range(1, SUB):
                    m[g][h] = jnp.where(row == k, lead[k][h], m[g][h])
            for q in range(g + 1, groups):
                low = []
                for k in range(SUB):
                    entry = column[q, k]
                    for j in range(k):
                        entry = entry - low[j] * u[j, k]
                    low.append(entry * root[k])
                for h in range(2):
                    for k in range(SUB):
                        m[q][h] = m[q][h] - low[k] * lead[k][h]
        for g in range(groups):
            for h in range(2):
                work[start + SUB * g : start + SUB * g + SUB, h * 128 : h * 128 + 128] = m[g][h]
        if start + BLOCK < PROBES:
            done = work[start : start + BLOCK, :]
            change = dot(done[:, :PROBES], done, 0, 0, lax.Precision.HIGHEST)
            work[start + BLOCK :, :] = work[start + BLOCK :, :] - change[start + BLOCK :, :]


def basis_kernel(table, sens_low, sens_high, parts, work, sketch, cross):
    highest = lax.Precision.HIGHEST
    corner = table[128:256, :]
    cross[0:128, 0:128] = table[0:128, :]
    cross[0:128, 128:256] = corner
    cross[128:256, 0:128] = corner.T
    cross[128:256, 128:256] = table[256:384, :]
    sketch[:, 0:128] = table[384:512, :]
    sketch[:, 128:256] = table[512:640, :]
    identity = jnp.where(
        lax.broadcasted_iota(jnp.int32, (PROBES, PROBES), 0)
        == lax.broadcasted_iota(jnp.int32, (PROBES, PROBES), 1),
        1.0,
        0.0,
    )

    def orthonormalize(step, carry):
        rows = sketch[...]
        work[:, 0:128] = dot(rows, rows, 1, 1, highest)
        work[:, 128:256] = identity
        eliminate(work)

        @pl.when(step < ITERS)
        def _():
            moved = dot(sketch[...], cross[...], 1, 0, highest)
            sketch[...] = dot(work[:, 128:256], moved, 1, 0, highest)

        return carry

    lax.fori_loop(0, ITERS + 1, orthonormalize, 0)
    basis = dot(work[:, 128:256], sketch[...], 1, 0, highest).astype(jnp.bfloat16)
    for layer, sens in enumerate((sens_low, sens_high)):
        for s in range(SUB):
            at = 1024 * layer + 128 * s
            parts[:, at : at + 128] = dot(basis, sens[s], 1, 0).astype(jnp.bfloat16)


def brick_moves(step):
    devices = lax.axis_size("brick")
    return [(i, step(i)) for i in range(devices)]


def coordinates(index):
    return index // 8, index // 2 % 4, index % 2


def along_x(k):
    return brick_moves(lambda i: (i + 8 * k) % 32)


def along_z(k):
    return brick_moves(lambda i: i // 8 * 8 + (i % 8 + 2 * k) % 8)


def across_cores():
    return brick_moves(lambda i: i ^ 1)


def pick(parts, index):
    return lax.dynamic_index_in_dim(parts, index, 0, keepdims=False)


def scattered_sum(parts, place, moves):
    count = len(moves) + 1
    got = [lax.ppermute(pick(parts, (place + k) % count), "brick", moves[k - 1]) for k in range(1, count)]
    total = pick(parts, place)
    for part in got:
        total = total + part
    return total


def gathered(part, place, moves):
    count = len(moves) + 1
    got = [part] + [lax.ppermute(part, "brick", move) for move in moves]
    back = jnp.stack((got[::-1] + got[::-1]))
    return lax.dynamic_slice_in_dim(back, (count - 1 - place) % count, count, 0)


def brick_sum(table):
    x, z, core = coordinates(lax.axis_index("brick"))
    x_moves = [along_x(k) for k in (1, 2, 3)]
    part = scattered_sum(table.reshape(2, -1, 128), core, [across_cores()])
    part = scattered_sum(part.reshape(4, -1, 128), x, x_moves)
    got = [part] + [lax.ppermute(part, "brick", along_z(k)) for k in (1, 2, 3)]
    ring = jnp.stack(got[::-1] + got[::-1])
    ring = lax.dynamic_slice_in_dim(ring, (3 - z) % 4, 4, 0)
    part = (ring[0] + ring[1]) + (ring[2] + ring[3])
    part = gathered(part, x, x_moves).reshape(-1, 128)
    return gathered(part, core, [across_cores()]).reshape(table.shape)


def shape(*dims, dtype=jnp.float32):
    return jax.ShapeDtypeStruct(dims, dtype)


def field_rows(count, parts, at):
    return pl.BlockSpec((count, parts, 16, LANES), lambda i: (0, at, 0, 0))


def whole(*dims):
    return pl.BlockSpec(dims, lambda i: (0,) * len(dims))


def local(forward, adjoint, probes, datum):
    fwd, adj, codes = tiled(forward), tiled(adjoint), datum[0]
    layer = (SUB, PANEL, LANES)
    upper, lowest = pl.pallas_call(
        upper_kernel,
        grid=(1,),
        in_specs=[SCALARS, field_rows(4, 4, 0), field_rows(160, 4, 0)],
        out_specs=(whole(PANEL * 16, LANES), whole(*layer)),
        out_shape=(shape(PANEL * 16, LANES), shape(*layer, dtype=jnp.bfloat16)),
        compiler_params=PARAMS,
        cost_estimate=cost(20_000_000, 6_000_000),
        name="upper",
    )(codes, fwd, adj)
    devices = range(lax.axis_size("brick"))
    above = lax.ppermute(lowest, "brick", [(i + 1, i) for i in devices if i + 1 in devices])
    sens_low, rest = pl.pallas_call(
        side_kernel,
        grid=(1,),
        in_specs=[SCALARS, field_rows(4, 2, 2), field_rows(160, 2, 2), whole(PANEL * 16, LANES)],
        out_specs=(whole(*layer), whole(*layer)),
        out_shape=(shape(*layer, dtype=jnp.bfloat16), shape(*layer)),
        scratch_shapes=[pltpu.VMEM((PANEL * 16, LANES), jnp.float32)],
        compiler_params=PARAMS,
        cost_estimate=cost(20_000_000, 30_000_000),
        name="side",
    )(codes, fwd, adj, upper)
    low_table = pl.pallas_call(
        low_sums_kernel,
        in_specs=[WHOLE] * 2,
        out_specs=WHOLE,
        out_shape=shape(640, 128),
        compiler_params=PARAMS,
        cost_estimate=cost(200_000_000, 3_000_000),
        name="low_sums",
    )(sens_low, probes)
    sens_high, table = pl.pallas_call(
        high_sums_kernel,
        in_specs=[WHOLE] * 4,
        out_specs=(WHOLE, WHOLE),
        out_shape=(shape(*layer, dtype=jnp.bfloat16), shape(640, 128)),
        compiler_params=PARAMS,
        cost_estimate=cost(200_000_000, 3_000_000),
        name="high_sums",
    )(rest, above, probes, low_table)
    table = brick_sum(table)
    parts = pl.pallas_call(
        basis_kernel,
        in_specs=[WHOLE] * 3,
        out_specs=WHOLE,
        out_shape=shape(PROBES, 2048, dtype=jnp.bfloat16),
        scratch_shapes=[
            pltpu.VMEM((PROBES, 2 * PROBES), jnp.float32),
            pltpu.VMEM((PROBES, PANEL), jnp.float32),
            pltpu.VMEM((PANEL, PANEL), jnp.float32),
        ],
        compiler_params=PARAMS,
        cost_estimate=cost(400_000_000, 60_000_000),
        name="basis",
    )(table, sens_low, sens_high)
    parts = lax.all_to_all(parts.reshape(8, 16, 2048), "freq", 0, 0)
    return parts.astype(jnp.float32).sum(0).reshape(16, 2, 1024)


def solution(mesh):
    return jax.shard_map(
        local,
        mesh=mesh,
        in_specs=(
            P("freq", None, None, "brick", None),
            P("freq", None, None, "brick", None),
            P("brick", None, None),
            P("freq", None),
        ),
        out_specs=P("freq", "brick", None),
        check_vma=False,
    )
```

profile of v0, /device:TPU:1, one launch (start us, length us, event | category | flops | bytes accessed | tf_op | source)
XLA Modules:
  0.0 106.3 jit_solution(6676420341719216826)
XLA Ops:
  0.0 0.0 copy-start.6
  0.0 0.0 copy-start
  0.0 2.1 %copy-done = bf16[1,160,6,2,1024]{4,3,2,1,0:T(2,128)(2,1)S(1)} copy-done((bf16[1,160,6,2,1024]{4,3,2,1,0:T(2,128)(2,1)S(1)}, bf16[1,160,6,2,1024]{4,3,2,1,0:T(2,128)(2,1)}, u32[]{:S(2)}) %copy-start) | copy-done | bytes 3932184
  2.1 0.0 copy-start.3
  2.1 0.9 copy-done.3
  3.0 0.0 copy-start.5
  3.0 0.7 copy-done.5
  3.7 0.0 copy-start.4
  3.7 0.0 copy-start.2
  3.7 7.5 %upper.1 = (f32[4096,128]{1,0:T(8,128)S(1)}, bf16[8,256,128]{2,1,0:T(8,128)(2,1)}) custom-call(s32[256]{0:T(256)S(1)} %bitcast.65, bf16[4,6,16,128]{3,2,1,0:T(8,128)(2,1)S(1)} %bitcast.61, bf16[160,6,16,128]{3,2,1,0:T(8,128)(2,1)S(1)} %bitcast.57), custom_call_target="tpu_custom_call" | custom-call | flops 20000000 | bytes 6000000 | tf_op jit(solution)/shard_map/upper/pallas_call | solution.py:317
  11.2 5.1 %collective-permute-start = (bf16[8,256,128]{2,1,0:T(8,128)(2,1)}, bf16[8,256,128]{2,1,0:T(8,128)(2,1)}, u32[]{:S(2)}, u32[]{:S(2)}) collective-permute-start(bf16[8,256,128]{2,1,0:T(8,128)(2,1)} %get-tuple-element.13), channel_id=1, source_target_pairs={{1,0},{2,1},{3,2},{4,3},{5,4},{6,5},{7,6},{8,7},{9,8},{10,9},{11,1... | collective-permute-start | bytes 1572872 | tf_op jit(solution)/shard_map/ppermute | solution.py:328
  16.4 0.0 copy-done.6
  16.4 0.0 copy-done.4
  16.4 0.0 copy-start.1
  16.4 2.1 %copy-done.1 = bf16[1,160,6,2,1024]{4,3,2,1,0:T(2,128)(2,1)S(1)} copy-done((bf16[1,160,6,2,1024]{4,3,2,1,0:T(2,128)(2,1)S(1)}, bf16[1,160,6,2,1024]{4,3,2,1,0:T(2,128)(2,1)}, u32[]{:S(2)}) %copy-start.1) | copy-done | bytes 3932184
  18.5 8.7 %side.1 = (bf16[8,256,128]{2,1,0:T(8,128)(2,1)S(1)}, f32[8,256,128]{2,1,0:T(8,128)S(1)}) custom-call(s32[256]{0:T(256)S(1)} %bitcast.66, bf16[4,6,16,128]{3,2,1,0:T(8,128)(2,1)S(1)} %bitcast.62, bf16[160,6,16,128]{3,2,1,0:T(8,128)(2,1)S(1)} %bitcast.58, f32[4096,128]{1,0:T(8,128)S(1)} %get-tuple-element.11.upper), custom_call_target="tpu_custom_call" | custom-call | flops 20000000 | bytes 30000000 | tf_op jit(solution)/shard_map/side/pallas_call | solution.py:329
  27.2 0.0 copy-done.2
  27.2 0.5 low_sums.1.low_table
  27.7 2.6 %collective-permute-done.above = bf16[8,256,128]{2,1,0:T(8,128)(2,1)} collective-permute-done((bf16[8,256,128]{2,1,0:T(8,128)(2,1)}, bf16[8,256,128]{2,1,0:T(8,128)(2,1)}, u32[]{:S(2)}, u32[]{:S(2)}) %collective-permute-start) | collective-permute-done | bytes 524320 | tf_op jit(solution)/shard_map/ppermute | solution.py:328
  30.3 1.7 %high_sums.1 = (bf16[8,256,128]{2,1,0:T(8,128)(2,1)S(1)}, f32[640,128]{1,0:T(8,128)S(1)}) custom-call(f32[8,256,128]{2,1,0:T(8,128)S(1)} %get-tuple-element.12.rest, bf16[8,256,128]{2,1,0:T(8,128)(2,1)} %collective-permute-done.above, bf16[2,1024,128]{2,1,0:T(8,128)(2,1)S(1)} %copy-done.2, f32[640,128]{1,0:T(8,128)S(1)} %low_sums.1.low_table), custom_call_target="tpu_custom_call" | custom-call | flops 200000000 | bytes 3000000 | tf_op jit(solution)/shard_map/high_sums/pallas_call | solution.py:349
  32.0 0.1 collective-permute-start.1
  32.2 1.3 %collective-permute-done.1 = f32[320,128]{1,0:T(8,128)S(1)} collective-permute-done((f32[320,128]{1,0:T(8,128)S(1)}, f32[320,128]{1,0:T(8,128)S(1)}, u32[]{:S(2)}, u32[]{:S(2)}) %collective-permute-start.1) | collective-permute-done | bytes 163872 | tf_op jit(solution)/shard_map/ppermute | solution.py:275
  33.6 5.2 %collective-permute-start.4 = (f32[80,128]{1,0:T(8,128)S(1)}, f32[80,128]{1,0:T(8,128)S(1)}, u32[]{:S(2)}, u32[]{:S(2)}) collective-permute-start(f32[80,128]{1,0:T(8,128)S(1)} %get-tuple-element.18), channel_id=1, source_target_pairs={{0,24},{1,25},{2,26},{3,27},{4,28},{5,29},{6,30},{7,31},{8,0},{9,1... | collective-permute-start | bytes 122888 | tf_op jit(solution)/shard_map/ppermute | solution.py:275
  38.7 0.2 collective-permute-start.3
  39.0 0.6 collective-permute-start.2
  39.6 0.3 collective-permute-done.4
  39.8 3.4 %collective-permute-done.3 = f32[80,128]{1,0:T(8,128)S(1)} collective-permute-done((f32[80,128]{1,0:T(8,128)S(1)}, f32[80,128]{1,0:T(8,128)S(1)}, u32[]{:S(2)}, u32[]{:S(2)}) %collective-permute-start.3) | collective-permute-done | bytes 40992 | tf_op jit(solution)/shard_map/ppermute | solution.py:275
  43.2 0.3 collective-permute-done.2
  43.5 4.5 %collective-permute-start.5 = (f32[80,128]{1,0:T(8,128)S(1)}, f32[80,128]{1,0:T(8,128)S(1)}, u32[]{:S(2)}, u32[]{:S(2)}) collective-permute-start(f32[80,128]{1,0:T(8,128)S(1)} %fusion.5), channel_id=1, source_target_pairs={{0,6},{1,7},{2,0},{3,1},{4,2},{5,3},{6,4},{7,5},{8,14},{9,15},{10,... | collective-permute-start | bytes 122888 | tf_op jit(solution)/shard_map/ppermute | solution.py:294
  48.0 0.5 collective-permute-start.6
  48.5 1.7 %collective-permute-start.7 = (f32[80,128]{1,0:T(8,128)S(1)}, f32[80,128]{1,0:T(8,128)S(1)}, u32[]{:S(2)}, u32[]{:S(2)}) collective-permute-start(f32[80,128]{1,0:T(8,128)S(1)} %fusion.5), channel_id=1, source_target_pairs={{0,2},{1,3},{2,4},{3,5},{4,6},{5,7},{6,0},{7,1},{8,10},{9,11},{10,... | collective-permute-start | bytes 122888 | tf_op jit(solution)/shard_map/ppermute | solution.py:294
  50.2 0.0 collective-permute-done.5
  50.2 4.8 %collective-permute-done.6 = f32[80,128]{1,0:T(8,128)S(1)} collective-permute-done((f32[80,128]{1,0:T(8,128)S(1)}, f32[80,128]{1,0:T(8,128)S(1)}, u32[]{:S(2)}, u32[]{:S(2)}) %collective-permute-start.6) | collective-permute-done | bytes 40992 | tf_op jit(solution)/shard_map/ppermute | solution.py:294
  55.0 0.0 collective-permute-done.7
  55.1 0.4 collective-permute-start.8
  55.5 1.4 %collective-permute-start.9 = (f32[80,128]{1,0:T(8,128)S(1)}, f32[80,128]{1,0:T(8,128)S(1)}, u32[]{:S(2)}, u32[]{:S(2)}) collective-permute-start(f32[80,128]{1,0:T(8,128)S(1)} %fusion.6), channel_id=1, source_target_pairs={{0,16},{1,17},{2,18},{3,19},{4,20},{5,21},{6,22},{7,23},{8,24},{9,... | collective-permute-start | bytes 122888 | tf_op jit(solution)/shard_map/ppermute | solution.py:284
  56.9 0.0 collective-permute-start.10
  56.9 1.1 %collective-permute-done.8 = f32[80,128]{1,0:T(8,128)S(1)} collective-permute-done((f32[80,128]{1,0:T(8,128)S(1)}, f32[80,128]{1,0:T(8,128)S(1)}, u32[]{:S(2)}, u32[]{:S(2)}) %collective-permute-start.8) | collective-permute-done | bytes 40992 | tf_op jit(solution)/shard_map/ppermute | solution.py:284
  58.1 1.8 %collective-permute-done.9 = f32[80,128]{1,0:T(8,128)S(1)} collective-permute-done((f32[80,128]{1,0:T(8,128)S(1)}, f32[80,128]{1,0:T(8,128)S(1)}, u32[]{:S(2)}, u32[]{:S(2)}) %collective-permute-start.9) | collective-permute-done | bytes 40992 | tf_op jit(solution)/shard_map/ppermute | solution.py:284
  59.9 1.1 %collective-permute-done.10 = f32[80,128]{1,0:T(8,128)S(1)} collective-permute-done((f32[80,128]{1,0:T(8,128)S(1)}, f32[80,128]{1,0:T(8,128)S(1)}, u32[]{:S(2)}, u32[]{:S(2)}) %collective-permute-start.10) | collective-permute-done | bytes 40992 | tf_op jit(solution)/shard_map/ppermute | solution.py:284
  61.1 4.7 %collective-permute-start.11 = (f32[320,128]{1,0:T(8,128)S(1)}, f32[320,128]{1,0:T(8,128)S(1)}, u32[]{:S(2)}, u32[]{:S(2)}) collective-permute-start(f32[320,128]{1,0:T(8,128)S(1)} %bitcast.69), channel_id=1, source_target_pairs={{0,1},{1,0},{2,3},{3,2},{4,5},{5,4},{6,7},{7,6},{8,9},{9,8},{10,11... | collective-permute-start | bytes 491528 | tf_op jit(solution)/shard_map/ppermute | solution.py:284
  65.8 1.0 collective-permute-done.11
  66.8 0.1 fusion.2
  66.9 25.4 %basis.1 = bf16[128,2048]{1,0:T(8,128)(2,1)S(1)} custom-call(f32[640,128]{1,0:T(8,128)S(1)} %bitcast.60, bf16[8,256,128]{2,1,0:T(8,128)(2,1)S(1)} %get-tuple-element.14.sens.sens_low, bf16[8,256,128]{2,1,0:T(8,128)(2,1)S(1)} %get-tuple-element.16.sens_high), custom_call_target="tpu_custom_call" | custom-call | flops 400000000 | bytes 60000000 | tf_op jit(solution)/shard_map/basis/pallas_call | solution.py:359
  92.3 13.2 %all_to_all.5 = bf16[8,16,2048]{2,1,0:T(8,128)(2,1)S(1)} all-to-all(bf16[8,16,2048]{2,1,0:T(8,128)(2,1)S(1)} %bitcast.59), channel_id=1, replica_groups=mesh['freq'=8,'brick'=32] {'freq'}, dimensions={0} | all-to-all | bytes 1048576 | tf_op jit(solution)/shard_map/all_to_all | solution.py:373
  105.4 0.1 convert_reduce_fusion
  105.5 0.8 reshape.42
  (22 shorter events, 0.2 us)
Async XLA Ops:
  0.0 16.4 %copy-start.6 = (s32[1,256]{1,0:T(1,128)S(1)}, s32[1,256]{1,0:T(1,128)}, u32[]{:S(2)}) copy-start(s32[1,256]{1,0:T(1,128)} %param.7) | copy-start | bytes 3076
  0.0 2.1 %copy-start = (bf16[1,160,6,2,1024]{4,3,2,1,0:T(2,128)(2,1)S(1)}, bf16[1,160,6,2,1024]{4,3,2,1,0:T(2,128)(2,1)}, u32[]{:S(2)}) copy-start(bf16[1,160,6,2,1024]{4,3,2,1,0:T(2,128)(2,1)} %param.5) | copy-start | bytes 11796484
  2.1 0.9 copy-start.3
  3.0 0.7 copy-start.5
  3.7 12.7 %copy-start.4 = (bf16[1,4,6,2,1024]{4,3,2,1,0:T(2,128)(2,1)S(1)}, bf16[1,4,6,2,1024]{4,3,2,1,0:T(2,128)(2,1)}, u32[]{:S(2)}) copy-start(bf16[1,4,6,2,1024]{4,3,2,1,0:T(2,128)(2,1)} %param.4) | copy-start | bytes 294916
  3.7 23.5 %copy-start.2 = (bf16[2,1024,128]{2,1,0:T(8,128)(2,1)S(1)}, bf16[2,1024,128]{2,1,0:T(8,128)(2,1)}, u32[]{:S(2)}) copy-start(bf16[2,1024,128]{2,1,0:T(8,128)(2,1)} %probes.3) | copy-start | bytes 1572868
  11.2 19.1 %collective-permute-start = (bf16[8,256,128]{2,1,0:T(8,128)(2,1)}, bf16[8,256,128]{2,1,0:T(8,128)(2,1)}, u32[]{:S(2)}, u32[]{:S(2)}) collective-permute-start(bf16[8,256,128]{2,1,0:T(8,128)(2,1)} %get-tuple-element.13), channel_id=1, source_target_pairs={{1,0},{2,1},{3,2},{4,3},{5,4},{6,5},{7,6},{8,7},{9,8},{10,9},{11,1... | collective-permute-start | bytes 1572872 | tf_op jit(solution)/shard_map/ppermute | solution.py:328
  16.4 2.1 %copy-start.1 = (bf16[1,160,6,2,1024]{4,3,2,1,0:T(2,128)(2,1)S(1)}, bf16[1,160,6,2,1024]{4,3,2,1,0:T(2,128)(2,1)}, u32[]{:S(2)}) copy-start(bf16[1,160,6,2,1024]{4,3,2,1,0:T(2,128)(2,1)} %param.5) | copy-start | bytes 11796484
  32.0 1.5 %collective-permute-start.1 = (f32[320,128]{1,0:T(8,128)S(1)}, f32[320,128]{1,0:T(8,128)S(1)}, u32[]{:S(2)}, u32[]{:S(2)}) collective-permute-start(f32[320,128]{1,0:T(8,128)S(1)} %dynamic-slice_bitcast_fusion), channel_id=1, source_target_pairs={{0,1},{1,0},{2,3},{3,2},{4,5},{5,4},{6,7},{7,6},{8,9},{9,8},{10,11... | collective-permute-start | bytes 491528 | tf_op jit(solution)/shard_map/ppermute | solution.py:275
  33.6 6.3 %collective-permute-start.4 = (f32[80,128]{1,0:T(8,128)S(1)}, f32[80,128]{1,0:T(8,128)S(1)}, u32[]{:S(2)}, u32[]{:S(2)}) collective-permute-start(f32[80,128]{1,0:T(8,128)S(1)} %get-tuple-element.18), channel_id=1, source_target_pairs={{0,24},{1,25},{2,26},{3,27},{4,28},{5,29},{6,30},{7,31},{8,0},{9,1... | collective-permute-start | bytes 122888 | tf_op jit(solution)/shard_map/ppermute | solution.py:275
  38.7 4.5 %collective-permute-start.3 = (f32[80,128]{1,0:T(8,128)S(1)}, f32[80,128]{1,0:T(8,128)S(1)}, u32[]{:S(2)}, u32[]{:S(2)}) collective-permute-start(f32[80,128]{1,0:T(8,128)S(1)} %get-tuple-element.19), channel_id=1, source_target_pairs={{0,16},{1,17},{2,18},{3,19},{4,20},{5,21},{6,22},{7,23},{8,24},{9,... | collective-permute-start | bytes 122888 | tf_op jit(solution)/shard_map/ppermute | solution.py:275
  39.0 4.5 %collective-permute-start.2 = (f32[80,128]{1,0:T(8,128)S(1)}, f32[80,128]{1,0:T(8,128)S(1)}, u32[]{:S(2)}, u32[]{:S(2)}) collective-permute-start(f32[80,128]{1,0:T(8,128)S(1)} %get-tuple-element.17), channel_id=1, source_target_pairs={{0,8},{1,9},{2,10},{3,11},{4,12},{5,13},{6,14},{7,15},{8,16},{9,17... | collective-permute-start | bytes 122888 | tf_op jit(solution)/shard_map/ppermute | solution.py:275
  43.5 6.8 %collective-permute-start.5 = (f32[80,128]{1,0:T(8,128)S(1)}, f32[80,128]{1,0:T(8,128)S(1)}, u32[]{:S(2)}, u32[]{:S(2)}) collective-permute-start(f32[80,128]{1,0:T(8,128)S(1)} %fusion.5), channel_id=1, source_target_pairs={{0,6},{1,7},{2,0},{3,1},{4,2},{5,3},{6,4},{7,5},{8,14},{9,15},{10,... | collective-permute-start | bytes 122888 | tf_op jit(solution)/shard_map/ppermute | solution.py:294
  48.0 7.0 %collective-permute-start.6 = (f32[80,128]{1,0:T(8,128)S(1)}, f32[80,128]{1,0:T(8,128)S(1)}, u32[]{:S(2)}, u32[]{:S(2)}) collective-permute-start(f32[80,128]{1,0:T(8,128)S(1)} %fusion.5), channel_id=1, source_target_pairs={{0,4},{1,5},{2,6},{3,7},{4,0},{5,1},{6,2},{7,3},{8,12},{9,13},{10,... | collective-permute-start | bytes 122888 | tf_op jit(solution)/shard_map/ppermute | solution.py:294
  48.5 6.5 %collective-permute-start.7 = (f32[80,128]{1,0:T(8,128)S(1)}, f32[80,128]{1,0:T(8,128)S(1)}, u32[]{:S(2)}, u32[]{:S(2)}) collective-permute-start(f32[80,128]{1,0:T(8,128)S(1)} %fusion.5), channel_id=1, source_target_pairs={{0,2},{1,3},{2,4},{3,5},{4,6},{5,7},{6,0},{7,1},{8,10},{9,11},{10,... | collective-permute-start | bytes 122888 | tf_op jit(solution)/shard_map/ppermute | solution.py:294
  55.1 2.9 %collective-permute-start.8 = (f32[80,128]{1,0:T(8,128)S(1)}, f32[80,128]{1,0:T(8,128)S(1)}, u32[]{:S(2)}, u32[]{:S(2)}) collective-permute-start(f32[80,128]{1,0:T(8,128)S(1)} %fusion.6), channel_id=1, source_target_pairs={{0,24},{1,25},{2,26},{3,27},{4,28},{5,29},{6,30},{7,31},{8,0},{9,1... | collective-permute-start | bytes 122888 | tf_op jit(solution)/shard_map/ppermute | solution.py:284
  55.5 4.4 %collective-permute-start.9 = (f32[80,128]{1,0:T(8,128)S(1)}, f32[80,128]{1,0:T(8,128)S(1)}, u32[]{:S(2)}, u32[]{:S(2)}) collective-permute-start(f32[80,128]{1,0:T(8,128)S(1)} %fusion.6), channel_id=1, source_target_pairs={{0,16},{1,17},{2,18},{3,19},{4,20},{5,21},{6,22},{7,23},{8,24},{9,... | collective-permute-start | bytes 122888 | tf_op jit(solution)/shard_map/ppermute | solution.py:284
  56.9 4.1 %collective-permute-start.10 = (f32[80,128]{1,0:T(8,128)S(1)}, f32[80,128]{1,0:T(8,128)S(1)}, u32[]{:S(2)}, u32[]{:S(2)}) collective-permute-start(f32[80,128]{1,0:T(8,128)S(1)} %fusion.6), channel_id=1, source_target_pairs={{0,8},{1,9},{2,10},{3,11},{4,12},{5,13},{6,14},{7,15},{8,16},{9,17... | collective-permute-start | bytes 122888 | tf_op jit(solution)/shard_map/ppermute | solution.py:284
  61.1 5.7 %collective-permute-start.11 = (f32[320,128]{1,0:T(8,128)S(1)}, f32[320,128]{1,0:T(8,128)S(1)}, u32[]{:S(2)}, u32[]{:S(2)}) collective-permute-start(f32[320,128]{1,0:T(8,128)S(1)} %bitcast.69), channel_id=1, source_target_pairs={{0,1},{1,0},{2,3},{3,2},{4,5},{5,4},{6,7},{7,6},{8,9},{9,8},{10,11... | collective-permute-start | bytes 491528 | tf_op jit(solution)/shard_map/ppermute | solution.py:284
where the time goes:
time: 107 us; the launch traced here: 106 us
  Pallas kernels  43.7 us (41%)
  starting transfers between devices  24.5 us (23%)
  waiting for transfers between devices  17.6 us (16%)
  blocking collectives  13.2 us (12%)
  local copies, waits for them, and re-layouts  6.72 us (6%)
    pallas_call x1, Pallas kernels, local(): pl.pallas_call(basis_kernel, in_specs=[WHOLE] * 3, out_specs=WHOLE, out_s...  25.4 us
    all_to_all x1, blocking collectives, local(): parts = lax.all_to_all(parts.reshape(8, 16, 2048), 'freq', 0, 0)  13.2 us
    pallas_call x1, Pallas kernels, local(): pl.pallas_call(side_kernel, grid=(1,), in_specs=[SCALARS, field_rows(4, 2...  8.72 us
    pallas_call x1, Pallas kernels, local(): pl.pallas_call(upper_kernel, grid=(1,), in_specs=[SCALARS, field_rows(4,...  7.48 us
    ppermute x3, starting transfers between devices, brick_sum(): got = [part] + [lax.ppermute(part, 'brick', along_z(k)) for k in (1, 2, 3)]  6.75 us
    ppermute x4, starting transfers between devices, gathered(): got = [part] + [lax.ppermute(part, 'brick', move) for move in moves]  6.5 us
    ppermute x4, starting transfers between devices, scattered_sum(): lax.ppermute(pick(parts, (place + k) % count), 'brick', moves[k - 1])  6.1 us
    unnamed x27, local copies, waits for them, and re-layouts  5.88 us
  transfers between devices with their start and end apart: 12, of which 10 were waited for; matrix products, arithmetic and copies ran while one was open for 0% of the time, Pallas kernels for 9%

commit v1 on v0

--- a/solution.py
+++ b/solution.py
@@ -37,7 +37,7 @@
 
 
 def position(axis):
-    return lax.broadcasted_iota(jnp.int32, (2 * SUB, LANES), axis)
+    return lax.broadcasted_iota(jnp.int32, (SUB, LANES), axis)
 
 
 def next_column(field):
@@ -46,72 +46,118 @@
 
 def next_row(field):
     swapped = pltpu.roll(field, NX, 1)
-    later = jnp.where(position(0) >= 2 * SUB - 2, 0.0, pltpu.roll(swapped, 2 * SUB - 2, 0))
+    later = jnp.where(position(0) == SUB - 1, 0.0, pltpu.roll(swapped, SUB - 1, 0))
     return jnp.where(position(1) < NX, swapped, later)
-
-
-def edge_product(fwd, adj, fwd_row, adj_row, orientation):
-    real, imag = 2 * orientation, 2 * orientation + 1
-
-    def wide(ref, row, part):
-        return ref[row, part].astype(jnp.float32)
-
-    return wide(fwd, fwd_row, real) * wide(adj, adj_row, real) - wide(fwd, fwd_row, imag) * wide(
-        adj, adj_row, imag
-    )
 
 
 def tile_rows(index, size):
     return pl.ds(pl.multiple_of(index * size, size), size)
 
 
-def layer_rows(table, block, s, layer):
+def widen(narrow, wide, start, count, parts):
+    def one(i, carry):
+        for k in range(parts):
+            wide[tile_rows(i * parts + k, 16), :] = narrow[i, k].astype(jnp.float32)
+        return carry
+
+    lax.fori_loop(start, start + count, one, 0, unroll=4)
+
+
+def load_rows(parts, codes, fwd, adj, scratch):
+    rows, row_table, fwd_narrow, adj_narrow, fwd_wide, adj_wide, done = scratch
+    half = adj.shape[0] // 2
+    low, high = slice(0, half), slice(half, 2 * half)
+    copies = [
+        pltpu.make_async_copy(adj.at[low, 0:parts], adj_narrow.at[low], done.at[0]),
+        pltpu.make_async_copy(fwd.at[:, 0:parts], fwd_narrow, done.at[1]),
+        pltpu.make_async_copy(adj.at[high, 0:parts], adj_narrow.at[high], done.at[2]),
+    ]
+    for copy in copies:
+        copy.start()
+    row_table[0:1, :], row_table[1:2, :] = decode(codes[...])
+    table_copy = pltpu.make_async_copy(row_table, rows, done.at[3])
+    table_copy.start()
+    copies[1].wait()
+    widen(fwd_narrow, fwd_wide, 0, fwd.shape[0], parts)
+    copies[0].wait()
+    widen(adj_narrow, adj_wide, 0, half, parts)
+    copies[2].wait()
+    widen(adj_narrow, adj_wide, half, half, parts)
+    table_copy.wait()
+
+    def product(d, orientation, layer):
+        def field(wide, row, part):
+            return wide[pl.ds(row * (parts * 16) + part * 16 + layer, SUB, stride=2), :]
+
+        fwd_row, adj_row = rows[0, d], rows[1, d]
+        real, imag = 2 * orientation, 2 * orientation + 1
+        return field(fwd_wide, fwd_row, real) * field(adj_wide, adj_row, real) - field(
+            fwd_wide, fwd_row, imag
+        ) * field(adj_wide, adj_row, imag)
+
+    return product
+
+
+def row_scratch(parts):
     return [
-        table[pl.ds(block * 256 + half * 128 + 2 * s + layer, SUB, stride=2 * SUB), :]
-        for half in range(2)
+        pltpu.SMEM((SUB, PANEL), jnp.int32),
+        pltpu.VMEM((SUB, PANEL), jnp.int32),
+        pltpu.VMEM((4, parts, 16, LANES), jnp.bfloat16),
+        pltpu.VMEM((160, parts, 16, LANES), jnp.bfloat16),
+        pltpu.VMEM((4 * parts * 16, LANES), jnp.float32),
+        pltpu.VMEM((160 * parts * 16, LANES), jnp.float32),
+        pltpu.SemaphoreType.DMA((4,)),
     ]
 
 
-def upper_kernel(codes, fwd, adj, upper, lowest):
+def chunk(table, block, s):
+    return [table[pl.ds(block * 128 + half * 64 + s, SUB, stride=SUB), :] for half in range(2)]
+
+
+def upper_kernel(codes, fwd, adj, low_upper, lowest, *scratch):
+    product = load_rows(4, codes, fwd, adj, scratch)
+
     def one(d, carry):
-        rows = decode(codes[d])
-        edge_x = edge_product(fwd, adj, *rows, 0)
-        edge_y = edge_product(fwd, adj, *rows, 1)
-        upper[tile_rows(d, 16), :] = edge_x + next_row(edge_x) + edge_y + next_column(edge_y)
-        return carry
-
-    lax.fori_loop(0, PANEL, one, 0, unroll=8)
+        edge_x, edge_y = product(d, 0, 0), product(d, 1, 0)
+        low_upper[tile_rows(d, SUB), :] = edge_x + next_row(edge_x) + (edge_y + next_column(edge_y))
+        return carry
+
+    lax.fori_loop(0, PANEL, one, 0, unroll=32)
 
     def block(i, carry):
         for s in range(SUB):
-            low = jnp.concatenate(layer_rows(upper, i, s, 0), axis=0)
-            lowest[s, tile_rows(i, 16), :] = low.astype(jnp.bfloat16)
-        return carry
-
-    lax.fori_loop(0, PANEL // 16, block, 0)
-
-
-def side_kernel(codes, fwd, adj, upper, sens, rest, summed):
+            piece = jnp.concatenate(chunk(low_upper, i, s), axis=0)
+            lowest[s, tile_rows(i, 16), :] = piece.astype(jnp.bfloat16)
+        return carry
+
+    lax.fori_loop(0, PANEL // 16, block, 0, unroll=2)
+
+
+def side_kernel(codes, fwd, adj, low_upper, sens, rest, low, high, *scratch):
+    product = load_rows(6, codes, fwd, adj, scratch)
+
     def one(d, carry):
-        edge_z = edge_product(fwd, adj, *decode(codes[d]), 0)
-        paired = edge_z + next_column(edge_z)
-        here = upper[tile_rows(d, 16), :]
-        above = jnp.where(position(0) % 2 == 0, pltpu.roll(here, 2 * SUB - 1, 0), 0.0)
-        summed[tile_rows(d, 16), :] = here + above + (paired + next_row(paired))
-        return carry
-
-    lax.fori_loop(0, PANEL, one, 0, unroll=8)
+        edge_x, edge_y = product(d, 0, 1), product(d, 1, 1)
+        edge_z = [product(d, 2, layer) for layer in range(2)]
+        across = edge_y + next_column(edge_y)
+        down = [edge_x + (edge + next_column(edge)) for edge in edge_z]
+        here = tile_rows(d, SUB)
+        low[here, :] = low_upper[here, :] + (across + (down[0] + next_row(down[0])))
+        high[here, :] = across + (down[1] + next_row(down[1]))
+        return carry
+
+    lax.fori_loop(0, PANEL, one, 0, unroll=16)
 
     def block(i, carry):
         for s in range(SUB):
-            low = jnp.concatenate(layer_rows(summed, i, s, 0), axis=0)
-            sens[s, tile_rows(i, 16), :] = (0.25 * low).astype(jnp.bfloat16)
-            high = layer_rows(summed, i, s, 1)
-            rest[s, tile_rows(2 * i, SUB), :] = high[0]
-            rest[s, tile_rows(2 * i + 1, SUB), :] = high[1]
-        return carry
-
-    lax.fori_loop(0, PANEL // 16, block, 0)
+            piece = jnp.concatenate(chunk(low, i, s), axis=0)
+            sens[s, tile_rows(i, 16), :] = (0.25 * piece).astype(jnp.bfloat16)
+            pieces = chunk(high, i, s)
+            rest[s, tile_rows(2 * i, SUB), :] = pieces[0]
+            rest[s, tile_rows(2 * i + 1, SUB), :] = pieces[1]
+        return carry
+
+    lax.fori_loop(0, PANEL // 16, block, 0, unroll=2)
 
 
 def dot(left, right, left_dim, right_dim, precision=None):
@@ -303,40 +349,32 @@
     return jax.ShapeDtypeStruct(dims, dtype)
 
 
-def field_rows(count, parts, at):
-    return pl.BlockSpec((count, parts, 16, LANES), lambda i: (0, at, 0, 0))
-
-
-def whole(*dims):
-    return pl.BlockSpec(dims, lambda i: (0,) * len(dims))
-
-
 def local(forward, adjoint, probes, datum):
-    fwd, adj, codes = tiled(forward), tiled(adjoint), datum[0]
+    fwd, adj = tiled(forward), tiled(adjoint)
     layer = (SUB, PANEL, LANES)
-    upper, lowest = pl.pallas_call(
+    anywhere = pl.BlockSpec(memory_space=pl.ANY)
+    low_upper, lowest = pl.pallas_call(
         upper_kernel,
-        grid=(1,),
-        in_specs=[SCALARS, field_rows(4, 4, 0), field_rows(160, 4, 0)],
-        out_specs=(whole(PANEL * 16, LANES), whole(*layer)),
-        out_shape=(shape(PANEL * 16, LANES), shape(*layer, dtype=jnp.bfloat16)),
-        compiler_params=PARAMS,
-        cost_estimate=cost(20_000_000, 6_000_000),
+        in_specs=[WHOLE, anywhere, anywhere],
+        out_specs=(WHOLE, WHOLE),
+        out_shape=(shape(PANEL * SUB, LANES), shape(*layer, dtype=jnp.bfloat16)),
+        scratch_shapes=row_scratch(4),
+        compiler_params=pltpu.CompilerParams(vmem_limit_bytes=60 * 1024 * 1024),
+        cost_estimate=cost(10_000_000, 8_000_000),
         name="upper",
-    )(codes, fwd, adj)
+    )(datum, fwd, adj)
     devices = range(lax.axis_size("brick"))
     above = lax.ppermute(lowest, "brick", [(i + 1, i) for i in devices if i + 1 in devices])
     sens_low, rest = pl.pallas_call(
         side_kernel,
-        grid=(1,),
-        in_specs=[SCALARS, field_rows(4, 2, 2), field_rows(160, 2, 2), whole(PANEL * 16, LANES)],
-        out_specs=(whole(*layer), whole(*layer)),
+        in_specs=[WHOLE, anywhere, anywhere, WHOLE],
+        out_specs=(WHOLE, WHOLE),
         out_shape=(shape(*layer, dtype=jnp.bfloat16), shape(*layer)),
-        scratch_shapes=[pltpu.VMEM((PANEL * 16, LANES), jnp.float32)],
+        scratch_shapes=[pltpu.VMEM((PANEL * SUB, LANES), jnp.float32)] * 2 + row_scratch(6),
         compiler_params=PARAMS,
         cost_estimate=cost(20_000_000, 30_000_000),
         name="side",
-    )(codes, fwd, adj, upper)
+    )(datum, fwd, adj, low_upper)
     low_table = pl.pallas_call(
         low_sums_kernel,
         in_specs=[WHOLE] * 2,

time: 107 us -> 100 us (0.935)
  Pallas kernels: 43.7 us -> 37.8 us
  local copies, waits for them, and re-layouts: 6.72 us -> 4.24 us
  waiting for transfers between devices: 17.6 us -> 19.4 us
    pallas_call x2, Pallas kernels: 16.2 us -> 11.3 us  [the longest x1 5.75 us: local(): pl.pallas_call(upper_kernel, in_specs=[WHOLE, anywhere, anywhere], out_sp...]
    unnamed x27 -> x23, local copies, waits for them, and re-layouts: 5.88 us -> 3.41 us
    ppermute x1, waiting for transfers between devices: 2.55 us -> 4.39 us  [local(): lax.ppermute(lowest, 'brick', [(i + 1, i) for i in devices if i + 1 in de...]
  transfers between devices with their start and end apart: 12 -> 12, of which waited for: 10 -> 10; matrix products, arithmetic and copies ran while one was open for 0% -> 0% of each run, Pallas kernels for 9% -> 6%
where the time goes in v1:
time: 100 us; the launch traced here: 99.7 us
  Pallas kernels  37.8 us (38%)
  starting transfers between devices  24.5 us (24%)
  waiting for transfers between devices  19.4 us (19%)
  blocking collectives  13.2 us (13%)
  local copies, waits for them, and re-layouts  4.24 us (4%)
    pallas_call x1, Pallas kernels, local(): pl.pallas_call(basis_kernel, in_specs=[WHOLE] * 3, out_specs=WHOLE, out_s...  25.3 us
    all_to_all x1, blocking collectives, local(): parts = lax.all_to_all(parts.reshape(8, 16, 2048), 'freq', 0, 0)  13.2 us
    ppermute x3, starting transfers between devices, brick_sum(): got = [part] + [lax.ppermute(part, 'brick', along_z(k)) for k in (1, 2, 3)]  6.64 us
    ppermute x4, starting transfers between devices, gathered(): got = [part] + [lax.ppermute(part, 'brick', move) for move in moves]  6.49 us
    ppermute x4, starting transfers between devices, scattered_sum(): lax.ppermute(pick(parts, (place + k) % count), 'brick', moves[k - 1])  6.21 us
    pallas_call x1, Pallas kernels, local(): pl.pallas_call(upper_kernel, in_specs=[WHOLE, anywhere, anywhere], out_sp...  5.75 us
    pallas_call x1, Pallas kernels, local(): pl.pallas_call(side_kernel, in_specs=[WHOLE, anywhere, anywhere, WHOLE],...  5.56 us
    ppermute x4, waiting for transfers between devices, scattered_sum(): lax.ppermute(pick(parts, (place + k) % count), 'brick', moves[k - 1])  5.2 us
  transfers between devices with their start and end apart: 12, of which 10 were waited for; matrix products, arithmetic and copies ran while one was open for 0% of the time, Pallas kernels for 6%

profile of v1, /device:TPU:1, one launch (start us, length us, event | category | flops | bytes accessed | tf_op | source)
XLA Modules:
  0.0 99.7 jit_solution(12812141063472494013)
XLA Ops:
  0.0 0.0 copy-start.4
  0.0 0.0 copy-start.3
  0.0 0.0 copy-start.1
  0.0 5.7 %upper.1 = (f32[2048,128]{1,0:T(8,128)}, bf16[8,256,128]{2,1,0:T(8,128)(2,1)}) custom-call(s32[1,256]{1,0:T(1,128)} %codes.3, bf16[4,6,16,128]{3,2,1,0:T(8,128)(2,1)} %bitcast.60, bf16[160,6,16,128]{3,2,1,0:T(8,128)(2,1)} %bitcast.56), custom_call_target="tpu_custom_call" | custom-call | flops 10000000 | bytes 8000000 | tf_op jit(solution)/shard_map/upper/pallas_call | solution.py:356
  5.8 5.1 %collective-permute-start = (bf16[8,256,128]{2,1,0:T(8,128)(2,1)}, bf16[8,256,128]{2,1,0:T(8,128)(2,1)S(1)}, u32[]{:S(2)}, u32[]{:S(2)}) collective-permute-start(bf16[8,256,128]{2,1,0:T(8,128)(2,1)} %get-tuple-element.13), channel_id=1, source_target_pairs={{1,0},{2,1},{3,2},{4,3},{5,4},{6,5},{7,6},{8,7},{9,8},{10,9},{11,1... | collective-permute-start | bytes 1572872 | tf_op jit(solution)/shard_map/ppermute | solution.py:367
  10.9 0.0 copy-done.4
  11.0 0.0 copy-done.3
  11.0 0.0 copy-start
  11.0 2.1 %copy-done = bf16[1,160,6,2,1024]{4,3,2,1,0:T(2,128)(2,1)S(1)} copy-done((bf16[1,160,6,2,1024]{4,3,2,1,0:T(2,128)(2,1)S(1)}, bf16[1,160,6,2,1024]{4,3,2,1,0:T(2,128)(2,1)}, u32[]{:S(2)}) %copy-start) | copy-done | bytes 3932184
  13.1 0.0 copy-start.2
  13.1 1.2 %copy-done.2 = f32[2048,128]{1,0:T(8,128)S(1)} copy-done((f32[2048,128]{1,0:T(8,128)S(1)}, f32[2048,128]{1,0:T(8,128)}, u32[]{:S(2)}) %copy-start.2) | copy-done | bytes 1048600
  14.3 5.6 %side.1 = (bf16[8,256,128]{2,1,0:T(8,128)(2,1)S(1)}, f32[8,256,128]{2,1,0:T(8,128)S(1)}) custom-call(s32[1,256]{1,0:T(1,128)S(1)} %copy-done.4, bf16[4,6,16,128]{3,2,1,0:T(8,128)(2,1)S(1)} %bitcast.61, bf16[160,6,16,128]{3,2,1,0:T(8,128)(2,1)S(1)} %bitcast.57, f32[2048,128]{1,0:T(8,128)S(1)} %copy-done.2), custom_call_target="tpu_custom_call" | custom-call | flops 20000000 | bytes 30000000 | tf_op jit(solution)/shard_map/side/pallas_call | solution.py:368
  19.9 0.0 copy-done.1
  19.9 0.5 low_sums.1.low_table
  20.4 4.4 %collective-permute-done.above = bf16[8,256,128]{2,1,0:T(8,128)(2,1)S(1)} collective-permute-done((bf16[8,256,128]{2,1,0:T(8,128)(2,1)}, bf16[8,256,128]{2,1,0:T(8,128)(2,1)S(1)}, u32[]{:S(2)}, u32[]{:S(2)}) %collective-permute-start) | collective-permute-done | bytes 524320 | tf_op jit(solution)/shard_map/ppermute | solution.py:367
  24.7 0.7 high_sums.1
  25.5 0.1 collective-permute-start.1
  25.6 1.3 %collective-permute-done.1 = f32[320,128]{1,0:T(8,128)S(1)} collective-permute-done((f32[320,128]{1,0:T(8,128)S(1)}, f32[320,128]{1,0:T(8,128)S(1)}, u32[]{:S(2)}, u32[]{:S(2)}) %collective-permute-start.1) | collective-permute-done | bytes 163872 | tf_op jit(solution)/shard_map/ppermute | solution.py:321
  27.0 5.3 %collective-permute-start.4 = (f32[80,128]{1,0:T(8,128)S(1)}, f32[80,128]{1,0:T(8,128)S(1)}, u32[]{:S(2)}, u32[]{:S(2)}) collective-permute-start(f32[80,128]{1,0:T(8,128)S(1)} %get-tuple-element.18), channel_id=1, source_target_pairs={{0,24},{1,25},{2,26},{3,27},{4,28},{5,29},{6,30},{7,31},{8,0},{9,1... | collective-permute-start | bytes 122888 | tf_op jit(solution)/shard_map/ppermute | solution.py:321
  32.3 0.2 collective-permute-start.3
  32.5 0.6 collective-permute-start.2
  33.1 0.3 collective-permute-done.4
  33.4 3.4 %collective-permute-done.3 = f32[80,128]{1,0:T(8,128)S(1)} collective-permute-done((f32[80,128]{1,0:T(8,128)S(1)}, f32[80,128]{1,0:T(8,128)S(1)}, u32[]{:S(2)}, u32[]{:S(2)}) %collective-permute-start.3) | collective-permute-done | bytes 40992 | tf_op jit(solution)/shard_map/ppermute | solution.py:321
  36.7 0.3 collective-permute-done.2
  37.0 4.4 %collective-permute-start.5 = (f32[80,128]{1,0:T(8,128)S(1)}, f32[80,128]{1,0:T(8,128)S(1)}, u32[]{:S(2)}, u32[]{:S(2)}) collective-permute-start(f32[80,128]{1,0:T(8,128)S(1)} %fusion.5), channel_id=1, source_target_pairs={{0,6},{1,7},{2,0},{3,1},{4,2},{5,3},{6,4},{7,5},{8,14},{9,15},{10,... | collective-permute-start | bytes 122888 | tf_op jit(solution)/shard_map/ppermute | solution.py:340
  41.4 0.5 collective-permute-start.6
  41.9 1.7 %collective-permute-start.7 = (f32[80,128]{1,0:T(8,128)S(1)}, f32[80,128]{1,0:T(8,128)S(1)}, u32[]{:S(2)}, u32[]{:S(2)}) collective-permute-start(f32[80,128]{1,0:T(8,128)S(1)} %fusion.5), channel_id=1, source_target_pairs={{0,2},{1,3},{2,4},{3,5},{4,6},{5,7},{6,0},{7,1},{8,10},{9,11},{10,... | collective-permute-start | bytes 122888 | tf_op jit(solution)/shard_map/ppermute | solution.py:340
  43.7 0.0 collective-permute-done.5
  43.7 4.8 %collective-permute-done.6 = f32[80,128]{1,0:T(8,128)S(1)} collective-permute-done((f32[80,128]{1,0:T(8,128)S(1)}, f32[80,128]{1,0:T(8,128)S(1)}, u32[]{:S(2)}, u32[]{:S(2)}) %collective-permute-start.6) | collective-permute-done | bytes 40992 | tf_op jit(solution)/shard_map/ppermute | solution.py:340
  48.5 0.0 collective-permute-done.7
  48.6 0.4 collective-permute-start.8
  49.0 1.4 %collective-permute-start.9 = (f32[80,128]{1,0:T(8,128)S(1)}, f32[80,128]{1,0:T(8,128)S(1)}, u32[]{:S(2)}, u32[]{:S(2)}) collective-permute-start(f32[80,128]{1,0:T(8,128)S(1)} %fusion.6), channel_id=1, source_target_pairs={{0,16},{1,17},{2,18},{3,19},{4,20},{5,21},{6,22},{7,23},{8,24},{9,... | collective-permute-start | bytes 122888 | tf_op jit(solution)/shard_map/ppermute | solution.py:330
  50.4 0.0 collective-permute-start.10
  50.4 1.1 %collective-permute-done.8 = f32[80,128]{1,0:T(8,128)S(1)} collective-permute-done((f32[80,128]{1,0:T(8,128)S(1)}, f32[80,128]{1,0:T(8,128)S(1)}, u32[]{:S(2)}, u32[]{:S(2)}) %collective-permute-start.8) | collective-permute-done | bytes 40992 | tf_op jit(solution)/shard_map/ppermute | solution.py:330
  51.5 1.8 %collective-permute-done.9 = f32[80,128]{1,0:T(8,128)S(1)} collective-permute-done((f32[80,128]{1,0:T(8,128)S(1)}, f32[80,128]{1,0:T(8,128)S(1)}, u32[]{:S(2)}, u32[]{:S(2)}) %collective-permute-start.9) | collective-permute-done | bytes 40992 | tf_op jit(solution)/shard_map/ppermute | solution.py:330
  53.4 1.1 %collective-permute-done.10 = f32[80,128]{1,0:T(8,128)S(1)} collective-permute-done((f32[80,128]{1,0:T(8,128)S(1)}, f32[80,128]{1,0:T(8,128)S(1)}, u32[]{:S(2)}, u32[]{:S(2)}) %collective-permute-start.10) | collective-permute-done | bytes 40992 | tf_op jit(solution)/shard_map/ppermute | solution.py:330
  54.6 4.7 %collective-permute-start.11 = (f32[320,128]{1,0:T(8,128)S(1)}, f32[320,128]{1,0:T(8,128)S(1)}, u32[]{:S(2)}, u32[]{:S(2)}) collective-permute-start(f32[320,128]{1,0:T(8,128)S(1)} %bitcast.66), channel_id=1, source_target_pairs={{0,1},{1,0},{2,3},{3,2},{4,5},{5,4},{6,7},{7,6},{8,9},{9,8},{10,11... | collective-permute-start | bytes 491528 | tf_op jit(solution)/shard_map/ppermute | solution.py:330
  59.2 1.0 %collective-permute-done.11 = f32[320,128]{1,0:T(8,128)S(1)} collective-permute-done((f32[320,128]{1,0:T(8,128)S(1)}, f32[320,128]{1,0:T(8,128)S(1)}, u32[]{:S(2)}, u32[]{:S(2)}) %collective-permute-start.11) | collective-permute-done | bytes 163872 | tf_op jit(solution)/shard_map/ppermute | solution.py:330
  60.3 0.1 fusion.2
  60.3 25.3 %basis.1 = bf16[128,2048]{1,0:T(8,128)(2,1)S(1)} custom-call(f32[640,128]{1,0:T(8,128)S(1)} %bitcast.59, bf16[8,256,128]{2,1,0:T(8,128)(2,1)S(1)} %get-tuple-element.14.sens.sens_low, bf16[8,256,128]{2,1,0:T(8,128)(2,1)S(1)} %get-tuple-element.16.sens_high), custom_call_target="tpu_custom_call" | custom-call | flops 400000000 | bytes 60000000 | tf_op jit(solution)/shard_map/basis/pallas_call | solution.py:397
  85.7 13.2 %all_to_all.5 = bf16[8,16,2048]{2,1,0:T(8,128)(2,1)S(1)} all-to-all(bf16[8,16,2048]{2,1,0:T(8,128)(2,1)S(1)} %bitcast.58), channel_id=1, replica_groups=mesh['freq'=8,'brick'=32] {'freq'}, dimensions={0} | all-to-all | bytes 1048576 | tf_op jit(solution)/shard_map/all_to_all | solution.py:411
  98.9 0.1 convert_reduce_fusion
  99.0 0.8 reshape.42
  (22 shorter events, 0.2 us)
Async XLA Ops:
  0.0 10.9 %copy-start.4 = (s32[1,256]{1,0:T(1,128)S(1)}, s32[1,256]{1,0:T(1,128)}, u32[]{:S(2)}) copy-start(s32[1,256]{1,0:T(1,128)} %codes.3) | copy-start | bytes 3076
  0.0 11.0 %copy-start.3 = (bf16[1,4,6,2,1024]{4,3,2,1,0:T(2,128)(2,1)S(1)}, bf16[1,4,6,2,1024]{4,3,2,1,0:T(2,128)(2,1)}, u32[]{:S(2)}) copy-start(bf16[1,4,6,2,1024]{4,3,2,1,0:T(2,128)(2,1)} %param.4) | copy-start | bytes 294916
  0.0 19.9 %copy-start.1 = (bf16[2,1024,128]{2,1,0:T(8,128)(2,1)S(1)}, bf16[2,1024,128]{2,1,0:T(8,128)(2,1)}, u32[]{:S(2)}) copy-start(bf16[2,1024,128]{2,1,0:T(8,128)(2,1)} %probes.3) | copy-start | bytes 1572868
  5.8 19.0 %collective-permute-start = (bf16[8,256,128]{2,1,0:T(8,128)(2,1)}, bf16[8,256,128]{2,1,0:T(8,128)(2,1)S(1)}, u32[]{:S(2)}, u32[]{:S(2)}) collective-permute-start(bf16[8,256,128]{2,1,0:T(8,128)(2,1)} %get-tuple-element.13), channel_id=1, source_target_pairs={{1,0},{2,1},{3,2},{4,3},{5,4},{6,5},{7,6},{8,7},{9,8},{10,9},{11,1... | collective-permute-start | bytes 1572872 | tf_op jit(solution)/shard_map/ppermute | solution.py:367
  11.0 2.1 %copy-start = (bf16[1,160,6,2,1024]{4,3,2,1,0:T(2,128)(2,1)S(1)}, bf16[1,160,6,2,1024]{4,3,2,1,0:T(2,128)(2,1)}, u32[]{:S(2)}) copy-start(bf16[1,160,6,2,1024]{4,3,2,1,0:T(2,128)(2,1)} %param.5) | copy-start | bytes 11796484
  13.1 1.2 %copy-start.2 = (f32[2048,128]{1,0:T(8,128)S(1)}, f32[2048,128]{1,0:T(8,128)}, u32[]{:S(2)}) copy-start(f32[2048,128]{1,0:T(8,128)} %get-tuple-element.11.low_upper) | copy-start | bytes 3145732
  25.5 1.5 %collective-permute-start.1 = (f32[320,128]{1,0:T(8,128)S(1)}, f32[320,128]{1,0:T(8,128)S(1)}, u32[]{:S(2)}, u32[]{:S(2)}) collective-permute-start(f32[320,128]{1,0:T(8,128)S(1)} %dynamic-slice_bitcast_fusion), channel_id=1, source_target_pairs={{0,1},{1,0},{2,3},{3,2},{4,5},{5,4},{6,7},{7,6},{8,9},{9,8},{10,11... | collective-permute-start | bytes 491528 | tf_op jit(solution)/shard_map/ppermute | solution.py:321
  27.0 6.4 %collective-permute-start.4 = (f32[80,128]{1,0:T(8,128)S(1)}, f32[80,128]{1,0:T(8,128)S(1)}, u32[]{:S(2)}, u32[]{:S(2)}) collective-permute-start(f32[80,128]{1,0:T(8,128)S(1)} %get-tuple-element.18), channel_id=1, source_target_pairs={{0,24},{1,25},{2,26},{3,27},{4,28},{5,29},{6,30},{7,31},{8,0},{9,1... | collective-permute-start | bytes 122888 | tf_op jit(solution)/shard_map/ppermute | solution.py:321
  32.3 4.5 %collective-permute-start.3 = (f32[80,128]{1,0:T(8,128)S(1)}, f32[80,128]{1,0:T(8,128)S(1)}, u32[]{:S(2)}, u32[]{:S(2)}) collective-permute-start(f32[80,128]{1,0:T(8,128)S(1)} %get-tuple-element.19), channel_id=1, source_target_pairs={{0,16},{1,17},{2,18},{3,19},{4,20},{5,21},{6,22},{7,23},{8,24},{9,... | collective-permute-start | bytes 122888 | tf_op jit(solution)/shard_map/ppermute | solution.py:321
  32.5 4.5 %collective-permute-start.2 = (f32[80,128]{1,0:T(8,128)S(1)}, f32[80,128]{1,0:T(8,128)S(1)}, u32[]{:S(2)}, u32[]{:S(2)}) collective-permute-start(f32[80,128]{1,0:T(8,128)S(1)} %get-tuple-element.17), channel_id=1, source_target_pairs={{0,8},{1,9},{2,10},{3,11},{4,12},{5,13},{6,14},{7,15},{8,16},{9,17... | collective-permute-start | bytes 122888 | tf_op jit(solution)/shard_map/ppermute | solution.py:321
  37.0 6.6 %collective-permute-start.5 = (f32[80,128]{1,0:T(8,128)S(1)}, f32[80,128]{1,0:T(8,128)S(1)}, u32[]{:S(2)}, u32[]{:S(2)}) collective-permute-start(f32[80,128]{1,0:T(8,128)S(1)} %fusion.5), channel_id=1, source_target_pairs={{0,6},{1,7},{2,0},{3,1},{4,2},{5,3},{6,4},{7,5},{8,14},{9,15},{10,... | collective-permute-start | bytes 122888 | tf_op jit(solution)/shard_map/ppermute | solution.py:340
  41.4 7.0 %collective-permute-start.6 = (f32[80,128]{1,0:T(8,128)S(1)}, f32[80,128]{1,0:T(8,128)S(1)}, u32[]{:S(2)}, u32[]{:S(2)}) collective-permute-start(f32[80,128]{1,0:T(8,128)S(1)} %fusion.5), channel_id=1, source_target_pairs={{0,4},{1,5},{2,6},{3,7},{4,0},{5,1},{6,2},{7,3},{8,12},{9,13},{10,... | collective-permute-start | bytes 122888 | tf_op jit(solution)/shard_map/ppermute | solution.py:340
  41.9 6.5 %collective-permute-start.7 = (f32[80,128]{1,0:T(8,128)S(1)}, f32[80,128]{1,0:T(8,128)S(1)}, u32[]{:S(2)}, u32[]{:S(2)}) collective-permute-start(f32[80,128]{1,0:T(8,128)S(1)} %fusion.5), channel_id=1, source_target_pairs={{0,2},{1,3},{2,4},{3,5},{4,6},{5,7},{6,0},{7,1},{8,10},{9,11},{10,... | collective-permute-start | bytes 122888 | tf_op jit(solution)/shard_map/ppermute | solution.py:340
  48.6 2.9 %collective-permute-start.8 = (f32[80,128]{1,0:T(8,128)S(1)}, f32[80,128]{1,0:T(8,128)S(1)}, u32[]{:S(2)}, u32[]{:S(2)}) collective-permute-start(f32[80,128]{1,0:T(8,128)S(1)} %fusion.6), channel_id=1, source_target_pairs={{0,24},{1,25},{2,26},{3,27},{4,28},{5,29},{6,30},{7,31},{8,0},{9,1... | collective-permute-start | bytes 122888 | tf_op jit(solution)/shard_map/ppermute | solution.py:330
  49.0 4.4 %collective-permute-start.9 = (f32[80,128]{1,0:T(8,128)S(1)}, f32[80,128]{1,0:T(8,128)S(1)}, u32[]{:S(2)}, u32[]{:S(2)}) collective-permute-start(f32[80,128]{1,0:T(8,128)S(1)} %fusion.6), channel_id=1, source_target_pairs={{0,16},{1,17},{2,18},{3,19},{4,20},{5,21},{6,22},{7,23},{8,24},{9,... | collective-permute-start | bytes 122888 | tf_op jit(solution)/shard_map/ppermute | solution.py:330
  50.4 4.1 %collective-permute-start.10 = (f32[80,128]{1,0:T(8,128)S(1)}, f32[80,128]{1,0:T(8,128)S(1)}, u32[]{:S(2)}, u32[]{:S(2)}) collective-permute-start(f32[80,128]{1,0:T(8,128)S(1)} %fusion.6), channel_id=1, source_target_pairs={{0,8},{1,9},{2,10},{3,11},{4,12},{5,13},{6,14},{7,15},{8,16},{9,17... | collective-permute-start | bytes 122888 | tf_op jit(solution)/shard_map/ppermute | solution.py:330
  54.6 5.7 %collective-permute-start.11 = (f32[320,128]{1,0:T(8,128)S(1)}, f32[320,128]{1,0:T(8,128)S(1)}, u32[]{:S(2)}, u32[]{:S(2)}) collective-permute-start(f32[320,128]{1,0:T(8,128)S(1)} %bitcast.66), channel_id=1, source_target_pairs={{0,1},{1,0},{2,3},{3,2},{4,5},{5,4},{6,7},{7,6},{8,9},{9,8},{10,11... | collective-permute-start | bytes 491528 | tf_op jit(solution)/shard_map/ppermute | solution.py:330

commit v2 on v1

--- a/solution.py
+++ b/solution.py
@@ -11,7 +11,7 @@
 PANEL = 256
 PROBES = 128
 SUB, LANES = 8, 128
-BLOCK = 64
+HALF = 64
 
 WHOLE = pl.BlockSpec(memory_space=pltpu.VMEM)
 SCALARS = pl.BlockSpec(memory_space=pltpu.SMEM)
@@ -197,98 +197,107 @@
         table[at, :] = low_table[at, :] + part
 
 
-def spread(column):
-    return jnp.broadcast_to(column, (SUB, LANES))
-
-
-def eliminate(work):
+def spread(piece):
+    return jnp.broadcast_to(piece, (SUB, LANES))
+
+
+def column_of_each(piece, at):
+    left = lax.broadcasted_iota(jnp.int32, (SUB, LANES), 1) < HALF
+    return jnp.where(left, spread(piece[:, at : at + 1]), spread(piece[:, HALF + at : HALF + at + 1]))
+
+
+def eliminate_panel(gram, inverse, g):
     row = lax.broadcasted_iota(jnp.int32, (SUB, LANES), 0)
-    groups = BLOCK // SUB
-    for start in range(0, PROBES, BLOCK):
-        m = [
-            [work[start + SUB * g : start + SUB * g + SUB, h * 128 : h * 128 + 128] for h in range(2)]
-            for g in range(groups)
-        ]
-        for g in range(groups):
-            at = start + SUB * g
-            column = {
-                (q, k): spread(m[q][0][:, at + k : at + k + 1])
-                for q in range(g, groups)
-                for k in range(SUB)
-            }
-            u = {(i, k): spread(column[g, k][i : i + 1, :]) for k in range(SUB) for i in range(k + 1)}
-            root = []
+    later = range(g + 1, len(gram))
+    column = {
+        (q, k): column_of_each(gram[q], SUB * g + k) for q in (g, *later) for k in range(SUB)
+    }
+    u = {(i, k): spread(column[g, k][i : i + 1, :]) for k in range(SUB) for i in range(k + 1)}
+    root = []
+    for k in range(SUB):
+        root.append(lax.rsqrt(u[k, k]))
+        for j in range(k + 1, SUB):
+            u[k, j] = u[k, j] * root[k]
+        for j in range(k + 1, SUB):
+            for i in range(k + 1, j + 1):
+                u[i, j] = u[i, j] - u[k, i] * u[k, j]
+    low = {}
+    for q in later:
+        for k in range(SUB):
+            entry = column[q, k]
+            for j in range(k):
+                entry = entry - low[q, j] * u[j, k]
+            low[q, k] = entry * root[k]
+    for table in (gram, inverse):
+        lead = [spread(table[g][k : k + 1, :]) for k in range(SUB)]
+        for k in range(SUB):
+            for j in range(k):
+                lead[k] = lead[k] - u[j, k] * lead[j]
+            lead[k] = lead[k] * root[k]
+        table[g] = lead[0]
+        for k in range(1, SUB):
+            table[g] = jnp.where(row == k, lead[k], table[g])
+        for q in later:
             for k in range(SUB):
-                root.append(lax.rsqrt(u[k, k]))
-                for j in range(k + 1, SUB):
-                    u[k, j] = u[k, j] * root[k]
-                for j in range(k + 1, SUB):
-                    for i in range(k + 1, j + 1):
-                        u[i, j] = u[i, j] - u[k, i] * u[k, j]
-            lead = [[spread(m[g][h][k : k + 1, :]) for h in range(2)] for k in range(SUB)]
-            for k in range(SUB):
-                for h in range(2):
-                    for j in range(k):
-                        lead[k][h] = lead[k][h] - u[j, k] * lead[j][h]
-                    lead[k][h] = lead[k][h] * root[k]
-            for h in range(2):
-                m[g][h] = lead[0][h]
-                for k in range(1, SUB):
-                    m[g][h] = jnp.where(row == k, lead[k][h], m[g][h])
-            for q in range(g + 1, groups):
-                low = []
-                for k in range(SUB):
-                    entry = column[q, k]
-                    for j in range(k):
-                        entry = entry - low[j] * u[j, k]
-                    low.append(entry * root[k])
-                for h in range(2):
-                    for k in range(SUB):
-                        m[q][h] = m[q][h] - low[k] * lead[k][h]
-        for g in range(groups):
-            for h in range(2):
-                work[start + SUB * g : start + SUB * g + SUB, h * 128 : h * 128 + 128] = m[g][h]
-        if start + BLOCK < PROBES:
-            done = work[start : start + BLOCK, :]
-            change = dot(done[:, :PROBES], done, 0, 0, lax.Precision.HIGHEST)
-            work[start + BLOCK :, :] = work[start + BLOCK :, :] - change[start + BLOCK :, :]
-
-
-def basis_kernel(table, sens_low, sens_high, parts, work, sketch, cross):
-    highest = lax.Precision.HIGHEST
+                table[q] = table[q] - low[q, k] * lead[k]
+
+
+def exact_dot(left, right, left_dim, right_dim):
+    return dot(left, right, left_dim, right_dim, lax.Precision.HIGHEST)
+
+
+def padded(block, side):
+    zeros = jnp.zeros_like(block)
+    return jnp.concatenate([zeros, block] if side else [block, zeros], axis=0)
+
+
+def basis_kernel(table, sens_low, sens_high, parts, basis, sketch, cross):
     corner = table[128:256, :]
     cross[0:128, 0:128] = table[0:128, :]
     cross[0:128, 128:256] = corner
     cross[128:256, 0:128] = corner.T
     cross[128:256, 128:256] = table[256:384, :]
-    sketch[:, 0:128] = table[384:512, :]
-    sketch[:, 128:256] = table[512:640, :]
+    sketch[0, :, 0:128] = table[384:512, :]
+    sketch[0, :, 128:256] = table[512:640, :]
     identity = jnp.where(
-        lax.broadcasted_iota(jnp.int32, (PROBES, PROBES), 0)
-        == lax.broadcasted_iota(jnp.int32, (PROBES, PROBES), 1),
+        lax.broadcasted_iota(jnp.int32, (HALF, LANES), 0)
+        == lax.broadcasted_iota(jnp.int32, (HALF, LANES), 1) % HALF,
         1.0,
         0.0,
     )
-
-    def orthonormalize(step, carry):
-        rows = sketch[...]
-        work[:, 0:128] = dot(rows, rows, 1, 1, highest)
-        work[:, 128:256] = identity
-        eliminate(work)
-
-        @pl.when(step < ITERS)
-        def _():
-            moved = dot(sketch[...], cross[...], 1, 0, highest)
-            sketch[...] = dot(work[:, 128:256], moved, 1, 0, highest)
-
-        return carry
-
-    lax.fori_loop(0, ITERS + 1, orthonormalize, 0)
-    basis = dot(work[:, 128:256], sketch[...], 1, 0, highest).astype(jnp.bfloat16)
+    halves = (slice(0, HALF), slice(HALF, PROBES))
+    for wave in range(ITERS + 2):
+        work = [(half, wave - half) for half in (0, 1) if 0 <= wave - half <= ITERS]
+        gram, rows = 0.0, []
+        for half, stage in work:
+            sides = (half,) if len(work) == 2 else (0, 1)
+            x = sketch[stage, halves[half], :]
+            for side in sides:
+                gram = gram + exact_dot(x, padded(x, side), 1, 1)
+            if half == 1:
+                before = basis[stage, halves[0], :]
+                overlap = exact_dot(x, before, 1, 1)
+                for side in sides:
+                    gram = gram - exact_dot(overlap, padded(overlap, side), 1, 1)
+                x = x - exact_dot(overlap, before, 1, 0)
+            rows.append(x)
+        moved = exact_dot(jnp.concatenate(rows, axis=0), cross[...], 1, 0)
+        gram_rows = [gram[SUB * g : SUB * g + SUB, :] for g in range(HALF // SUB)]
+        inverse_rows = [identity[SUB * g : SUB * g + SUB, :] for g in range(HALF // SUB)]
+        for g in range(HALF // SUB):
+            eliminate_panel(gram_rows, inverse_rows, g)
+        inverse = jnp.concatenate(inverse_rows, axis=0)
+        for at, (half, stage) in enumerate(work):
+            both = jnp.concatenate([rows[at], moved[HALF * at : HALF * at + HALF, :]], axis=1)
+            done = exact_dot(inverse[:, halves[half]], both, 1, 0)
+            basis[stage, halves[half], :] = done[:, :PANEL]
+            if stage < ITERS:
+                sketch[stage + 1, halves[half], :] = done[:, PANEL:]
+    final = basis[ITERS].astype(jnp.bfloat16)
     for layer, sens in enumerate((sens_low, sens_high)):
         for s in range(SUB):
             at = 1024 * layer + 128 * s
-            parts[:, at : at + 128] = dot(basis, sens[s], 1, 0).astype(jnp.bfloat16)
+            parts[:, at : at + 128] = dot(final, sens[s], 1, 0).astype(jnp.bfloat16)
 
 
 def brick_moves(step):
@@ -400,8 +409,8 @@
         out_specs=WHOLE,
         out_shape=shape(PROBES, 2048, dtype=jnp.bfloat16),
         scratch_shapes=[
-            pltpu.VMEM((PROBES, 2 * PROBES), jnp.float32),
-            pltpu.VMEM((PROBES, PANEL), jnp.float32),
+            pltpu.VMEM((ITERS + 1, PROBES, PANEL), jnp.float32),
+            pltpu.VMEM((ITERS + 1, PROBES, PANEL), jnp.float32),
             pltpu.VMEM((PANEL, PANEL), jnp.float32),
         ],
         compiler_params=PARAMS,

time: 100 us -> 89.2 us (0.89)
  Pallas kernels: 37.8 us -> 27 us
    pallas_call x1, Pallas kernels: 25.3 us -> 14.5 us  [local(): pl.pallas_call(basis_kernel, in_specs=[WHOLE] * 3, out_specs=WHOLE, out_s...]
  transfers between devices with their start and end apart: 12 -> 12, of which waited for: 10 -> 10; matrix products, arithmetic and copies ran while one was open for 0% -> 0% of each run, Pallas kernels for 6% -> 7%
where the time goes in v2:
time: 89.2 us; the launch traced here: 88.9 us
  Pallas kernels  27 us (30%)
  starting transfers between devices  24.5 us (27%)
  waiting for transfers between devices  19.4 us (22%)
  blocking collectives  13.2 us (15%)
  local copies, waits for them, and re-layouts  4.24 us (5%)
    pallas_call x1, Pallas kernels, local(): pl.pallas_call(basis_kernel, in_specs=[WHOLE] * 3, out_specs=WHOLE, out_s...  14.5 us
    all_to_all x1, blocking collectives, local(): parts = lax.all_to_all(parts.reshape(8, 16, 2048), 'freq', 0, 0)  13.2 us
    ppermute x3, starting transfers between devices, brick_sum(): got = [part] + [lax.ppermute(part, 'brick', along_z(k)) for k in (1, 2, 3)]  6.64 us
    ppermute x4, starting transfers between devices, gathered(): got = [part] + [lax.ppermute(part, 'brick', move) for move in moves]  6.49 us
    ppermute x4, starting transfers between devices, scattered_sum(): lax.ppermute(pick(parts, (place + k) % count), 'brick', moves[k - 1])  6.21 us
    pallas_call x1, Pallas kernels, local(): pl.pallas_call(upper_kernel, in_specs=[WHOLE, anywhere, anywhere], out_sp...  5.75 us
    pallas_call x1, Pallas kernels, local(): pl.pallas_call(side_kernel, in_specs=[WHOLE, anywhere, anywhere, WHOLE],...  5.56 us
    ppermute x4, waiting for transfers between devices, scattered_sum(): lax.ppermute(pick(parts, (place + k) % count), 'brick', moves[k - 1])  5.2 us
  transfers between devices with their start and end apart: 12, of which 10 were waited for; matrix products, arithmetic and copies ran while one was open for 0% of the time, Pallas kernels for 7%

profile of v2, /device:TPU:1, one launch (start us, length us, event | category | flops | bytes accessed | tf_op | source)
XLA Modules:
  0.0 88.9 jit_solution(2325356295502605867)
XLA Ops:
  0.0 0.0 copy-start.4
  0.0 0.0 copy-start.3
  0.0 0.0 copy-start.1
  0.0 5.7 %upper.1 = (f32[2048,128]{1,0:T(8,128)}, bf16[8,256,128]{2,1,0:T(8,128)(2,1)}) custom-call(s32[1,256]{1,0:T(1,128)} %codes.3, bf16[4,6,16,128]{3,2,1,0:T(8,128)(2,1)} %bitcast.60, bf16[160,6,16,128]{3,2,1,0:T(8,128)(2,1)} %bitcast.56), custom_call_target="tpu_custom_call" | custom-call | flops 10000000 | bytes 8000000 | tf_op jit(solution)/shard_map/upper/pallas_call | solution.py:365
  5.8 5.1 %collective-permute-start = (bf16[8,256,128]{2,1,0:T(8,128)(2,1)}, bf16[8,256,128]{2,1,0:T(8,128)(2,1)S(1)}, u32[]{:S(2)}, u32[]{:S(2)}) collective-permute-start(bf16[8,256,128]{2,1,0:T(8,128)(2,1)} %get-tuple-element.13), channel_id=1, source_target_pairs={{1,0},{2,1},{3,2},{4,3},{5,4},{6,5},{7,6},{8,7},{9,8},{10,9},{11,1... | collective-permute-start | bytes 1572872 | tf_op jit(solution)/shard_map/ppermute | solution.py:376
  10.9 0.0 copy-done.4
  11.0 0.0 copy-done.3
  11.0 0.0 copy-start
  11.0 2.1 %copy-done = bf16[1,160,6,2,1024]{4,3,2,1,0:T(2,128)(2,1)S(1)} copy-done((bf16[1,160,6,2,1024]{4,3,2,1,0:T(2,128)(2,1)S(1)}, bf16[1,160,6,2,1024]{4,3,2,1,0:T(2,128)(2,1)}, u32[]{:S(2)}) %copy-start) | copy-done | bytes 3932184
  13.1 0.0 copy-start.2
  13.1 1.2 %copy-done.2 = f32[2048,128]{1,0:T(8,128)S(1)} copy-done((f32[2048,128]{1,0:T(8,128)S(1)}, f32[2048,128]{1,0:T(8,128)}, u32[]{:S(2)}) %copy-start.2) | copy-done | bytes 1048600
  14.3 5.6 %side.1 = (bf16[8,256,128]{2,1,0:T(8,128)(2,1)S(1)}, f32[8,256,128]{2,1,0:T(8,128)S(1)}) custom-call(s32[1,256]{1,0:T(1,128)S(1)} %copy-done.4, bf16[4,6,16,128]{3,2,1,0:T(8,128)(2,1)S(1)} %bitcast.61, bf16[160,6,16,128]{3,2,1,0:T(8,128)(2,1)S(1)} %bitcast.57, f32[2048,128]{1,0:T(8,128)S(1)} %copy-done.2), custom_call_target="tpu_custom_call" | custom-call | flops 20000000 | bytes 30000000 | tf_op jit(solution)/shard_map/side/pallas_call | solution.py:377
  19.9 0.0 copy-done.1
  19.9 0.5 low_sums.1.low_table
  20.4 4.4 %collective-permute-done.above = bf16[8,256,128]{2,1,0:T(8,128)(2,1)S(1)} collective-permute-done((bf16[8,256,128]{2,1,0:T(8,128)(2,1)}, bf16[8,256,128]{2,1,0:T(8,128)(2,1)S(1)}, u32[]{:S(2)}, u32[]{:S(2)}) %collective-permute-start) | collective-permute-done | bytes 524320 | tf_op jit(solution)/shard_map/ppermute | solution.py:376
  24.7 0.7 high_sums.1
  25.5 0.1 collective-permute-start.1
  25.6 1.3 %collective-permute-done.1 = f32[320,128]{1,0:T(8,128)S(1)} collective-permute-done((f32[320,128]{1,0:T(8,128)S(1)}, f32[320,128]{1,0:T(8,128)S(1)}, u32[]{:S(2)}, u32[]{:S(2)}) %collective-permute-start.1) | collective-permute-done | bytes 163872 | tf_op jit(solution)/shard_map/ppermute | solution.py:330
  27.0 5.3 %collective-permute-start.4 = (f32[80,128]{1,0:T(8,128)S(1)}, f32[80,128]{1,0:T(8,128)S(1)}, u32[]{:S(2)}, u32[]{:S(2)}) collective-permute-start(f32[80,128]{1,0:T(8,128)S(1)} %get-tuple-element.18), channel_id=1, source_target_pairs={{0,24},{1,25},{2,26},{3,27},{4,28},{5,29},{6,30},{7,31},{8,0},{9,1... | collective-permute-start | bytes 122888 | tf_op jit(solution)/shard_map/ppermute | solution.py:330
  32.3 0.2 collective-permute-start.3
  32.5 0.6 collective-permute-start.2
  33.1 0.3 collective-permute-done.4
  33.4 3.4 %collective-permute-done.3 = f32[80,128]{1,0:T(8,128)S(1)} collective-permute-done((f32[80,128]{1,0:T(8,128)S(1)}, f32[80,128]{1,0:T(8,128)S(1)}, u32[]{:S(2)}, u32[]{:S(2)}) %collective-permute-start.3) | collective-permute-done | bytes 40992 | tf_op jit(solution)/shard_map/ppermute | solution.py:330
  36.7 0.3 collective-permute-done.2
  37.0 4.4 %collective-permute-start.5 = (f32[80,128]{1,0:T(8,128)S(1)}, f32[80,128]{1,0:T(8,128)S(1)}, u32[]{:S(2)}, u32[]{:S(2)}) collective-permute-start(f32[80,128]{1,0:T(8,128)S(1)} %fusion.5), channel_id=1, source_target_pairs={{0,6},{1,7},{2,0},{3,1},{4,2},{5,3},{6,4},{7,5},{8,14},{9,15},{10,... | collective-permute-start | bytes 122888 | tf_op jit(solution)/shard_map/ppermute | solution.py:349
  41.4 0.5 collective-permute-start.6
  41.9 1.7 %collective-permute-start.7 = (f32[80,128]{1,0:T(8,128)S(1)}, f32[80,128]{1,0:T(8,128)S(1)}, u32[]{:S(2)}, u32[]{:S(2)}) collective-permute-start(f32[80,128]{1,0:T(8,128)S(1)} %fusion.5), channel_id=1, source_target_pairs={{0,2},{1,3},{2,4},{3,5},{4,6},{5,7},{6,0},{7,1},{8,10},{9,11},{10,... | collective-permute-start | bytes 122888 | tf_op jit(solution)/shard_map/ppermute | solution.py:349
  43.7 0.0 collective-permute-done.5
  43.7 4.8 %collective-permute-done.6 = f32[80,128]{1,0:T(8,128)S(1)} collective-permute-done((f32[80,128]{1,0:T(8,128)S(1)}, f32[80,128]{1,0:T(8,128)S(1)}, u32[]{:S(2)}, u32[]{:S(2)}) %collective-permute-start.6) | collective-permute-done | bytes 40992 | tf_op jit(solution)/shard_map/ppermute | solution.py:349
  48.5 0.0 collective-permute-done.7
  48.6 0.4 collective-permute-start.8
  49.0 1.4 %collective-permute-start.9 = (f32[80,128]{1,0:T(8,128)S(1)}, f32[80,128]{1,0:T(8,128)S(1)}, u32[]{:S(2)}, u32[]{:S(2)}) collective-permute-start(f32[80,128]{1,0:T(8,128)S(1)} %fusion.6), channel_id=1, source_target_pairs={{0,16},{1,17},{2,18},{3,19},{4,20},{5,21},{6,22},{7,23},{8,24},{9,... | collective-permute-start | bytes 122888 | tf_op jit(solution)/shard_map/ppermute | solution.py:339
  50.4 0.0 collective-permute-start.10
  50.4 1.1 %collective-permute-done.8 = f32[80,128]{1,0:T(8,128)S(1)} collective-permute-done((f32[80,128]{1,0:T(8,128)S(1)}, f32[80,128]{1,0:T(8,128)S(1)}, u32[]{:S(2)}, u32[]{:S(2)}) %collective-permute-start.8) | collective-permute-done | bytes 40992 | tf_op jit(solution)/shard_map/ppermute | solution.py:339
  51.5 1.8 %collective-permute-done.9 = f32[80,128]{1,0:T(8,128)S(1)} collective-permute-done((f32[80,128]{1,0:T(8,128)S(1)}, f32[80,128]{1,0:T(8,128)S(1)}, u32[]{:S(2)}, u32[]{:S(2)}) %collective-permute-start.9) | collective-permute-done | bytes 40992 | tf_op jit(solution)/shard_map/ppermute | solution.py:339
  53.4 1.1 %collective-permute-done.10 = f32[80,128]{1,0:T(8,128)S(1)} collective-permute-done((f32[80,128]{1,0:T(8,128)S(1)}, f32[80,128]{1,0:T(8,128)S(1)}, u32[]{:S(2)}, u32[]{:S(2)}) %collective-permute-start.10) | collective-permute-done | bytes 40992 | tf_op jit(solution)/shard_map/ppermute | solution.py:339
  54.6 4.7 %collective-permute-start.11 = (f32[320,128]{1,0:T(8,128)S(1)}, f32[320,128]{1,0:T(8,128)S(1)}, u32[]{:S(2)}, u32[]{:S(2)}) collective-permute-start(f32[320,128]{1,0:T(8,128)S(1)} %bitcast.66), channel_id=1, source_target_pairs={{0,1},{1,0},{2,3},{3,2},{4,5},{5,4},{6,7},{7,6},{8,9},{9,8},{10,11... | collective-permute-start | bytes 491528 | tf_op jit(solution)/shard_map/ppermute | solution.py:339
  59.2 1.0 %collective-permute-done.11 = f32[320,128]{1,0:T(8,128)S(1)} collective-permute-done((f32[320,128]{1,0:T(8,128)S(1)}, f32[320,128]{1,0:T(8,128)S(1)}, u32[]{:S(2)}, u32[]{:S(2)}) %collective-permute-start.11) | collective-permute-done | bytes 163872 | tf_op jit(solution)/shard_map/ppermute | solution.py:339
  60.3 0.1 fusion.2
  60.3 14.5 %basis.1 = bf16[128,2048]{1,0:T(8,128)(2,1)S(1)} custom-call(f32[640,128]{1,0:T(8,128)S(1)} %bitcast.59, bf16[8,256,128]{2,1,0:T(8,128)(2,1)S(1)} %get-tuple-element.14.sens.sens_low, bf16[8,256,128]{2,1,0:T(8,128)(2,1)S(1)} %get-tuple-element.16.sens_high), custom_call_target="tpu_custom_call" | custom-call | flops 400000000 | bytes 60000000 | tf_op jit(solution)/shard_map/basis/pallas_call | solution.py:406
  74.8 13.2 %all_to_all.5 = bf16[8,16,2048]{2,1,0:T(8,128)(2,1)S(1)} all-to-all(bf16[8,16,2048]{2,1,0:T(8,128)(2,1)S(1)} %bitcast.58), channel_id=1, replica_groups=mesh['freq'=8,'brick'=32] {'freq'}, dimensions={0} | all-to-all | bytes 1048576 | tf_op jit(solution)/shard_map/all_to_all | solution.py:420
  88.1 0.1 convert_reduce_fusion
  88.1 0.8 reshape.42
  (22 shorter events, 0.2 us)
Async XLA Ops:
  0.0 10.9 %copy-start.4 = (s32[1,256]{1,0:T(1,128)S(1)}, s32[1,256]{1,0:T(1,128)}, u32[]{:S(2)}) copy-start(s32[1,256]{1,0:T(1,128)} %codes.3) | copy-start | bytes 3076
  0.0 11.0 %copy-start.3 = (bf16[1,4,6,2,1024]{4,3,2,1,0:T(2,128)(2,1)S(1)}, bf16[1,4,6,2,1024]{4,3,2,1,0:T(2,128)(2,1)}, u32[]{:S(2)}) copy-start(bf16[1,4,6,2,1024]{4,3,2,1,0:T(2,128)(2,1)} %param.4) | copy-start | bytes 294916
  0.0 19.9 %copy-start.1 = (bf16[2,1024,128]{2,1,0:T(8,128)(2,1)S(1)}, bf16[2,1024,128]{2,1,0:T(8,128)(2,1)}, u32[]{:S(2)}) copy-start(bf16[2,1024,128]{2,1,0:T(8,128)(2,1)} %probes.3) | copy-start | bytes 1572868
  5.8 19.0 %collective-permute-start = (bf16[8,256,128]{2,1,0:T(8,128)(2,1)}, bf16[8,256,128]{2,1,0:T(8,128)(2,1)S(1)}, u32[]{:S(2)}, u32[]{:S(2)}) collective-permute-start(bf16[8,256,128]{2,1,0:T(8,128)(2,1)} %get-tuple-element.13), channel_id=1, source_target_pairs={{1,0},{2,1},{3,2},{4,3},{5,4},{6,5},{7,6},{8,7},{9,8},{10,9},{11,1... | collective-permute-start | bytes 1572872 | tf_op jit(solution)/shard_map/ppermute | solution.py:376
  11.0 2.1 %copy-start = (bf16[1,160,6,2,1024]{4,3,2,1,0:T(2,128)(2,1)S(1)}, bf16[1,160,6,2,1024]{4,3,2,1,0:T(2,128)(2,1)}, u32[]{:S(2)}) copy-start(bf16[1,160,6,2,1024]{4,3,2,1,0:T(2,128)(2,1)} %param.5) | copy-start | bytes 11796484
  13.1 1.2 %copy-start.2 = (f32[2048,128]{1,0:T(8,128)S(1)}, f32[2048,128]{1,0:T(8,128)}, u32[]{:S(2)}) copy-start(f32[2048,128]{1,0:T(8,128)} %get-tuple-element.11.low_upper) | copy-start | bytes 3145732
  25.5 1.5 %collective-permute-start.1 = (f32[320,128]{1,0:T(8,128)S(1)}, f32[320,128]{1,0:T(8,128)S(1)}, u32[]{:S(2)}, u32[]{:S(2)}) collective-permute-start(f32[320,128]{1,0:T(8,128)S(1)} %dynamic-slice_bitcast_fusion), channel_id=1, source_target_pairs={{0,1},{1,0},{2,3},{3,2},{4,5},{5,4},{6,7},{7,6},{8,9},{9,8},{10,11... | collective-permute-start | bytes 491528 | tf_op jit(solution)/shard_map/ppermute | solution.py:330
  27.0 6.4 %collective-permute-start.4 = (f32[80,128]{1,0:T(8,128)S(1)}, f32[80,128]{1,0:T(8,128)S(1)}, u32[]{:S(2)}, u32[]{:S(2)}) collective-permute-start(f32[80,128]{1,0:T(8,128)S(1)} %get-tuple-element.18), channel_id=1, source_target_pairs={{0,24},{1,25},{2,26},{3,27},{4,28},{5,29},{6,30},{7,31},{8,0},{9,1... | collective-permute-start | bytes 122888 | tf_op jit(solution)/shard_map/ppermute | solution.py:330
  32.3 4.5 %collective-permute-start.3 = (f32[80,128]{1,0:T(8,128)S(1)}, f32[80,128]{1,0:T(8,128)S(1)}, u32[]{:S(2)}, u32[]{:S(2)}) collective-permute-start(f32[80,128]{1,0:T(8,128)S(1)} %get-tuple-element.19), channel_id=1, source_target_pairs={{0,16},{1,17},{2,18},{3,19},{4,20},{5,21},{6,22},{7,23},{8,24},{9,... | collective-permute-start | bytes 122888 | tf_op jit(solution)/shard_map/ppermute | solution.py:330
  32.5 4.5 %collective-permute-start.2 = (f32[80,128]{1,0:T(8,128)S(1)}, f32[80,128]{1,0:T(8,128)S(1)}, u32[]{:S(2)}, u32[]{:S(2)}) collective-permute-start(f32[80,128]{1,0:T(8,128)S(1)} %get-tuple-element.17), channel_id=1, source_target_pairs={{0,8},{1,9},{2,10},{3,11},{4,12},{5,13},{6,14},{7,15},{8,16},{9,17... | collective-permute-start | bytes 122888 | tf_op jit(solution)/shard_map/ppermute | solution.py:330
  37.0 6.6 %collective-permute-start.5 = (f32[80,128]{1,0:T(8,128)S(1)}, f32[80,128]{1,0:T(8,128)S(1)}, u32[]{:S(2)}, u32[]{:S(2)}) collective-permute-start(f32[80,128]{1,0:T(8,128)S(1)} %fusion.5), channel_id=1, source_target_pairs={{0,6},{1,7},{2,0},{3,1},{4,2},{5,3},{6,4},{7,5},{8,14},{9,15},{10,... | collective-permute-start | bytes 122888 | tf_op jit(solution)/shard_map/ppermute | solution.py:349
  41.4 7.0 %collective-permute-start.6 = (f32[80,128]{1,0:T(8,128)S(1)}, f32[80,128]{1,0:T(8,128)S(1)}, u32[]{:S(2)}, u32[]{:S(2)}) collective-permute-start(f32[80,128]{1,0:T(8,128)S(1)} %fusion.5), channel_id=1, source_target_pairs={{0,4},{1,5},{2,6},{3,7},{4,0},{5,1},{6,2},{7,3},{8,12},{9,13},{10,... | collective-permute-start | bytes 122888 | tf_op jit(solution)/shard_map/ppermute | solution.py:349
  41.9 6.5 %collective-permute-start.7 = (f32[80,128]{1,0:T(8,128)S(1)}, f32[80,128]{1,0:T(8,128)S(1)}, u32[]{:S(2)}, u32[]{:S(2)}) collective-permute-start(f32[80,128]{1,0:T(8,128)S(1)} %fusion.5), channel_id=1, source_target_pairs={{0,2},{1,3},{2,4},{3,5},{4,6},{5,7},{6,0},{7,1},{8,10},{9,11},{10,... | collective-permute-start | bytes 122888 | tf_op jit(solution)/shard_map/ppermute | solution.py:349
  48.6 2.9 %collective-permute-start.8 = (f32[80,128]{1,0:T(8,128)S(1)}, f32[80,128]{1,0:T(8,128)S(1)}, u32[]{:S(2)}, u32[]{:S(2)}) collective-permute-start(f32[80,128]{1,0:T(8,128)S(1)} %fusion.6), channel_id=1, source_target_pairs={{0,24},{1,25},{2,26},{3,27},{4,28},{5,29},{6,30},{7,31},{8,0},{9,1... | collective-permute-start | bytes 122888 | tf_op jit(solution)/shard_map/ppermute | solution.py:339
  49.0 4.4 %collective-permute-start.9 = (f32[80,128]{1,0:T(8,128)S(1)}, f32[80,128]{1,0:T(8,128)S(1)}, u32[]{:S(2)}, u32[]{:S(2)}) collective-permute-start(f32[80,128]{1,0:T(8,128)S(1)} %fusion.6), channel_id=1, source_target_pairs={{0,16},{1,17},{2,18},{3,19},{4,20},{5,21},{6,22},{7,23},{8,24},{9,... | collective-permute-start | bytes 122888 | tf_op jit(solution)/shard_map/ppermute | solution.py:339
  50.4 4.1 %collective-permute-start.10 = (f32[80,128]{1,0:T(8,128)S(1)}, f32[80,128]{1,0:T(8,128)S(1)}, u32[]{:S(2)}, u32[]{:S(2)}) collective-permute-start(f32[80,128]{1,0:T(8,128)S(1)} %fusion.6), channel_id=1, source_target_pairs={{0,8},{1,9},{2,10},{3,11},{4,12},{5,13},{6,14},{7,15},{8,16},{9,17... | collective-permute-start | bytes 122888 | tf_op jit(solution)/shard_map/ppermute | solution.py:339
  54.6 5.7 %collective-permute-start.11 = (f32[320,128]{1,0:T(8,128)S(1)}, f32[320,128]{1,0:T(8,128)S(1)}, u32[]{:S(2)}, u32[]{:S(2)}) collective-permute-start(f32[320,128]{1,0:T(8,128)S(1)} %bitcast.66), channel_id=1, source_target_pairs={{0,1},{1,0},{2,3},{3,2},{4,5},{5,4},{6,7},{7,6},{8,9},{9,8},{10,11... | collective-permute-start | bytes 491528 | tf_op jit(solution)/shard_map/ppermute | solution.py:339

commit v3 on v2

--- a/solution.py
+++ b/solution.py
@@ -122,7 +122,7 @@
         low_upper[tile_rows(d, SUB), :] = edge_x + next_row(edge_x) + (edge_y + next_column(edge_y))
         return carry
 
-    lax.fori_loop(0, PANEL, one, 0, unroll=32)
+    lax.fori_loop(0, PANEL, one, 0, unroll=64)
 
     def block(i, carry):
         for s in range(SUB):
@@ -176,15 +176,18 @@
         pair = jnp.concatenate([sens[s], sens[s + 1]], axis=1)
         cross = cross + dot(pair, pair, 1, 1)
         sketch = sketch + dot(probes[layer, 128 * s : 128 * s + 256, :], pair, 0, 1)
-    return [cross[:128, :128], cross[:128, 128:], cross[128:, 128:], sketch[:, :128], sketch[:, 128:]]
-
-
-def low_sums_kernel(sens, probes, table):
-    for i, part in enumerate(layer_sums(sens, probes, 0)):
-        table[128 * i : 128 * i + 128, :] = part
-
-
-def high_sums_kernel(rest, above, probes, low_table, sens, table):
+    return cross, sketch
+
+
+def block_index(axis):
+    return lax.broadcasted_iota(jnp.int32, (LANES, LANES), axis)
+
+
+def low_sums_kernel(sens, probes, cross, sketch):
+    cross[...], sketch[...] = layer_sums(sens, probes, 0)
+
+
+def high_sums_kernel(rest, above, probes, low_cross, low_sketch, sens, table):
     def block(i, carry):
         for s in range(SUB):
             here = (s, tile_rows(i, 16), slice(None))
@@ -192,9 +195,14 @@
         return carry
 
     lax.fori_loop(0, PANEL // 16, block, 0)
-    for i, part in enumerate(layer_sums(sens, probes, 1)):
-        at = slice(128 * i, 128 * i + 128)
-        table[at, :] = low_table[at, :] + part
+    cross, sketch = layer_sums(sens, probes, 1)
+    cross, sketch = cross + low_cross[...], sketch + low_sketch[...]
+    table[0:128, :], table[128:256, :] = sketch[:, :128], sketch[:, 128:]
+    table[256:384, :] = cross[:128, 128:]
+    last = cross[128:, 128:]
+    table[384:512, :] = jnp.where(block_index(0) <= block_index(1), cross[:128, :128], last)
+    diagonal = jnp.sum(jnp.where(block_index(0) == block_index(1), last, 0.0), axis=0, keepdims=True)
+    table[512:544, :] = jnp.broadcast_to(diagonal, (32, LANES))
 
 
 def spread(piece):
@@ -206,13 +214,16 @@
     return jnp.where(left, spread(piece[:, at : at + 1]), spread(piece[:, HALF + at : HALF + at + 1]))
 
 
-def eliminate_panel(gram, inverse, g):
+def own_columns(gram, g):
+    return [column_of_each(gram[g], SUB * g + k) for k in range(SUB)]
+
+
+def eliminate_panel(gram, inverse, g, own):
     row = lax.broadcasted_iota(jnp.int32, (SUB, LANES), 0)
     later = range(g + 1, len(gram))
-    column = {
-        (q, k): column_of_each(gram[q], SUB * g + k) for q in (g, *later) for k in range(SUB)
-    }
-    u = {(i, k): spread(column[g, k][i : i + 1, :]) for k in range(SUB) for i in range(k + 1)}
+    column = {(q, k): column_of_each(gram[q], SUB * g + k) for q in later for k in range(SUB)}
+    following = own_columns(gram, g + 1) if later else None
+    u = {(i, k): spread(own[k][i : i + 1, :]) for k in range(SUB) for i in range(k + 1)}
     root = []
     for k in range(SUB):
         root.append(lax.rsqrt(u[k, k]))
@@ -228,6 +239,11 @@
             for j in range(k):
                 entry = entry - low[q, j] * u[j, k]
             low[q, k] = entry * root[k]
+    if later:
+        for c in range(SUB):
+            for k in range(SUB):
+                across = low[g + 1, k]
+                following[c] = following[c] - across * spread(across[c : c + 1, :])
     for table in (gram, inverse):
         lead = [spread(table[g][k : k + 1, :]) for k in range(SUB)]
         for k in range(SUB):
@@ -240,6 +256,7 @@
         for q in later:
             for k in range(SUB):
                 table[q] = table[q] - low[q, k] * lead[k]
+    return following
 
 
 def exact_dot(left, right, left_dim, right_dim):
@@ -252,13 +269,15 @@
 
 
 def basis_kernel(table, sens_low, sens_high, parts, basis, sketch, cross):
-    corner = table[128:256, :]
-    cross[0:128, 0:128] = table[0:128, :]
+    sketch[0, :, 0:128], sketch[0, :, 128:256] = table[0:128, :], table[128:256, :]
+    corner, packed = table[256:384, :], table[384:512, :]
+    turned = packed.T
+    row, column = block_index(0), block_index(1)
+    cross[0:128, 0:128] = jnp.where(row <= column, packed, turned)
     cross[0:128, 128:256] = corner
     cross[128:256, 0:128] = corner.T
-    cross[128:256, 128:256] = table[256:384, :]
-    sketch[0, :, 0:128] = table[384:512, :]
-    sketch[0, :, 128:256] = table[512:640, :]
+    last = jnp.where(row > column, packed, turned)
+    cross[128:256, 128:256] = jnp.where(row == column, table[512:513, :], last)
     identity = jnp.where(
         lax.broadcasted_iota(jnp.int32, (HALF, LANES), 0)
         == lax.broadcasted_iota(jnp.int32, (HALF, LANES), 1) % HALF,
@@ -284,8 +303,9 @@
         moved = exact_dot(jnp.concatenate(rows, axis=0), cross[...], 1, 0)
         gram_rows = [gram[SUB * g : SUB * g + SUB, :] for g in range(HALF // SUB)]
         inverse_rows = [identity[SUB * g : SUB * g + SUB, :] for g in range(HALF // SUB)]
+        own = own_columns(gram_rows, 0)
         for g in range(HALF // SUB):
-            eliminate_panel(gram_rows, inverse_rows, g)
+            own = eliminate_panel(gram_rows, inverse_rows, g, own)
         inverse = jnp.concatenate(inverse_rows, axis=0)
         for at, (half, stage) in enumerate(work):
             both = jnp.concatenate([rows[at], moved[HALF * at : HALF * at + HALF, :]], axis=1)
@@ -309,14 +329,6 @@
     return index // 8, index // 2 % 4, index % 2
 
 
-def along_x(k):
-    return brick_moves(lambda i: (i + 8 * k) % 32)
-
-
-def along_z(k):
-    return brick_moves(lambda i: i // 8 * 8 + (i % 8 + 2 * k) % 8)
-
-
 def across_cores():
     return brick_moves(lambda i: i ^ 1)
 
@@ -325,33 +337,38 @@
     return lax.dynamic_index_in_dim(parts, index, 0, keepdims=False)
 
 
-def scattered_sum(parts, place, moves):
-    count = len(moves) + 1
-    got = [lax.ppermute(pick(parts, (place + k) % count), "brick", moves[k - 1]) for k in range(1, count)]
-    total = pick(parts, place)
-    for part in got:
-        total = total + part
-    return total
-
-
-def gathered(part, place, moves):
-    count = len(moves) + 1
-    got = [part] + [lax.ppermute(part, "brick", move) for move in moves]
-    back = jnp.stack((got[::-1] + got[::-1]))
-    return lax.dynamic_slice_in_dim(back, (count - 1 - place) % count, count, 0)
+def pairs(i, step):
+    return i ^ 1 if step == 0 else 3 - i
+
+
+def pair_x(step):
+    return brick_moves(lambda i: pairs(i // 8, step) * 8 + i % 8)
+
+
+def pair_z(step):
+    return brick_moves(lambda i: i // 8 * 8 + pairs(i % 8 // 2, step) * 2 + i % 2)
+
+
+def halved(table, keep, move):
+    parts = table.reshape(2, -1, 128)
+    return pick(parts, keep) + lax.ppermute(pick(parts, 1 - keep), "brick", move)
+
+
+def doubled(part, kept, move):
+    other = lax.ppermute(part, "brick", move)
+    return jnp.where(kept == 0, jnp.concatenate([part, other]), jnp.concatenate([other, part]))
 
 
 def brick_sum(table):
-    x, z, core = coordinates(lax.axis_index("brick"))
-    x_moves = [along_x(k) for k in (1, 2, 3)]
-    part = scattered_sum(table.reshape(2, -1, 128), core, [across_cores()])
-    part = scattered_sum(part.reshape(4, -1, 128), x, x_moves)
-    got = [part] + [lax.ppermute(part, "brick", along_z(k)) for k in (1, 2, 3)]
-    ring = jnp.stack(got[::-1] + got[::-1])
-    ring = lax.dynamic_slice_in_dim(ring, (3 - z) % 4, 4, 0)
-    part = (ring[0] + ring[1]) + (ring[2] + ring[3])
-    part = gathered(part, x, x_moves).reshape(-1, 128)
-    return gathered(part, core, [across_cores()]).reshape(table.shape)
+    x, _, core = coordinates(lax.axis_index("brick"))
+    inner = ((x == 1) | (x == 2)).astype(jnp.int32)
+    part = halved(table, core, across_cores())
+    part = halved(part, inner, pair_x(0))
+    part = part + lax.ppermute(part, "brick", pair_x(1))
+    part = part + lax.ppermute(part, "brick", pair_z(0))
+    part = part + lax.ppermute(part, "brick", pair_z(1))
+    part = doubled(part, inner, pair_x(0))
+    return doubled(part, core, across_cores())
 
 
 def shape(*dims, dtype=jnp.float32):
@@ -384,24 +401,24 @@
         cost_estimate=cost(20_000_000, 30_000_000),
         name="side",
     )(datum, fwd, adj, low_upper)
-    low_table = pl.pallas_call(
+    low_cross, low_sketch = pl.pallas_call(
         low_sums_kernel,
         in_specs=[WHOLE] * 2,
-        out_specs=WHOLE,
-        out_shape=shape(640, 128),
+        out_specs=(WHOLE, WHOLE),
+        out_shape=(shape(PANEL, PANEL), shape(PROBES, PANEL)),
         compiler_params=PARAMS,
         cost_estimate=cost(200_000_000, 3_000_000),
         name="low_sums",
     )(sens_low, probes)
     sens_high, table = pl.pallas_call(
         high_sums_kernel,
-        in_specs=[WHOLE] * 4,
+        in_specs=[WHOLE] * 5,
         out_specs=(WHOLE, WHOLE),
-        out_shape=(shape(*layer, dtype=jnp.bfloat16), shape(640, 128)),
+        out_shape=(shape(*layer, dtype=jnp.bfloat16), shape(544, 128)),
         compiler_params=PARAMS,
         cost_estimate=cost(200_000_000, 3_000_000),
         name="high_sums",
-    )(rest, above, probes, low_table)
+    )(rest, above, probes, low_cross, low_sketch)
     table = brick_sum(table)
     parts = pl.pallas_call(
         basis_kernel,

time: 89.2 us -> 85.7 us (0.961)
  Pallas kernels: 27 us -> 25.7 us
  waiting for transfers between devices: 19.4 us -> 18.1 us
    ppermute x11 -> x7, waiting for transfers between devices: 15.1 us -> 13.8 us  [the longest x2 4.43 us: doubled(): other = lax.ppermute(part, 'brick', move)]
    pallas_call x1, Pallas kernels: 14.5 us -> 13.6 us  [local(): pl.pallas_call(basis_kernel, in_specs=[WHOLE] * 3, out_specs=WHOLE, out_s...]
    ppermute x11 -> x7, starting transfers between devices: 19.3 us -> 18.8 us  [the longest x2 5.36 us: doubled(): other = lax.ppermute(part, 'brick', move)]
    unnamed x23 -> x10, local copies, waits for them, and re-layouts: 3.41 us -> 3.34 us
  transfers between devices with their start and end apart: 12 -> 8, of which waited for: 10 -> 8; matrix products, arithmetic and copies ran while one was open for 0% -> 0% of each run, Pallas kernels for 7% -> 7%
where the time goes in v3:
time: 85.7 us; the launch traced here: 85.5 us
  Pallas kernels  25.7 us (30%)
  starting transfers between devices  23.9 us (28%)
  waiting for transfers between devices  18.1 us (21%)
  blocking collectives  13.2 us (15%)
  local copies, waits for them, and re-layouts  4.15 us (5%)
    pallas_call x1, Pallas kernels, local(): pl.pallas_call(basis_kernel, in_specs=[WHOLE] * 3, out_specs=WHOLE, out_s...  13.6 us
    all_to_all x1, blocking collectives, local(): parts = lax.all_to_all(parts.reshape(8, 16, 2048), 'freq', 0, 0)  13.2 us
    pallas_call x1, Pallas kernels, local(): pl.pallas_call(side_kernel, in_specs=[WHOLE, anywhere, anywhere, WHOLE],...  5.56 us
    pallas_call x1, Pallas kernels, local(): pl.pallas_call(upper_kernel, in_specs=[WHOLE, anywhere, anywhere], out_sp...  5.41 us
    ppermute x2, starting transfers between devices, doubled(): other = lax.ppermute(part, 'brick', move)  5.36 us
    ppermute x1, starting transfers between devices, local(): lax.ppermute(lowest, 'brick', [(i + 1, i) for i in devices if i + 1 in de...  5.15 us
    ppermute x1, starting transfers between devices, brick_sum(): part = part + lax.ppermute(part, 'brick', pair_z(1))  5.02 us
    ppermute x2, waiting for transfers between devices, doubled(): other = lax.ppermute(part, 'brick', move)  4.43 us
  transfers between devices with their start and end apart: 8, of which 8 were waited for; matrix products, arithmetic and copies ran while one was open for 0% of the time, Pallas kernels for 7%

profile of v3, /device:TPU:1, one launch (start us, length us, event | category | flops | bytes accessed | tf_op | source)
XLA Modules:
  0.0 85.5 jit_solution(10637724541411211659)
XLA Ops:
  0.0 0.0 copy-start.4
  0.0 0.0 copy-start.3
  0.0 0.0 copy-start.1
  0.0 5.4 %upper.1 = (f32[2048,128]{1,0:T(8,128)}, bf16[8,256,128]{2,1,0:T(8,128)(2,1)}) custom-call(s32[1,256]{1,0:T(1,128)} %codes.3, bf16[4,6,16,128]{3,2,1,0:T(8,128)(2,1)} %bitcast.24, bf16[160,6,16,128]{3,2,1,0:T(8,128)(2,1)} %bitcast.21), custom_call_target="tpu_custom_call" | custom-call | flops 10000000 | bytes 8000000 | tf_op jit(solution)/shard_map/upper/pallas_call | solution.py:382
  5.4 5.1 %collective-permute-start = (bf16[8,256,128]{2,1,0:T(8,128)(2,1)}, bf16[8,256,128]{2,1,0:T(8,128)(2,1)S(1)}, u32[]{:S(2)}, u32[]{:S(2)}) collective-permute-start(bf16[8,256,128]{2,1,0:T(8,128)(2,1)} %get-tuple-element.15), channel_id=1, source_target_pairs={{1,0},{2,1},{3,2},{4,3},{5,4},{6,5},{7,6},{8,7},{9,8},{10,9},{11,1... | collective-permute-start | bytes 1572872 | tf_op jit(solution)/shard_map/ppermute | solution.py:393
  10.6 0.0 copy-done.4
  10.6 0.0 copy-done.3
  10.6 0.0 copy-start
  10.6 2.1 %copy-done = bf16[1,160,6,2,1024]{4,3,2,1,0:T(2,128)(2,1)S(1)} copy-done((bf16[1,160,6,2,1024]{4,3,2,1,0:T(2,128)(2,1)S(1)}, bf16[1,160,6,2,1024]{4,3,2,1,0:T(2,128)(2,1)}, u32[]{:S(2)}) %copy-start) | copy-done | bytes 3932184
  12.7 0.0 copy-start.2
  12.7 1.2 %copy-done.2 = f32[2048,128]{1,0:T(8,128)S(1)} copy-done((f32[2048,128]{1,0:T(8,128)S(1)}, f32[2048,128]{1,0:T(8,128)}, u32[]{:S(2)}) %copy-start.2) | copy-done | bytes 1048600
  14.0 5.6 %side.1 = (bf16[8,256,128]{2,1,0:T(8,128)(2,1)S(1)}, f32[8,256,128]{2,1,0:T(8,128)S(1)}) custom-call(s32[1,256]{1,0:T(1,128)S(1)} %copy-done.4, bf16[4,6,16,128]{3,2,1,0:T(8,128)(2,1)S(1)} %bitcast.25, bf16[160,6,16,128]{3,2,1,0:T(8,128)(2,1)S(1)} %bitcast.22, f32[2048,128]{1,0:T(8,128)S(1)} %copy-done.2), custom_call_target="tpu_custom_call" | custom-call | flops 20000000 | bytes 30000000 | tf_op jit(solution)/shard_map/side/pallas_call | solution.py:394
  19.5 0.0 copy-done.1
  19.5 0.5 low_sums.1
  20.0 4.4 %collective-permute-done.above = bf16[8,256,128]{2,1,0:T(8,128)(2,1)S(1)} collective-permute-done((bf16[8,256,128]{2,1,0:T(8,128)(2,1)}, bf16[8,256,128]{2,1,0:T(8,128)(2,1)S(1)}, u32[]{:S(2)}, u32[]{:S(2)}) %collective-permute-start) | collective-permute-done | bytes 524320 | tf_op jit(solution)/shard_map/ppermute | solution.py:393
  24.4 0.7 high_sums.1
  25.1 0.1 collective-permute-start.1
  25.3 1.3 %collective-permute-done.1 = f32[272,128]{1,0:T(8,128)S(1)} collective-permute-done((f32[272,128]{1,0:T(8,128)S(1)}, f32[272,128]{1,0:T(8,128)S(1)}, u32[]{:S(2)}, u32[]{:S(2)}) %collective-permute-start.1) | collective-permute-done | bytes 139296 | tf_op jit(solution)/shard_map/ppermute | solution.py:354
  26.6 3.7 %collective-permute-start.2 = (f32[136,128]{1,0:T(8,128)S(1)}, f32[136,128]{1,0:T(8,128)S(1)}, u32[]{:S(2)}, u32[]{:S(2)}) collective-permute-start(f32[136,128]{1,0:T(8,128)S(1)} %dynamic-slice_bitcast_fusion.1), channel_id=1, source_target_pairs={{0,8},{1,9},{2,10},{3,11},{4,12},{5,13},{6,14},{7,15},{8,0},{9,1},... | collective-permute-start | bytes 208904 | tf_op jit(solution)/shard_map/ppermute | solution.py:354
  30.4 2.3 %collective-permute-done.2 = f32[136,128]{1,0:T(8,128)S(1)} collective-permute-done((f32[136,128]{1,0:T(8,128)S(1)}, f32[136,128]{1,0:T(8,128)S(1)}, u32[]{:S(2)}, u32[]{:S(2)}) %collective-permute-start.2) | collective-permute-done | bytes 69664 | tf_op jit(solution)/shard_map/ppermute | solution.py:354
  32.6 2.5 %collective-permute-start.3 = (f32[136,128]{1,0:T(8,128)S(1)}, f32[136,128]{1,0:T(8,128)S(1)}, u32[]{:S(2)}, u32[]{:S(2)}) collective-permute-start(f32[136,128]{1,0:T(8,128)S(1)} %bitcast_add_fusion.1), channel_id=1, source_target_pairs={{0,24},{1,25},{2,26},{3,27},{4,28},{5,29},{6,30},{7,31},{8,16},{9,... | collective-permute-start | bytes 208904 | tf_op jit(solution)/shard_map/ppermute | solution.py:367
  35.2 1.9 %collective-permute-done.3 = f32[136,128]{1,0:T(8,128)S(1)} collective-permute-done((f32[136,128]{1,0:T(8,128)S(1)}, f32[136,128]{1,0:T(8,128)S(1)}, u32[]{:S(2)}, u32[]{:S(2)}) %collective-permute-start.3) | collective-permute-done | bytes 69664 | tf_op jit(solution)/shard_map/ppermute | solution.py:367
  37.1 2.0 %collective-permute-start.4 = (f32[136,128]{1,0:T(8,128)S(1)}, f32[136,128]{1,0:T(8,128)S(1)}, u32[]{:S(2)}, u32[]{:S(2)}) collective-permute-start(f32[136,128]{1,0:T(8,128)S(1)} %add.43), channel_id=1, source_target_pairs={{0,2},{1,3},{2,0},{3,1},{4,6},{5,7},{6,4},{7,5},{8,10},{9,11},{10,... | collective-permute-start | bytes 208904 | tf_op jit(solution)/shard_map/ppermute | solution.py:368
  39.1 2.1 %collective-permute-done.4 = f32[136,128]{1,0:T(8,128)S(1)} collective-permute-done((f32[136,128]{1,0:T(8,128)S(1)}, f32[136,128]{1,0:T(8,128)S(1)}, u32[]{:S(2)}, u32[]{:S(2)}) %collective-permute-start.4) | collective-permute-done | bytes 69664 | tf_op jit(solution)/shard_map/ppermute | solution.py:368
  41.3 5.0 %collective-permute-start.5 = (f32[136,128]{1,0:T(8,128)S(1)}, f32[136,128]{1,0:T(8,128)S(1)}, u32[]{:S(2)}, u32[]{:S(2)}) collective-permute-start(f32[136,128]{1,0:T(8,128)S(1)} %add.44), channel_id=1, source_target_pairs={{0,6},{1,7},{2,4},{3,5},{4,2},{5,3},{6,0},{7,1},{8,14},{9,15},{10,... | collective-permute-start | bytes 208904 | tf_op jit(solution)/shard_map/ppermute | solution.py:369
  46.3 1.7 %collective-permute-done.5 = f32[136,128]{1,0:T(8,128)S(1)} collective-permute-done((f32[136,128]{1,0:T(8,128)S(1)}, f32[136,128]{1,0:T(8,128)S(1)}, u32[]{:S(2)}, u32[]{:S(2)}) %collective-permute-start.5) | collective-permute-done | bytes 69664 | tf_op jit(solution)/shard_map/ppermute | solution.py:369
  48.0 0.1 collective-permute-start.6
  48.1 3.4 %collective-permute-done.6 = f32[136,128]{1,0:T(8,128)S(1)} collective-permute-done((f32[136,128]{1,0:T(8,128)S(1)}, f32[136,128]{1,0:T(8,128)S(1)}, u32[]{:S(2)}, u32[]{:S(2)}) %collective-permute-start.6) | collective-permute-done | bytes 69664 | tf_op jit(solution)/shard_map/ppermute | solution.py:358
  51.6 5.3 %collective-permute-start.7 = (f32[272,128]{1,0:T(8,128)S(1)}, f32[272,128]{1,0:T(8,128)S(1)}, u32[]{:S(2)}, u32[]{:S(2)}) collective-permute-start(f32[272,128]{1,0:T(8,128)S(1)} %maximum_select_fusion.1), channel_id=1, source_target_pairs={{0,1},{1,0},{2,3},{3,2},{4,5},{5,4},{6,7},{7,6},{8,9},{9,8},{10,11... | collective-permute-start | bytes 417800 | tf_op jit(solution)/shard_map/ppermute | solution.py:358
  56.8 1.0 %collective-permute-done.7 = f32[272,128]{1,0:T(8,128)S(1)} collective-permute-done((f32[272,128]{1,0:T(8,128)S(1)}, f32[272,128]{1,0:T(8,128)S(1)}, u32[]{:S(2)}, u32[]{:S(2)}) %collective-permute-start.7) | collective-permute-done | bytes 139296 | tf_op jit(solution)/shard_map/ppermute | solution.py:358
  57.8 13.6 %basis.1 = bf16[128,2048]{1,0:T(8,128)(2,1)S(1)} custom-call(f32[544,128]{1,0:T(8,128)S(1)} %maximum_select_fusion.table, bf16[8,256,128]{2,1,0:T(8,128)(2,1)S(1)} %get-tuple-element.16.sens.sens_low, bf16[8,256,128]{2,1,0:T(8,128)(2,1)S(1)} %get-tuple-element.20.sens_high), custom_call_target="tpu_custom_call" | custom-call | flops 400000000 | bytes 60000000 | tf_op jit(solution)/shard_map/basis/pallas_call | solution.py:423
  71.4 13.2 %all_to_all.5 = bf16[8,16,2048]{2,1,0:T(8,128)(2,1)S(1)} all-to-all(bf16[8,16,2048]{2,1,0:T(8,128)(2,1)S(1)} %bitcast.23), channel_id=1, replica_groups=mesh['freq'=8,'brick'=32] {'freq'}, dimensions={0} | all-to-all | bytes 1048576 | tf_op jit(solution)/shard_map/all_to_all | solution.py:437
  84.6 0.1 convert_reduce_fusion
  84.7 0.8 reshape.31
  (9 shorter events, 0.1 us)
Async XLA Ops:
  0.0 10.6 %copy-start.4 = (s32[1,256]{1,0:T(1,128)S(1)}, s32[1,256]{1,0:T(1,128)}, u32[]{:S(2)}) copy-start(s32[1,256]{1,0:T(1,128)} %codes.3) | copy-start | bytes 3076
  0.0 10.6 %copy-start.3 = (bf16[1,4,6,2,1024]{4,3,2,1,0:T(2,128)(2,1)S(1)}, bf16[1,4,6,2,1024]{4,3,2,1,0:T(2,128)(2,1)}, u32[]{:S(2)}) copy-start(bf16[1,4,6,2,1024]{4,3,2,1,0:T(2,128)(2,1)} %param.4) | copy-start | bytes 294916
  0.0 19.5 %copy-start.1 = (bf16[2,1024,128]{2,1,0:T(8,128)(2,1)S(1)}, bf16[2,1024,128]{2,1,0:T(8,128)(2,1)}, u32[]{:S(2)}) copy-start(bf16[2,1024,128]{2,1,0:T(8,128)(2,1)} %probes.3) | copy-start | bytes 1572868
  5.4 19.0 %collective-permute-start = (bf16[8,256,128]{2,1,0:T(8,128)(2,1)}, bf16[8,256,128]{2,1,0:T(8,128)(2,1)S(1)}, u32[]{:S(2)}, u32[]{:S(2)}) collective-permute-start(bf16[8,256,128]{2,1,0:T(8,128)(2,1)} %get-tuple-element.15), channel_id=1, source_target_pairs={{1,0},{2,1},{3,2},{4,3},{5,4},{6,5},{7,6},{8,7},{9,8},{10,9},{11,1... | collective-permute-start | bytes 1572872 | tf_op jit(solution)/shard_map/ppermute | solution.py:393
  10.6 2.1 %copy-start = (bf16[1,160,6,2,1024]{4,3,2,1,0:T(2,128)(2,1)S(1)}, bf16[1,160,6,2,1024]{4,3,2,1,0:T(2,128)(2,1)}, u32[]{:S(2)}) copy-start(bf16[1,160,6,2,1024]{4,3,2,1,0:T(2,128)(2,1)} %param.5) | copy-start | bytes 11796484
  12.7 1.2 %copy-start.2 = (f32[2048,128]{1,0:T(8,128)S(1)}, f32[2048,128]{1,0:T(8,128)}, u32[]{:S(2)}) copy-start(f32[2048,128]{1,0:T(8,128)} %get-tuple-element.13.low_upper) | copy-start | bytes 3145732
  25.1 1.4 %collective-permute-start.1 = (f32[272,128]{1,0:T(8,128)S(1)}, f32[272,128]{1,0:T(8,128)S(1)}, u32[]{:S(2)}, u32[]{:S(2)}) collective-permute-start(f32[272,128]{1,0:T(8,128)S(1)} %dynamic-slice_bitcast_fusion), channel_id=1, source_target_pairs={{0,1},{1,0},{2,3},{3,2},{4,5},{5,4},{6,7},{7,6},{8,9},{9,8},{10,11... | collective-permute-start | bytes 417800 | tf_op jit(solution)/shard_map/ppermute | solution.py:354
  26.6 6.0 %collective-permute-start.2 = (f32[136,128]{1,0:T(8,128)S(1)}, f32[136,128]{1,0:T(8,128)S(1)}, u32[]{:S(2)}, u32[]{:S(2)}) collective-permute-start(f32[136,128]{1,0:T(8,128)S(1)} %dynamic-slice_bitcast_fusion.1), channel_id=1, source_target_pairs={{0,8},{1,9},{2,10},{3,11},{4,12},{5,13},{6,14},{7,15},{8,0},{9,1},... | collective-permute-start | bytes 208904 | tf_op jit(solution)/shard_map/ppermute | solution.py:354
  32.6 4.5 %collective-permute-start.3 = (f32[136,128]{1,0:T(8,128)S(1)}, f32[136,128]{1,0:T(8,128)S(1)}, u32[]{:S(2)}, u32[]{:S(2)}) collective-permute-start(f32[136,128]{1,0:T(8,128)S(1)} %bitcast_add_fusion.1), channel_id=1, source_target_pairs={{0,24},{1,25},{2,26},{3,27},{4,28},{5,29},{6,30},{7,31},{8,16},{9,... | collective-permute-start | bytes 208904 | tf_op jit(solution)/shard_map/ppermute | solution.py:367
  37.1 4.1 %collective-permute-start.4 = (f32[136,128]{1,0:T(8,128)S(1)}, f32[136,128]{1,0:T(8,128)S(1)}, u32[]{:S(2)}, u32[]{:S(2)}) collective-permute-start(f32[136,128]{1,0:T(8,128)S(1)} %add.43), channel_id=1, source_target_pairs={{0,2},{1,3},{2,0},{3,1},{4,6},{5,7},{6,4},{7,5},{8,10},{9,11},{10,... | collective-permute-start | bytes 208904 | tf_op jit(solution)/shard_map/ppermute | solution.py:368
  41.3 6.7 %collective-permute-start.5 = (f32[136,128]{1,0:T(8,128)S(1)}, f32[136,128]{1,0:T(8,128)S(1)}, u32[]{:S(2)}, u32[]{:S(2)}) collective-permute-start(f32[136,128]{1,0:T(8,128)S(1)} %add.44), channel_id=1, source_target_pairs={{0,6},{1,7},{2,4},{3,5},{4,2},{5,3},{6,0},{7,1},{8,14},{9,15},{10,... | collective-permute-start | bytes 208904 | tf_op jit(solution)/shard_map/ppermute | solution.py:369
  48.0 3.5 %collective-permute-start.6 = (f32[136,128]{1,0:T(8,128)S(1)}, f32[136,128]{1,0:T(8,128)S(1)}, u32[]{:S(2)}, u32[]{:S(2)}) collective-permute-start(f32[136,128]{1,0:T(8,128)S(1)} %add.45), channel_id=1, source_target_pairs={{0,8},{1,9},{2,10},{3,11},{4,12},{5,13},{6,14},{7,15},{8,0},{9,1},... | collective-permute-start | bytes 208904 | tf_op jit(solution)/shard_map/ppermute | solution.py:358
  51.6 6.3 %collective-permute-start.7 = (f32[272,128]{1,0:T(8,128)S(1)}, f32[272,128]{1,0:T(8,128)S(1)}, u32[]{:S(2)}, u32[]{:S(2)}) collective-permute-start(f32[272,128]{1,0:T(8,128)S(1)} %maximum_select_fusion.1), channel_id=1, source_target_pairs={{0,1},{1,0},{2,3},{3,2},{4,5},{5,4},{6,7},{7,6},{8,9},{9,8},{10,11... | collective-permute-start | bytes 417800 | tf_op jit(solution)/shard_map/ppermute | solution.py:358

commit v4 on v3

--- a/solution.py
+++ b/solution.py
@@ -114,7 +114,7 @@
     return [table[pl.ds(block * 128 + half * 64 + s, SUB, stride=SUB), :] for half in range(2)]
 
 
-def upper_kernel(codes, fwd, adj, low_upper, lowest, *scratch):
+def upper_kernel(codes, fwd, adj, lowest, low_upper, *scratch):
     product = load_rows(4, codes, fwd, adj, scratch)
 
     def one(d, carry):
@@ -133,17 +133,19 @@
     lax.fori_loop(0, PANEL // 16, block, 0, unroll=2)
 
 
-def side_kernel(codes, fwd, adj, low_upper, sens, rest, low, high, *scratch):
+def side_kernel(codes, fwd, adj, sens, rest, low, high, *scratch):
     product = load_rows(6, codes, fwd, adj, scratch)
 
     def one(d, carry):
-        edge_x, edge_y = product(d, 0, 1), product(d, 1, 1)
-        edge_z = [product(d, 2, layer) for layer in range(2)]
-        across = edge_y + next_column(edge_y)
-        down = [edge_x + (edge + next_column(edge)) for edge in edge_z]
-        here = tile_rows(d, SUB)
-        low[here, :] = low_upper[here, :] + (across + (down[0] + next_row(down[0])))
-        high[here, :] = across + (down[1] + next_row(down[1]))
+        edge_x, edge_y, edge_z = [
+            [product(d, orientation, layer) for layer in range(2)] for orientation in range(3)
+        ]
+        paired = [edge + next_column(edge) for edge in edge_z]
+        across = edge_y[1] + next_column(edge_y[1])
+        both = edge_y[0] + next_column(edge_y[0]) + across
+        down = [edge_x[0] + edge_x[1] + paired[0], edge_x[1] + paired[1]]
+        low[tile_rows(d, SUB), :] = both + (down[0] + next_row(down[0]))
+        high[tile_rows(d, SUB), :] = across + (down[1] + next_row(down[1]))
         return carry
 
     lax.fori_loop(0, PANEL, one, 0, unroll=16)
@@ -362,13 +364,19 @@
 def brick_sum(table):
     x, _, core = coordinates(lax.axis_index("brick"))
     inner = ((x == 1) | (x == 2)).astype(jnp.int32)
-    part = halved(table, core, across_cores())
-    part = halved(part, inner, pair_x(0))
+    moves = [pair_x(0), across_cores(), brick_moves(lambda i: pairs(i // 8, 0) * 8 + (i % 8 ^ 1))]
+    quarters = table.reshape(4, -1, 128)
+    place = core * 2 + inner
+    part = pick(quarters, place)
+    got = [lax.ppermute(pick(quarters, place ^ (k + 1)), "brick", moves[k]) for k in range(3)]
+    part = (part + got[0]) + (got[1] + got[2])
     part = part + lax.ppermute(part, "brick", pair_x(1))
     part = part + lax.ppermute(part, "brick", pair_z(0))
     part = part + lax.ppermute(part, "brick", pair_z(1))
-    part = doubled(part, inner, pair_x(0))
-    return doubled(part, core, across_cores())
+    got = [lax.ppermute(part, "brick", move) for move in moves]
+    own = jnp.where(inner == 0, jnp.concatenate([part, got[0]]), jnp.concatenate([got[0], part]))
+    other = jnp.where(inner == 0, jnp.concatenate(got[1:]), jnp.concatenate(got[:0:-1]))
+    return jnp.where(core == 0, jnp.concatenate([own, other]), jnp.concatenate([other, own]))
 
 
 def shape(*dims, dtype=jnp.float32):
@@ -379,12 +387,12 @@
     fwd, adj = tiled(forward), tiled(adjoint)
     layer = (SUB, PANEL, LANES)
     anywhere = pl.BlockSpec(memory_space=pl.ANY)
-    low_upper, lowest = pl.pallas_call(
+    lowest = pl.pallas_call(
         upper_kernel,
         in_specs=[WHOLE, anywhere, anywhere],
-        out_specs=(WHOLE, WHOLE),
-        out_shape=(shape(PANEL * SUB, LANES), shape(*layer, dtype=jnp.bfloat16)),
-        scratch_shapes=row_scratch(4),
+        out_specs=WHOLE,
+        out_shape=shape(*layer, dtype=jnp.bfloat16),
+        scratch_shapes=[pltpu.VMEM((PANEL * SUB, LANES), jnp.float32)] + row_scratch(4),
         compiler_params=pltpu.CompilerParams(vmem_limit_bytes=60 * 1024 * 1024),
         cost_estimate=cost(10_000_000, 8_000_000),
         name="upper",
@@ -393,14 +401,14 @@
     above = lax.ppermute(lowest, "brick", [(i + 1, i) for i in devices if i + 1 in devices])
     sens_low, rest = pl.pallas_call(
         side_kernel,
-        in_specs=[WHOLE, anywhere, anywhere, WHOLE],
+        in_specs=[WHOLE, anywhere, anywhere],
         out_specs=(WHOLE, WHOLE),
         out_shape=(shape(*layer, dtype=jnp.bfloat16), shape(*layer)),
         scratch_shapes=[pltpu.VMEM((PANEL * SUB, LANES), jnp.float32)] * 2 + row_scratch(6),
         compiler_params=PARAMS,
         cost_estimate=cost(20_000_000, 30_000_000),
         name="side",
-    )(datum, fwd, adj, low_upper)
+    )(datum, fwd, adj)
     low_cross, low_sketch = pl.pallas_call(
         low_sums_kernel,
         in_specs=[WHOLE] * 2,

time: 85.7 us -> 85.1 us (level)
  waiting for transfers between devices: 18.1 us -> 21.2 us
  starting transfers between devices: 23.9 us -> 21.1 us
  local copies, waits for them, and re-layouts: 4.15 us -> 2.91 us
    ppermute x1, waiting for transfers between devices: 2.14 us -> 4.14 us  [brick_sum(): part = part + lax.ppermute(part, 'brick', pair_z(0))]
    ppermute x1, starting transfers between devices: 5.02 us -> 3.07 us  [brick_sum(): part = part + lax.ppermute(part, 'brick', pair_z(1))]
    unnamed x10 -> x8, local copies, waits for them, and re-layouts: 3.34 us -> 2.12 us
    ppermute x4 -> x6, waiting for transfers between devices: 8.01 us -> 6.79 us  [the longest x3 3.79 us: brick_sum(): lax.ppermute(pick(quarters, place ^ k + 1), 'brick', moves[k])]
    ppermute x1, waiting for transfers between devices: 4.39 us -> 5.55 us  [local(): lax.ppermute(lowest, 'brick', [(i + 1, i) for i in devices if i + 1 in de...]
    ppermute x4 -> x6, starting transfers between devices: 9.19 us -> 9.03 us  [the longest x3 4.64 us: brick_sum(): got = [lax.ppermute(part, 'brick', move) for move in moves]]
  transfers between devices with their start and end apart: 8 -> 10, of which waited for: 8 -> 7; matrix products, arithmetic and copies ran while one was open for 0% -> 0% of each run, Pallas kernels for 7% -> 7%
where the time goes in v4:
time: 85.1 us; the launch traced here: 84.7 us
  Pallas kernels  25.4 us (30%)
  waiting for transfers between devices  21.2 us (25%)
  starting transfers between devices  21.1 us (25%)
  blocking collectives  13.8 us (16%)
  local copies, waits for them, and re-layouts  2.91 us (3%)
    all_to_all x1, blocking collectives, local(): parts = lax.all_to_all(parts.reshape(8, 16, 2048), 'freq', 0, 0)  13.8 us
    pallas_call x1, Pallas kernels, local(): pl.pallas_call(basis_kernel, in_specs=[WHOLE] * 3, out_specs=WHOLE, out_s...  13.6 us
    pallas_call x1, Pallas kernels, local(): pl.pallas_call(side_kernel, in_specs=[WHOLE, anywhere, anywhere], out_spe...  5.59 us
    ppermute x1, waiting for transfers between devices, local(): lax.ppermute(lowest, 'brick', [(i + 1, i) for i in devices if i + 1 in de...  5.55 us
    ppermute x1, starting transfers between devices, local(): lax.ppermute(lowest, 'brick', [(i + 1, i) for i in devices if i + 1 in de...  5.15 us
    pallas_call x1, Pallas kernels, local(): pl.pallas_call(upper_kernel, in_specs=[WHOLE, anywhere, anywhere], out_sp...  5.04 us
    ppermute x3, starting transfers between devices, brick_sum(): got = [lax.ppermute(part, 'brick', move) for move in moves]  4.64 us
    ppermute x3, starting transfers between devices, brick_sum(): lax.ppermute(pick(quarters, place ^ k + 1), 'brick', moves[k])  4.38 us
  transfers between devices with their start and end apart: 10, of which 7 were waited for; matrix products, arithmetic and copies ran while one was open for 0% of the time, Pallas kernels for 7%

profile of v4, /device:TPU:1, one launch (start us, length us, event | category | flops | bytes accessed | tf_op | source)
XLA Modules:
  0.0 84.7 jit_solution(15919363622135170065)
XLA Ops:
  0.0 0.0 copy-start.3
  0.0 0.0 copy-start.2
  0.0 0.0 copy-start.1
  0.0 5.0 %upper.1 = bf16[8,256,128]{2,1,0:T(8,128)(2,1)} custom-call(s32[1,256]{1,0:T(1,128)} %codes.3, bf16[4,6,16,128]{3,2,1,0:T(8,128)(2,1)} %bitcast.25, bf16[160,6,16,128]{3,2,1,0:T(8,128)(2,1)} %bitcast.22), custom_call_target="tpu_custom_call" | custom-call | flops 10000000 | bytes 8000000 | tf_op jit(solution)/shard_map/upper/pallas_call | solution.py:390
  5.1 5.1 %collective-permute-start = (bf16[8,256,128]{2,1,0:T(8,128)(2,1)}, bf16[8,256,128]{2,1,0:T(8,128)(2,1)S(1)}, u32[]{:S(2)}, u32[]{:S(2)}) collective-permute-start(bf16[8,256,128]{2,1,0:T(8,128)(2,1)} %upper.1), channel_id=1, source_target_pairs={{1,0},{2,1},{3,2},{4,3},{5,4},{6,5},{7,6},{8,7},{9,8},{10,9},{11,1... | collective-permute-start | bytes 1572872 | tf_op jit(solution)/shard_map/ppermute | solution.py:401
  10.3 0.0 copy-done.3
  10.3 0.0 copy-done.2
  10.3 0.0 copy-start
  10.3 2.1 %copy-done = bf16[1,160,6,2,1024]{4,3,2,1,0:T(2,128)(2,1)S(1)} copy-done((bf16[1,160,6,2,1024]{4,3,2,1,0:T(2,128)(2,1)S(1)}, bf16[1,160,6,2,1024]{4,3,2,1,0:T(2,128)(2,1)}, u32[]{:S(2)}) %copy-start) | copy-done | bytes 3932184
  12.4 5.6 %side.1 = (bf16[8,256,128]{2,1,0:T(8,128)(2,1)S(1)}, f32[8,256,128]{2,1,0:T(8,128)S(1)}) custom-call(s32[1,256]{1,0:T(1,128)S(1)} %copy-done.3, bf16[4,6,16,128]{3,2,1,0:T(8,128)(2,1)S(1)} %bitcast.26, bf16[160,6,16,128]{3,2,1,0:T(8,128)(2,1)S(1)} %bitcast.23), custom_call_target="tpu_custom_call" | custom-call | flops 20000000 | bytes 30000000 | tf_op jit(solution)/shard_map/side/pallas_call | solution.py:402
  18.0 0.0 copy-done.1
  18.0 0.5 low_sums.1
  18.5 5.5 %collective-permute-done.above = bf16[8,256,128]{2,1,0:T(8,128)(2,1)S(1)} collective-permute-done((bf16[8,256,128]{2,1,0:T(8,128)(2,1)}, bf16[8,256,128]{2,1,0:T(8,128)(2,1)S(1)}, u32[]{:S(2)}, u32[]{:S(2)}) %collective-permute-start) | collective-permute-done | bytes 524320 | tf_op jit(solution)/shard_map/ppermute | solution.py:401
  24.0 0.7 high_sums.1
  24.8 1.3 %collective-permute-start.1 = (f32[136,128]{1,0:T(8,128)S(1)}, f32[136,128]{1,0:T(8,128)S(1)}, u32[]{:S(2)}, u32[]{:S(2)}) collective-permute-start(f32[136,128]{1,0:T(8,128)S(1)} %get-tuple-element.19), channel_id=1, source_target_pairs={{0,8},{1,9},{2,10},{3,11},{4,12},{5,13},{6,14},{7,15},{8,0},{9,1},... | collective-permute-start | bytes 208904 | tf_op jit(solution)/shard_map/ppermute | solution.py:371
  26.1 3.1 %collective-permute-start.2 = (f32[136,128]{1,0:T(8,128)S(1)}, f32[136,128]{1,0:T(8,128)S(1)}, u32[]{:S(2)}, u32[]{:S(2)}) collective-permute-start(f32[136,128]{1,0:T(8,128)S(1)} %get-tuple-element.18), channel_id=1, source_target_pairs={{0,1},{1,0},{2,3},{3,2},{4,5},{5,4},{6,7},{7,6},{8,9},{9,8},{10,11... | collective-permute-start | bytes 208904 | tf_op jit(solution)/shard_map/ppermute | solution.py:371
  29.2 0.0 collective-permute-start.3
  29.2 0.0 collective-permute-done.1
  29.2 0.9 %collective-permute-done.2 = f32[136,128]{1,0:T(8,128)S(1)} collective-permute-done((f32[136,128]{1,0:T(8,128)S(1)}, f32[136,128]{1,0:T(8,128)S(1)}, u32[]{:S(2)}, u32[]{:S(2)}) %collective-permute-start.2) | collective-permute-done | bytes 69664 | tf_op jit(solution)/shard_map/ppermute | solution.py:371
  30.1 2.9 %collective-permute-done.3 = f32[136,128]{1,0:T(8,128)S(1)} collective-permute-done((f32[136,128]{1,0:T(8,128)S(1)}, f32[136,128]{1,0:T(8,128)S(1)}, u32[]{:S(2)}, u32[]{:S(2)}) %collective-permute-start.3) | collective-permute-done | bytes 69664 | tf_op jit(solution)/shard_map/ppermute | solution.py:371
  33.0 2.6 %collective-permute-start.4 = (f32[136,128]{1,0:T(8,128)S(1)}, f32[136,128]{1,0:T(8,128)S(1)}, u32[]{:S(2)}, u32[]{:S(2)}) collective-permute-start(f32[136,128]{1,0:T(8,128)S(1)} %fusion), channel_id=1, source_target_pairs={{0,24},{1,25},{2,26},{3,27},{4,28},{5,29},{6,30},{7,31},{8,16},{9,... | collective-permute-start | bytes 208904 | tf_op jit(solution)/shard_map/ppermute | solution.py:373
  35.6 2.4 %collective-permute-done.4 = f32[136,128]{1,0:T(8,128)S(1)} collective-permute-done((f32[136,128]{1,0:T(8,128)S(1)}, f32[136,128]{1,0:T(8,128)S(1)}, u32[]{:S(2)}, u32[]{:S(2)}) %collective-permute-start.4) | collective-permute-done | bytes 69664 | tf_op jit(solution)/shard_map/ppermute | solution.py:373
  38.0 1.2 %collective-permute-start.5 = (f32[136,128]{1,0:T(8,128)S(1)}, f32[136,128]{1,0:T(8,128)S(1)}, u32[]{:S(2)}, u32[]{:S(2)}) collective-permute-start(f32[136,128]{1,0:T(8,128)S(1)} %add.48), channel_id=1, source_target_pairs={{0,2},{1,3},{2,0},{3,1},{4,6},{5,7},{6,4},{7,5},{8,10},{9,11},{10,... | collective-permute-start | bytes 208904 | tf_op jit(solution)/shard_map/ppermute | solution.py:374
  39.3 4.1 %collective-permute-done.5 = f32[136,128]{1,0:T(8,128)S(1)} collective-permute-done((f32[136,128]{1,0:T(8,128)S(1)}, f32[136,128]{1,0:T(8,128)S(1)}, u32[]{:S(2)}, u32[]{:S(2)}) %collective-permute-start.5) | collective-permute-done | bytes 69664 | tf_op jit(solution)/shard_map/ppermute | solution.py:374
  43.4 3.1 %collective-permute-start.6 = (f32[136,128]{1,0:T(8,128)S(1)}, f32[136,128]{1,0:T(8,128)S(1)}, u32[]{:S(2)}, u32[]{:S(2)}) collective-permute-start(f32[136,128]{1,0:T(8,128)S(1)} %add.49), channel_id=1, source_target_pairs={{0,6},{1,7},{2,4},{3,5},{4,2},{5,3},{6,0},{7,1},{8,14},{9,15},{10,... | collective-permute-start | bytes 208904 | tf_op jit(solution)/shard_map/ppermute | solution.py:375
  46.5 2.3 %collective-permute-done.6 = f32[136,128]{1,0:T(8,128)S(1)} collective-permute-done((f32[136,128]{1,0:T(8,128)S(1)}, f32[136,128]{1,0:T(8,128)S(1)}, u32[]{:S(2)}, u32[]{:S(2)}) %collective-permute-start.6) | collective-permute-done | bytes 69664 | tf_op jit(solution)/shard_map/ppermute | solution.py:375
  48.8 0.1 collective-permute-start.7
  48.9 4.5 %collective-permute-start.9 = (f32[136,128]{1,0:T(8,128)S(1)}, f32[136,128]{1,0:T(8,128)S(1)}, u32[]{:S(2)}, u32[]{:S(2)}) collective-permute-start(f32[136,128]{1,0:T(8,128)S(1)} %add.50), channel_id=1, source_target_pairs={{0,9},{1,8},{2,11},{3,10},{4,13},{5,12},{6,15},{7,14},{8,1},{9,0},... | collective-permute-start | bytes 208904 | tf_op jit(solution)/shard_map/ppermute | solution.py:376
  53.4 0.0 collective-permute-start.8
  53.4 0.0 collective-permute-done.7
  53.4 3.0 %collective-permute-done.9 = f32[136,128]{1,0:T(8,128)S(1)} collective-permute-done((f32[136,128]{1,0:T(8,128)S(1)}, f32[136,128]{1,0:T(8,128)S(1)}, u32[]{:S(2)}, u32[]{:S(2)}) %collective-permute-start.9) | collective-permute-done | bytes 69664 | tf_op jit(solution)/shard_map/ppermute | solution.py:376
  56.4 0.0 collective-permute-done.8
  56.5 13.6 %basis.1 = bf16[128,2048]{1,0:T(8,128)(2,1)S(1)} custom-call(f32[544,128]{1,0:T(8,128)S(1)} %maximum_select_fusion.table, bf16[8,256,128]{2,1,0:T(8,128)(2,1)S(1)} %get-tuple-element.12.sens.sens_low, bf16[8,256,128]{2,1,0:T(8,128)(2,1)S(1)} %get-tuple-element.16.sens_high), custom_call_target="tpu_custom_call" | custom-call | flops 400000000 | bytes 60000000 | tf_op jit(solution)/shard_map/basis/pallas_call | solution.py:431
  70.1 13.8 %all_to_all.5 = bf16[8,16,2048]{2,1,0:T(8,128)(2,1)S(1)} all-to-all(bf16[8,16,2048]{2,1,0:T(8,128)(2,1)S(1)} %bitcast.24), channel_id=1, replica_groups=mesh['freq'=8,'brick'=32] {'freq'}, dimensions={0} | all-to-all | bytes 1048576 | tf_op jit(solution)/shard_map/all_to_all | solution.py:445
  83.9 0.1 convert_reduce_fusion
  84.0 0.8 reshape.27
  (8 shorter events, 0.1 us)
Async XLA Ops:
  0.0 10.3 %copy-start.3 = (s32[1,256]{1,0:T(1,128)S(1)}, s32[1,256]{1,0:T(1,128)}, u32[]{:S(2)}) copy-start(s32[1,256]{1,0:T(1,128)} %codes.3) | copy-start | bytes 3076
  0.0 10.3 %copy-start.2 = (bf16[1,4,6,2,1024]{4,3,2,1,0:T(2,128)(2,1)S(1)}, bf16[1,4,6,2,1024]{4,3,2,1,0:T(2,128)(2,1)}, u32[]{:S(2)}) copy-start(bf16[1,4,6,2,1024]{4,3,2,1,0:T(2,128)(2,1)} %param.4) | copy-start | bytes 294916
  0.0 18.0 %copy-start.1 = (bf16[2,1024,128]{2,1,0:T(8,128)(2,1)S(1)}, bf16[2,1024,128]{2,1,0:T(8,128)(2,1)}, u32[]{:S(2)}) copy-start(bf16[2,1024,128]{2,1,0:T(8,128)(2,1)} %probes.3) | copy-start | bytes 1572868
  5.1 19.0 %collective-permute-start = (bf16[8,256,128]{2,1,0:T(8,128)(2,1)}, bf16[8,256,128]{2,1,0:T(8,128)(2,1)S(1)}, u32[]{:S(2)}, u32[]{:S(2)}) collective-permute-start(bf16[8,256,128]{2,1,0:T(8,128)(2,1)} %upper.1), channel_id=1, source_target_pairs={{1,0},{2,1},{3,2},{4,3},{5,4},{6,5},{7,6},{8,7},{9,8},{10,9},{11,1... | collective-permute-start | bytes 1572872 | tf_op jit(solution)/shard_map/ppermute | solution.py:401
  10.3 2.1 %copy-start = (bf16[1,160,6,2,1024]{4,3,2,1,0:T(2,128)(2,1)S(1)}, bf16[1,160,6,2,1024]{4,3,2,1,0:T(2,128)(2,1)}, u32[]{:S(2)}) copy-start(bf16[1,160,6,2,1024]{4,3,2,1,0:T(2,128)(2,1)} %param.5) | copy-start | bytes 11796484
  24.8 4.4 %collective-permute-start.1 = (f32[136,128]{1,0:T(8,128)S(1)}, f32[136,128]{1,0:T(8,128)S(1)}, u32[]{:S(2)}, u32[]{:S(2)}) collective-permute-start(f32[136,128]{1,0:T(8,128)S(1)} %get-tuple-element.19), channel_id=1, source_target_pairs={{0,8},{1,9},{2,10},{3,11},{4,12},{5,13},{6,14},{7,15},{8,0},{9,1},... | collective-permute-start | bytes 208904 | tf_op jit(solution)/shard_map/ppermute | solution.py:371
  26.1 4.0 %collective-permute-start.2 = (f32[136,128]{1,0:T(8,128)S(1)}, f32[136,128]{1,0:T(8,128)S(1)}, u32[]{:S(2)}, u32[]{:S(2)}) collective-permute-start(f32[136,128]{1,0:T(8,128)S(1)} %get-tuple-element.18), channel_id=1, source_target_pairs={{0,1},{1,0},{2,3},{3,2},{4,5},{5,4},{6,7},{7,6},{8,9},{9,8},{10,11... | collective-permute-start | bytes 208904 | tf_op jit(solution)/shard_map/ppermute | solution.py:371
  29.2 3.8 %collective-permute-start.3 = (f32[136,128]{1,0:T(8,128)S(1)}, f32[136,128]{1,0:T(8,128)S(1)}, u32[]{:S(2)}, u32[]{:S(2)}) collective-permute-start(f32[136,128]{1,0:T(8,128)S(1)} %get-tuple-element.17), channel_id=1, source_target_pairs={{0,9},{1,8},{2,11},{3,10},{4,13},{5,12},{6,15},{7,14},{8,1},{9,0},... | collective-permute-start | bytes 208904 | tf_op jit(solution)/shard_map/ppermute | solution.py:371
  33.0 5.1 %collective-permute-start.4 = (f32[136,128]{1,0:T(8,128)S(1)}, f32[136,128]{1,0:T(8,128)S(1)}, u32[]{:S(2)}, u32[]{:S(2)}) collective-permute-start(f32[136,128]{1,0:T(8,128)S(1)} %fusion), channel_id=1, source_target_pairs={{0,24},{1,25},{2,26},{3,27},{4,28},{5,29},{6,30},{7,31},{8,16},{9,... | collective-permute-start | bytes 208904 | tf_op jit(solution)/shard_map/ppermute | solution.py:373
  38.0 5.4 %collective-permute-start.5 = (f32[136,128]{1,0:T(8,128)S(1)}, f32[136,128]{1,0:T(8,128)S(1)}, u32[]{:S(2)}, u32[]{:S(2)}) collective-permute-start(f32[136,128]{1,0:T(8,128)S(1)} %add.48), channel_id=1, source_target_pairs={{0,2},{1,3},{2,0},{3,1},{4,6},{5,7},{6,4},{7,5},{8,10},{9,11},{10,... | collective-permute-start | bytes 208904 | tf_op jit(solution)/shard_map/ppermute | solution.py:374
  43.4 5.4 %collective-permute-start.6 = (f32[136,128]{1,0:T(8,128)S(1)}, f32[136,128]{1,0:T(8,128)S(1)}, u32[]{:S(2)}, u32[]{:S(2)}) collective-permute-start(f32[136,128]{1,0:T(8,128)S(1)} %add.49), channel_id=1, source_target_pairs={{0,6},{1,7},{2,4},{3,5},{4,2},{5,3},{6,0},{7,1},{8,14},{9,15},{10,... | collective-permute-start | bytes 208904 | tf_op jit(solution)/shard_map/ppermute | solution.py:375
  48.8 4.6 %collective-permute-start.7 = (f32[136,128]{1,0:T(8,128)S(1)}, f32[136,128]{1,0:T(8,128)S(1)}, u32[]{:S(2)}, u32[]{:S(2)}) collective-permute-start(f32[136,128]{1,0:T(8,128)S(1)} %add.50), channel_id=1, source_target_pairs={{0,8},{1,9},{2,10},{3,11},{4,12},{5,13},{6,14},{7,15},{8,0},{9,1},... | collective-permute-start | bytes 208904 | tf_op jit(solution)/shard_map/ppermute | solution.py:376
  48.9 7.5 %collective-permute-start.9 = (f32[136,128]{1,0:T(8,128)S(1)}, f32[136,128]{1,0:T(8,128)S(1)}, u32[]{:S(2)}, u32[]{:S(2)}) collective-permute-start(f32[136,128]{1,0:T(8,128)S(1)} %add.50), channel_id=1, source_target_pairs={{0,9},{1,8},{2,11},{3,10},{4,13},{5,12},{6,15},{7,14},{8,1},{9,0},... | collective-permute-start | bytes 208904 | tf_op jit(solution)/shard_map/ppermute | solution.py:376
  53.4 3.0 %collective-permute-start.8 = (f32[136,128]{1,0:T(8,128)S(1)}, f32[136,128]{1,0:T(8,128)S(1)}, u32[]{:S(2)}, u32[]{:S(2)}) collective-permute-start(f32[136,128]{1,0:T(8,128)S(1)} %add.50), channel_id=1, source_target_pairs={{0,1},{1,0},{2,3},{3,2},{4,5},{5,4},{6,7},{7,6},{8,9},{9,8},{10,11... | collective-permute-start | bytes 208904 | tf_op jit(solution)/shard_map/ppermute | solution.py:376

commit v5 on v4

--- a/solution.py
+++ b/solution.py
@@ -122,7 +122,7 @@
         low_upper[tile_rows(d, SUB), :] = edge_x + next_row(edge_x) + (edge_y + next_column(edge_y))
         return carry
 
-    lax.fori_loop(0, PANEL, one, 0, unroll=64)
+    lax.fori_loop(0, PANEL, one, 0, unroll=128)
 
     def block(i, carry):
         for s in range(SUB):
@@ -317,9 +317,10 @@
                 sketch[stage + 1, halves[half], :] = done[:, PANEL:]
     final = basis[ITERS].astype(jnp.bfloat16)
     for layer, sens in enumerate((sens_low, sens_high)):
-        for s in range(SUB):
+        for s in range(0, SUB, 2):
             at = 1024 * layer + 128 * s
-            parts[:, at : at + 128] = dot(final, sens[s], 1, 0).astype(jnp.bfloat16)
+            pair = jnp.concatenate([sens[s], sens[s + 1]], axis=1)
+            parts[:, at : at + 256] = dot(final, pair, 1, 0).astype(jnp.bfloat16)
 
 
 def brick_moves(step):

time: 85.1 us -> 84.8 us (level)
  no operation moved by 1% of the time
where the time goes in v5:
time: 84.8 us; the launch traced here: 84.6 us
  Pallas kernels  25.1 us (30%)
  waiting for transfers between devices  21.2 us (25%)
  starting transfers between devices  21.1 us (25%)
  blocking collectives  13.9 us (16%)
  local copies, waits for them, and re-layouts  2.91 us (3%)
    all_to_all x1, blocking collectives, local(): parts = lax.all_to_all(parts.reshape(8, 16, 2048), 'freq', 0, 0)  13.9 us
    pallas_call x1, Pallas kernels, local(): pl.pallas_call(basis_kernel, in_specs=[WHOLE] * 3, out_specs=WHOLE, out_s...  13.4 us
    pallas_call x1, Pallas kernels, local(): pl.pallas_call(side_kernel, in_specs=[WHOLE, anywhere, anywhere], out_spe...  5.59 us
    ppermute x1, waiting for transfers between devices, local(): lax.ppermute(lowest, 'brick', [(i + 1, i) for i in devices if i + 1 in de...  5.55 us
    ppermute x1, starting transfers between devices, local(): lax.ppermute(lowest, 'brick', [(i + 1, i) for i in devices if i + 1 in de...  5.15 us
    pallas_call x1, Pallas kernels, local(): pl.pallas_call(upper_kernel, in_specs=[WHOLE, anywhere, anywhere], out_sp...  4.88 us
    ppermute x3, starting transfers between devices, brick_sum(): got = [lax.ppermute(part, 'brick', move) for move in moves]  4.65 us
    ppermute x3, starting transfers between devices, brick_sum(): lax.ppermute(pick(quarters, place ^ k + 1), 'brick', moves[k])  4.38 us
  transfers between devices with their start and end apart: 10, of which 7 were waited for; matrix products, arithmetic and copies ran while one was open for 0% of the time, Pallas kernels for 7%

profile of v5, /device:TPU:1, one launch (start us, length us, event | category | flops | bytes accessed | tf_op | source)
XLA Modules:
  0.0 84.6 jit_solution(13298228582348387191)
XLA Ops:
  0.0 0.0 copy-start.3
  0.0 0.0 copy-start.2
  0.0 0.0 copy-start.1
  0.0 4.9 %upper.1 = bf16[8,256,128]{2,1,0:T(8,128)(2,1)} custom-call(s32[1,256]{1,0:T(1,128)} %codes.3, bf16[4,6,16,128]{3,2,1,0:T(8,128)(2,1)} %bitcast.25, bf16[160,6,16,128]{3,2,1,0:T(8,128)(2,1)} %bitcast.22), custom_call_target="tpu_custom_call" | custom-call | flops 10000000 | bytes 8000000 | tf_op jit(solution)/shard_map/upper/pallas_call | solution.py:391
  4.9 5.1 %collective-permute-start = (bf16[8,256,128]{2,1,0:T(8,128)(2,1)}, bf16[8,256,128]{2,1,0:T(8,128)(2,1)S(1)}, u32[]{:S(2)}, u32[]{:S(2)}) collective-permute-start(bf16[8,256,128]{2,1,0:T(8,128)(2,1)} %upper.1), channel_id=1, source_target_pairs={{1,0},{2,1},{3,2},{4,3},{5,4},{6,5},{7,6},{8,7},{9,8},{10,9},{11,1... | collective-permute-start | bytes 1572872 | tf_op jit(solution)/shard_map/ppermute | solution.py:402
  10.1 0.0 copy-done.3
  10.1 0.0 copy-done.2
  10.1 0.0 copy-start
  10.1 2.1 %copy-done = bf16[1,160,6,2,1024]{4,3,2,1,0:T(2,128)(2,1)S(1)} copy-done((bf16[1,160,6,2,1024]{4,3,2,1,0:T(2,128)(2,1)S(1)}, bf16[1,160,6,2,1024]{4,3,2,1,0:T(2,128)(2,1)}, u32[]{:S(2)}) %copy-start) | copy-done | bytes 3932184
  12.2 5.6 %side.1 = (bf16[8,256,128]{2,1,0:T(8,128)(2,1)S(1)}, f32[8,256,128]{2,1,0:T(8,128)S(1)}) custom-call(s32[1,256]{1,0:T(1,128)S(1)} %copy-done.3, bf16[4,6,16,128]{3,2,1,0:T(8,128)(2,1)S(1)} %bitcast.26, bf16[160,6,16,128]{3,2,1,0:T(8,128)(2,1)S(1)} %bitcast.23), custom_call_target="tpu_custom_call" | custom-call | flops 20000000 | bytes 30000000 | tf_op jit(solution)/shard_map/side/pallas_call | solution.py:403
  17.8 0.0 copy-done.1
  17.9 0.5 low_sums.1
  18.3 5.5 %collective-permute-done.above = bf16[8,256,128]{2,1,0:T(8,128)(2,1)S(1)} collective-permute-done((bf16[8,256,128]{2,1,0:T(8,128)(2,1)}, bf16[8,256,128]{2,1,0:T(8,128)(2,1)S(1)}, u32[]{:S(2)}, u32[]{:S(2)}) %collective-permute-start) | collective-permute-done | bytes 524320 | tf_op jit(solution)/shard_map/ppermute | solution.py:402
  23.9 0.7 high_sums.1
  24.6 1.3 %collective-permute-start.1 = (f32[136,128]{1,0:T(8,128)S(1)}, f32[136,128]{1,0:T(8,128)S(1)}, u32[]{:S(2)}, u32[]{:S(2)}) collective-permute-start(f32[136,128]{1,0:T(8,128)S(1)} %get-tuple-element.19), channel_id=1, source_target_pairs={{0,8},{1,9},{2,10},{3,11},{4,12},{5,13},{6,14},{7,15},{8,0},{9,1},... | collective-permute-start | bytes 208904 | tf_op jit(solution)/shard_map/ppermute | solution.py:372
  25.9 3.1 %collective-permute-start.2 = (f32[136,128]{1,0:T(8,128)S(1)}, f32[136,128]{1,0:T(8,128)S(1)}, u32[]{:S(2)}, u32[]{:S(2)}) collective-permute-start(f32[136,128]{1,0:T(8,128)S(1)} %get-tuple-element.18), channel_id=1, source_target_pairs={{0,1},{1,0},{2,3},{3,2},{4,5},{5,4},{6,7},{7,6},{8,9},{9,8},{10,11... | collective-permute-start | bytes 208904 | tf_op jit(solution)/shard_map/ppermute | solution.py:372
  29.0 0.0 collective-permute-start.3
  29.0 0.0 collective-permute-done.1
  29.0 0.9 %collective-permute-done.2 = f32[136,128]{1,0:T(8,128)S(1)} collective-permute-done((f32[136,128]{1,0:T(8,128)S(1)}, f32[136,128]{1,0:T(8,128)S(1)}, u32[]{:S(2)}, u32[]{:S(2)}) %collective-permute-start.2) | collective-permute-done | bytes 69664 | tf_op jit(solution)/shard_map/ppermute | solution.py:372
  29.9 2.9 %collective-permute-done.3 = f32[136,128]{1,0:T(8,128)S(1)} collective-permute-done((f32[136,128]{1,0:T(8,128)S(1)}, f32[136,128]{1,0:T(8,128)S(1)}, u32[]{:S(2)}, u32[]{:S(2)}) %collective-permute-start.3) | collective-permute-done | bytes 69664 | tf_op jit(solution)/shard_map/ppermute | solution.py:372
  32.8 2.6 %collective-permute-start.4 = (f32[136,128]{1,0:T(8,128)S(1)}, f32[136,128]{1,0:T(8,128)S(1)}, u32[]{:S(2)}, u32[]{:S(2)}) collective-permute-start(f32[136,128]{1,0:T(8,128)S(1)} %fusion), channel_id=1, source_target_pairs={{0,24},{1,25},{2,26},{3,27},{4,28},{5,29},{6,30},{7,31},{8,16},{9,... | collective-permute-start | bytes 208904 | tf_op jit(solution)/shard_map/ppermute | solution.py:374
  35.5 2.4 %collective-permute-done.4 = f32[136,128]{1,0:T(8,128)S(1)} collective-permute-done((f32[136,128]{1,0:T(8,128)S(1)}, f32[136,128]{1,0:T(8,128)S(1)}, u32[]{:S(2)}, u32[]{:S(2)}) %collective-permute-start.4) | collective-permute-done | bytes 69664 | tf_op jit(solution)/shard_map/ppermute | solution.py:374
  37.9 1.2 %collective-permute-start.5 = (f32[136,128]{1,0:T(8,128)S(1)}, f32[136,128]{1,0:T(8,128)S(1)}, u32[]{:S(2)}, u32[]{:S(2)}) collective-permute-start(f32[136,128]{1,0:T(8,128)S(1)} %add.48), channel_id=1, source_target_pairs={{0,2},{1,3},{2,0},{3,1},{4,6},{5,7},{6,4},{7,5},{8,10},{9,11},{10,... | collective-permute-start | bytes 208904 | tf_op jit(solution)/shard_map/ppermute | solution.py:375
  39.1 4.1 %collective-permute-done.5 = f32[136,128]{1,0:T(8,128)S(1)} collective-permute-done((f32[136,128]{1,0:T(8,128)S(1)}, f32[136,128]{1,0:T(8,128)S(1)}, u32[]{:S(2)}, u32[]{:S(2)}) %collective-permute-start.5) | collective-permute-done | bytes 69664 | tf_op jit(solution)/shard_map/ppermute | solution.py:375
  43.3 3.1 %collective-permute-start.6 = (f32[136,128]{1,0:T(8,128)S(1)}, f32[136,128]{1,0:T(8,128)S(1)}, u32[]{:S(2)}, u32[]{:S(2)}) collective-permute-start(f32[136,128]{1,0:T(8,128)S(1)} %add.49), channel_id=1, source_target_pairs={{0,6},{1,7},{2,4},{3,5},{4,2},{5,3},{6,0},{7,1},{8,14},{9,15},{10,... | collective-permute-start | bytes 208904 | tf_op jit(solution)/shard_map/ppermute | solution.py:376
  46.3 2.3 %collective-permute-done.6 = f32[136,128]{1,0:T(8,128)S(1)} collective-permute-done((f32[136,128]{1,0:T(8,128)S(1)}, f32[136,128]{1,0:T(8,128)S(1)}, u32[]{:S(2)}, u32[]{:S(2)}) %collective-permute-start.6) | collective-permute-done | bytes 69664 | tf_op jit(solution)/shard_map/ppermute | solution.py:376
  48.6 0.2 collective-permute-start.7
  48.8 4.5 %collective-permute-start.9 = (f32[136,128]{1,0:T(8,128)S(1)}, f32[136,128]{1,0:T(8,128)S(1)}, u32[]{:S(2)}, u32[]{:S(2)}) collective-permute-start(f32[136,128]{1,0:T(8,128)S(1)} %add.50), channel_id=1, source_target_pairs={{0,9},{1,8},{2,11},{3,10},{4,13},{5,12},{6,15},{7,14},{8,1},{9,0},... | collective-permute-start | bytes 208904 | tf_op jit(solution)/shard_map/ppermute | solution.py:377
  53.3 0.0 collective-permute-start.8
  53.3 0.0 collective-permute-done.7
  53.3 3.0 %collective-permute-done.9 = f32[136,128]{1,0:T(8,128)S(1)} collective-permute-done((f32[136,128]{1,0:T(8,128)S(1)}, f32[136,128]{1,0:T(8,128)S(1)}, u32[]{:S(2)}, u32[]{:S(2)}) %collective-permute-start.9) | collective-permute-done | bytes 69664 | tf_op jit(solution)/shard_map/ppermute | solution.py:377
  56.3 0.0 collective-permute-done.8
  56.3 13.4 %basis.1 = bf16[128,2048]{1,0:T(8,128)(2,1)S(1)} custom-call(f32[544,128]{1,0:T(8,128)S(1)} %maximum_select_fusion.table, bf16[8,256,128]{2,1,0:T(8,128)(2,1)S(1)} %get-tuple-element.12.sens.sens_low, bf16[8,256,128]{2,1,0:T(8,128)(2,1)S(1)} %get-tuple-element.16.sens_high), custom_call_target="tpu_custom_call" | custom-call | flops 400000000 | bytes 60000000 | tf_op jit(solution)/shard_map/basis/pallas_call | solution.py:432
  69.8 13.9 %all_to_all.5 = bf16[8,16,2048]{2,1,0:T(8,128)(2,1)S(1)} all-to-all(bf16[8,16,2048]{2,1,0:T(8,128)(2,1)S(1)} %bitcast.24), channel_id=1, replica_groups=mesh['freq'=8,'brick'=32] {'freq'}, dimensions={0} | all-to-all | bytes 1048576 | tf_op jit(solution)/shard_map/all_to_all | solution.py:446
  83.7 0.1 convert_reduce_fusion
  83.8 0.8 reshape.27
  (8 shorter events, 0.1 us)
Async XLA Ops:
  0.0 10.1 %copy-start.3 = (s32[1,256]{1,0:T(1,128)S(1)}, s32[1,256]{1,0:T(1,128)}, u32[]{:S(2)}) copy-start(s32[1,256]{1,0:T(1,128)} %codes.3) | copy-start | bytes 3076
  0.0 10.1 %copy-start.2 = (bf16[1,4,6,2,1024]{4,3,2,1,0:T(2,128)(2,1)S(1)}, bf16[1,4,6,2,1024]{4,3,2,1,0:T(2,128)(2,1)}, u32[]{:S(2)}) copy-start(bf16[1,4,6,2,1024]{4,3,2,1,0:T(2,128)(2,1)} %param.4) | copy-start | bytes 294916
  0.0 17.8 %copy-start.1 = (bf16[2,1024,128]{2,1,0:T(8,128)(2,1)S(1)}, bf16[2,1024,128]{2,1,0:T(8,128)(2,1)}, u32[]{:S(2)}) copy-start(bf16[2,1024,128]{2,1,0:T(8,128)(2,1)} %probes.3) | copy-start | bytes 1572868
  4.9 19.0 %collective-permute-start = (bf16[8,256,128]{2,1,0:T(8,128)(2,1)}, bf16[8,256,128]{2,1,0:T(8,128)(2,1)S(1)}, u32[]{:S(2)}, u32[]{:S(2)}) collective-permute-start(bf16[8,256,128]{2,1,0:T(8,128)(2,1)} %upper.1), channel_id=1, source_target_pairs={{1,0},{2,1},{3,2},{4,3},{5,4},{6,5},{7,6},{8,7},{9,8},{10,9},{11,1... | collective-permute-start | bytes 1572872 | tf_op jit(solution)/shard_map/ppermute | solution.py:402
  10.1 2.1 %copy-start = (bf16[1,160,6,2,1024]{4,3,2,1,0:T(2,128)(2,1)S(1)}, bf16[1,160,6,2,1024]{4,3,2,1,0:T(2,128)(2,1)}, u32[]{:S(2)}) copy-start(bf16[1,160,6,2,1024]{4,3,2,1,0:T(2,128)(2,1)} %param.5) | copy-start | bytes 11796484
  24.6 4.4 %collective-permute-start.1 = (f32[136,128]{1,0:T(8,128)S(1)}, f32[136,128]{1,0:T(8,128)S(1)}, u32[]{:S(2)}, u32[]{:S(2)}) collective-permute-start(f32[136,128]{1,0:T(8,128)S(1)} %get-tuple-element.19), channel_id=1, source_target_pairs={{0,8},{1,9},{2,10},{3,11},{4,12},{5,13},{6,14},{7,15},{8,0},{9,1},... | collective-permute-start | bytes 208904 | tf_op jit(solution)/shard_map/ppermute | solution.py:372
  25.9 4.0 %collective-permute-start.2 = (f32[136,128]{1,0:T(8,128)S(1)}, f32[136,128]{1,0:T(8,128)S(1)}, u32[]{:S(2)}, u32[]{:S(2)}) collective-permute-start(f32[136,128]{1,0:T(8,128)S(1)} %get-tuple-element.18), channel_id=1, source_target_pairs={{0,1},{1,0},{2,3},{3,2},{4,5},{5,4},{6,7},{7,6},{8,9},{9,8},{10,11... | collective-permute-start | bytes 208904 | tf_op jit(solution)/shard_map/ppermute | solution.py:372
  29.0 3.8 %collective-permute-start.3 = (f32[136,128]{1,0:T(8,128)S(1)}, f32[136,128]{1,0:T(8,128)S(1)}, u32[]{:S(2)}, u32[]{:S(2)}) collective-permute-start(f32[136,128]{1,0:T(8,128)S(1)} %get-tuple-element.17), channel_id=1, source_target_pairs={{0,9},{1,8},{2,11},{3,10},{4,13},{5,12},{6,15},{7,14},{8,1},{9,0},... | collective-permute-start | bytes 208904 | tf_op jit(solution)/shard_map/ppermute | solution.py:372
  32.8 5.1 %collective-permute-start.4 = (f32[136,128]{1,0:T(8,128)S(1)}, f32[136,128]{1,0:T(8,128)S(1)}, u32[]{:S(2)}, u32[]{:S(2)}) collective-permute-start(f32[136,128]{1,0:T(8,128)S(1)} %fusion), channel_id=1, source_target_pairs={{0,24},{1,25},{2,26},{3,27},{4,28},{5,29},{6,30},{7,31},{8,16},{9,... | collective-permute-start | bytes 208904 | tf_op jit(solution)/shard_map/ppermute | solution.py:374
  37.9 5.4 %collective-permute-start.5 = (f32[136,128]{1,0:T(8,128)S(1)}, f32[136,128]{1,0:T(8,128)S(1)}, u32[]{:S(2)}, u32[]{:S(2)}) collective-permute-start(f32[136,128]{1,0:T(8,128)S(1)} %add.48), channel_id=1, source_target_pairs={{0,2},{1,3},{2,0},{3,1},{4,6},{5,7},{6,4},{7,5},{8,10},{9,11},{10,... | collective-permute-start | bytes 208904 | tf_op jit(solution)/shard_map/ppermute | solution.py:375
  43.3 5.4 %collective-permute-start.6 = (f32[136,128]{1,0:T(8,128)S(1)}, f32[136,128]{1,0:T(8,128)S(1)}, u32[]{:S(2)}, u32[]{:S(2)}) collective-permute-start(f32[136,128]{1,0:T(8,128)S(1)} %add.49), channel_id=1, source_target_pairs={{0,6},{1,7},{2,4},{3,5},{4,2},{5,3},{6,0},{7,1},{8,14},{9,15},{10,... | collective-permute-start | bytes 208904 | tf_op jit(solution)/shard_map/ppermute | solution.py:376
  48.6 4.7 %collective-permute-start.7 = (f32[136,128]{1,0:T(8,128)S(1)}, f32[136,128]{1,0:T(8,128)S(1)}, u32[]{:S(2)}, u32[]{:S(2)}) collective-permute-start(f32[136,128]{1,0:T(8,128)S(1)} %add.50), channel_id=1, source_target_pairs={{0,8},{1,9},{2,10},{3,11},{4,12},{5,13},{6,14},{7,15},{8,0},{9,1},... | collective-permute-start | bytes 208904 | tf_op jit(solution)/shard_map/ppermute | solution.py:377
  48.8 7.5 %collective-permute-start.9 = (f32[136,128]{1,0:T(8,128)S(1)}, f32[136,128]{1,0:T(8,128)S(1)}, u32[]{:S(2)}, u32[]{:S(2)}) collective-permute-start(f32[136,128]{1,0:T(8,128)S(1)} %add.50), channel_id=1, source_target_pairs={{0,9},{1,8},{2,11},{3,10},{4,13},{5,12},{6,15},{7,14},{8,1},{9,0},... | collective-permute-start | bytes 208904 | tf_op jit(solution)/shard_map/ppermute | solution.py:377
  53.3 3.0 %collective-permute-start.8 = (f32[136,128]{1,0:T(8,128)S(1)}, f32[136,128]{1,0:T(8,128)S(1)}, u32[]{:S(2)}, u32[]{:S(2)}) collective-permute-start(f32[136,128]{1,0:T(8,128)S(1)} %add.50), channel_id=1, source_target_pairs={{0,1},{1,0},{2,3},{3,2},{4,5},{5,4},{6,7},{7,6},{8,9},{9,8},{10,11... | collective-permute-start | bytes 208904 | tf_op jit(solution)/shard_map/ppermute | solution.py:377

commit v6 on v5

--- a/solution.py
+++ b/solution.py
@@ -196,7 +196,7 @@
             sens[here] = (0.25 * (rest[here] + above[here].astype(jnp.float32))).astype(jnp.bfloat16)
         return carry
 
-    lax.fori_loop(0, PANEL // 16, block, 0)
+    lax.fori_loop(0, PANEL // 16, block, 0, unroll=4)
     cross, sketch = layer_sums(sens, probes, 1)
     cross, sketch = cross + low_cross[...], sketch + low_sketch[...]
     table[0:128, :], table[128:256, :] = sketch[:, :128], sketch[:, 128:]

time: 84.8 us -> 84.7 us (level)
  no operation moved by 1% of the time
where the time goes in v6:
time: 84.7 us; the launch traced here: 84.5 us
  Pallas kernels  25 us (30%)
  waiting for transfers between devices  21.2 us (25%)
  starting transfers between devices  21.1 us (25%)
  blocking collectives  13.9 us (16%)
  local copies, waits for them, and re-layouts  2.91 us (3%)
    all_to_all x1, blocking collectives, local(): parts = lax.all_to_all(parts.reshape(8, 16, 2048), 'freq', 0, 0)  13.9 us
    pallas_call x1, Pallas kernels, local(): pl.pallas_call(basis_kernel, in_specs=[WHOLE] * 3, out_specs=WHOLE, out_s...  13.4 us
    pallas_call x1, Pallas kernels, local(): pl.pallas_call(side_kernel, in_specs=[WHOLE, anywhere, anywhere], out_spe...  5.59 us
    ppermute x1, waiting for transfers between devices, local(): lax.ppermute(lowest, 'brick', [(i + 1, i) for i in devices if i + 1 in de...  5.55 us
    ppermute x1, starting transfers between devices, local(): lax.ppermute(lowest, 'brick', [(i + 1, i) for i in devices if i + 1 in de...  5.15 us
    pallas_call x1, Pallas kernels, local(): pl.pallas_call(upper_kernel, in_specs=[WHOLE, anywhere, anywhere], out_sp...  4.88 us
    ppermute x3, starting transfers between devices, brick_sum(): got = [lax.ppermute(part, 'brick', move) for move in moves]  4.65 us
    ppermute x3, starting transfers between devices, brick_sum(): lax.ppermute(pick(quarters, place ^ k + 1), 'brick', moves[k])  4.38 us
  transfers between devices with their start and end apart: 10, of which 7 were waited for; matrix products, arithmetic and copies ran while one was open for 0% of the time, Pallas kernels for 7%

profile of v6, /device:TPU:1, one launch (start us, length us, event | category | flops | bytes accessed | tf_op | source)
XLA Modules:
  0.0 84.5 jit_solution(10983126847058168087)
XLA Ops:
  0.0 0.0 copy-start.3
  0.0 0.0 copy-start.2
  0.0 0.0 copy-start.1
  0.0 4.9 %upper.1 = bf16[8,256,128]{2,1,0:T(8,128)(2,1)} custom-call(s32[1,256]{1,0:T(1,128)} %codes.3, bf16[4,6,16,128]{3,2,1,0:T(8,128)(2,1)} %bitcast.25, bf16[160,6,16,128]{3,2,1,0:T(8,128)(2,1)} %bitcast.22), custom_call_target="tpu_custom_call" | custom-call | flops 10000000 | bytes 8000000 | tf_op jit(solution)/shard_map/upper/pallas_call | solution.py:391
  4.9 5.1 %collective-permute-start = (bf16[8,256,128]{2,1,0:T(8,128)(2,1)}, bf16[8,256,128]{2,1,0:T(8,128)(2,1)S(1)}, u32[]{:S(2)}, u32[]{:S(2)}) collective-permute-start(bf16[8,256,128]{2,1,0:T(8,128)(2,1)} %upper.1), channel_id=1, source_target_pairs={{1,0},{2,1},{3,2},{4,3},{5,4},{6,5},{7,6},{8,7},{9,8},{10,9},{11,1... | collective-permute-start | bytes 1572872 | tf_op jit(solution)/shard_map/ppermute | solution.py:402
  10.1 0.0 copy-done.3
  10.1 0.0 copy-done.2
  10.1 0.0 copy-start
  10.1 2.1 %copy-done = bf16[1,160,6,2,1024]{4,3,2,1,0:T(2,128)(2,1)S(1)} copy-done((bf16[1,160,6,2,1024]{4,3,2,1,0:T(2,128)(2,1)S(1)}, bf16[1,160,6,2,1024]{4,3,2,1,0:T(2,128)(2,1)}, u32[]{:S(2)}) %copy-start) | copy-done | bytes 3932184
  12.2 5.6 %side.1 = (bf16[8,256,128]{2,1,0:T(8,128)(2,1)S(1)}, f32[8,256,128]{2,1,0:T(8,128)S(1)}) custom-call(s32[1,256]{1,0:T(1,128)S(1)} %copy-done.3, bf16[4,6,16,128]{3,2,1,0:T(8,128)(2,1)S(1)} %bitcast.26, bf16[160,6,16,128]{3,2,1,0:T(8,128)(2,1)S(1)} %bitcast.23), custom_call_target="tpu_custom_call" | custom-call | flops 20000000 | bytes 30000000 | tf_op jit(solution)/shard_map/side/pallas_call | solution.py:403
  17.8 0.0 copy-done.1
  17.9 0.5 low_sums.1
  18.3 5.5 %collective-permute-done.above = bf16[8,256,128]{2,1,0:T(8,128)(2,1)S(1)} collective-permute-done((bf16[8,256,128]{2,1,0:T(8,128)(2,1)}, bf16[8,256,128]{2,1,0:T(8,128)(2,1)S(1)}, u32[]{:S(2)}, u32[]{:S(2)}) %collective-permute-start) | collective-permute-done | bytes 524320 | tf_op jit(solution)/shard_map/ppermute | solution.py:402
  23.9 0.6 high_sums.1
  24.6 1.3 %collective-permute-start.1 = (f32[136,128]{1,0:T(8,128)S(1)}, f32[136,128]{1,0:T(8,128)S(1)}, u32[]{:S(2)}, u32[]{:S(2)}) collective-permute-start(f32[136,128]{1,0:T(8,128)S(1)} %get-tuple-element.19), channel_id=1, source_target_pairs={{0,8},{1,9},{2,10},{3,11},{4,12},{5,13},{6,14},{7,15},{8,0},{9,1},... | collective-permute-start | bytes 208904 | tf_op jit(solution)/shard_map/ppermute | solution.py:372
  25.9 3.1 %collective-permute-start.2 = (f32[136,128]{1,0:T(8,128)S(1)}, f32[136,128]{1,0:T(8,128)S(1)}, u32[]{:S(2)}, u32[]{:S(2)}) collective-permute-start(f32[136,128]{1,0:T(8,128)S(1)} %get-tuple-element.18), channel_id=1, source_target_pairs={{0,1},{1,0},{2,3},{3,2},{4,5},{5,4},{6,7},{7,6},{8,9},{9,8},{10,11... | collective-permute-start | bytes 208904 | tf_op jit(solution)/shard_map/ppermute | solution.py:372
  28.9 0.0 collective-permute-start.3
  28.9 0.0 collective-permute-done.1
  28.9 0.9 %collective-permute-done.2 = f32[136,128]{1,0:T(8,128)S(1)} collective-permute-done((f32[136,128]{1,0:T(8,128)S(1)}, f32[136,128]{1,0:T(8,128)S(1)}, u32[]{:S(2)}, u32[]{:S(2)}) %collective-permute-start.2) | collective-permute-done | bytes 69664 | tf_op jit(solution)/shard_map/ppermute | solution.py:372
  29.8 2.9 %collective-permute-done.3 = f32[136,128]{1,0:T(8,128)S(1)} collective-permute-done((f32[136,128]{1,0:T(8,128)S(1)}, f32[136,128]{1,0:T(8,128)S(1)}, u32[]{:S(2)}, u32[]{:S(2)}) %collective-permute-start.3) | collective-permute-done | bytes 69664 | tf_op jit(solution)/shard_map/ppermute | solution.py:372
  32.8 2.6 %collective-permute-start.4 = (f32[136,128]{1,0:T(8,128)S(1)}, f32[136,128]{1,0:T(8,128)S(1)}, u32[]{:S(2)}, u32[]{:S(2)}) collective-permute-start(f32[136,128]{1,0:T(8,128)S(1)} %fusion), channel_id=1, source_target_pairs={{0,24},{1,25},{2,26},{3,27},{4,28},{5,29},{6,30},{7,31},{8,16},{9,... | collective-permute-start | bytes 208904 | tf_op jit(solution)/shard_map/ppermute | solution.py:374
  35.4 2.4 %collective-permute-done.4 = f32[136,128]{1,0:T(8,128)S(1)} collective-permute-done((f32[136,128]{1,0:T(8,128)S(1)}, f32[136,128]{1,0:T(8,128)S(1)}, u32[]{:S(2)}, u32[]{:S(2)}) %collective-permute-start.4) | collective-permute-done | bytes 69664 | tf_op jit(solution)/shard_map/ppermute | solution.py:374
  37.8 1.2 %collective-permute-start.5 = (f32[136,128]{1,0:T(8,128)S(1)}, f32[136,128]{1,0:T(8,128)S(1)}, u32[]{:S(2)}, u32[]{:S(2)}) collective-permute-start(f32[136,128]{1,0:T(8,128)S(1)} %add.48), channel_id=1, source_target_pairs={{0,2},{1,3},{2,0},{3,1},{4,6},{5,7},{6,4},{7,5},{8,10},{9,11},{10,... | collective-permute-start | bytes 208904 | tf_op jit(solution)/shard_map/ppermute | solution.py:375
  39.0 4.1 %collective-permute-done.5 = f32[136,128]{1,0:T(8,128)S(1)} collective-permute-done((f32[136,128]{1,0:T(8,128)S(1)}, f32[136,128]{1,0:T(8,128)S(1)}, u32[]{:S(2)}, u32[]{:S(2)}) %collective-permute-start.5) | collective-permute-done | bytes 69664 | tf_op jit(solution)/shard_map/ppermute | solution.py:375
  43.2 3.1 %collective-permute-start.6 = (f32[136,128]{1,0:T(8,128)S(1)}, f32[136,128]{1,0:T(8,128)S(1)}, u32[]{:S(2)}, u32[]{:S(2)}) collective-permute-start(f32[136,128]{1,0:T(8,128)S(1)} %add.49), channel_id=1, source_target_pairs={{0,6},{1,7},{2,4},{3,5},{4,2},{5,3},{6,0},{7,1},{8,14},{9,15},{10,... | collective-permute-start | bytes 208904 | tf_op jit(solution)/shard_map/ppermute | solution.py:376
  46.3 2.3 %collective-permute-done.6 = f32[136,128]{1,0:T(8,128)S(1)} collective-permute-done((f32[136,128]{1,0:T(8,128)S(1)}, f32[136,128]{1,0:T(8,128)S(1)}, u32[]{:S(2)}, u32[]{:S(2)}) %collective-permute-start.6) | collective-permute-done | bytes 69664 | tf_op jit(solution)/shard_map/ppermute | solution.py:376
  48.6 0.2 collective-permute-start.7
  48.7 4.5 %collective-permute-start.9 = (f32[136,128]{1,0:T(8,128)S(1)}, f32[136,128]{1,0:T(8,128)S(1)}, u32[]{:S(2)}, u32[]{:S(2)}) collective-permute-start(f32[136,128]{1,0:T(8,128)S(1)} %add.50), channel_id=1, source_target_pairs={{0,9},{1,8},{2,11},{3,10},{4,13},{5,12},{6,15},{7,14},{8,1},{9,0},... | collective-permute-start | bytes 208904 | tf_op jit(solution)/shard_map/ppermute | solution.py:377
  53.2 0.0 collective-permute-start.8
  53.2 0.0 collective-permute-done.7
  53.2 3.0 %collective-permute-done.9 = f32[136,128]{1,0:T(8,128)S(1)} collective-permute-done((f32[136,128]{1,0:T(8,128)S(1)}, f32[136,128]{1,0:T(8,128)S(1)}, u32[]{:S(2)}, u32[]{:S(2)}) %collective-permute-start.9) | collective-permute-done | bytes 69664 | tf_op jit(solution)/shard_map/ppermute | solution.py:377
  56.2 0.0 collective-permute-done.8
  56.3 13.4 %basis.1 = bf16[128,2048]{1,0:T(8,128)(2,1)S(1)} custom-call(f32[544,128]{1,0:T(8,128)S(1)} %maximum_select_fusion.table, bf16[8,256,128]{2,1,0:T(8,128)(2,1)S(1)} %get-tuple-element.12.sens.sens_low, bf16[8,256,128]{2,1,0:T(8,128)(2,1)S(1)} %get-tuple-element.16.sens_high), custom_call_target="tpu_custom_call" | custom-call | flops 400000000 | bytes 60000000 | tf_op jit(solution)/shard_map/basis/pallas_call | solution.py:432
  69.7 13.9 %all_to_all.5 = bf16[8,16,2048]{2,1,0:T(8,128)(2,1)S(1)} all-to-all(bf16[8,16,2048]{2,1,0:T(8,128)(2,1)S(1)} %bitcast.24), channel_id=1, replica_groups=mesh['freq'=8,'brick'=32] {'freq'}, dimensions={0} | all-to-all | bytes 1048576 | tf_op jit(solution)/shard_map/all_to_all | solution.py:446
  83.7 0.1 convert_reduce_fusion
  83.7 0.8 reshape.27
  (8 shorter events, 0.1 us)
Async XLA Ops:
  0.0 10.1 %copy-start.3 = (s32[1,256]{1,0:T(1,128)S(1)}, s32[1,256]{1,0:T(1,128)}, u32[]{:S(2)}) copy-start(s32[1,256]{1,0:T(1,128)} %codes.3) | copy-start | bytes 3076
  0.0 10.1 %copy-start.2 = (bf16[1,4,6,2,1024]{4,3,2,1,0:T(2,128)(2,1)S(1)}, bf16[1,4,6,2,1024]{4,3,2,1,0:T(2,128)(2,1)}, u32[]{:S(2)}) copy-start(bf16[1,4,6,2,1024]{4,3,2,1,0:T(2,128)(2,1)} %param.4) | copy-start | bytes 294916
  0.0 17.8 %copy-start.1 = (bf16[2,1024,128]{2,1,0:T(8,128)(2,1)S(1)}, bf16[2,1024,128]{2,1,0:T(8,128)(2,1)}, u32[]{:S(2)}) copy-start(bf16[2,1024,128]{2,1,0:T(8,128)(2,1)} %probes.3) | copy-start | bytes 1572868
  4.9 19.0 %collective-permute-start = (bf16[8,256,128]{2,1,0:T(8,128)(2,1)}, bf16[8,256,128]{2,1,0:T(8,128)(2,1)S(1)}, u32[]{:S(2)}, u32[]{:S(2)}) collective-permute-start(bf16[8,256,128]{2,1,0:T(8,128)(2,1)} %upper.1), channel_id=1, source_target_pairs={{1,0},{2,1},{3,2},{4,3},{5,4},{6,5},{7,6},{8,7},{9,8},{10,9},{11,1... | collective-permute-start | bytes 1572872 | tf_op jit(solution)/shard_map/ppermute | solution.py:402
  10.1 2.1 %copy-start = (bf16[1,160,6,2,1024]{4,3,2,1,0:T(2,128)(2,1)S(1)}, bf16[1,160,6,2,1024]{4,3,2,1,0:T(2,128)(2,1)}, u32[]{:S(2)}) copy-start(bf16[1,160,6,2,1024]{4,3,2,1,0:T(2,128)(2,1)} %param.5) | copy-start | bytes 11796484
  24.6 4.4 %collective-permute-start.1 = (f32[136,128]{1,0:T(8,128)S(1)}, f32[136,128]{1,0:T(8,128)S(1)}, u32[]{:S(2)}, u32[]{:S(2)}) collective-permute-start(f32[136,128]{1,0:T(8,128)S(1)} %get-tuple-element.19), channel_id=1, source_target_pairs={{0,8},{1,9},{2,10},{3,11},{4,12},{5,13},{6,14},{7,15},{8,0},{9,1},... | collective-permute-start | bytes 208904 | tf_op jit(solution)/shard_map/ppermute | solution.py:372
  25.9 4.0 %collective-permute-start.2 = (f32[136,128]{1,0:T(8,128)S(1)}, f32[136,128]{1,0:T(8,128)S(1)}, u32[]{:S(2)}, u32[]{:S(2)}) collective-permute-start(f32[136,128]{1,0:T(8,128)S(1)} %get-tuple-element.18), channel_id=1, source_target_pairs={{0,1},{1,0},{2,3},{3,2},{4,5},{5,4},{6,7},{7,6},{8,9},{9,8},{10,11... | collective-permute-start | bytes 208904 | tf_op jit(solution)/shard_map/ppermute | solution.py:372
  28.9 3.8 %collective-permute-start.3 = (f32[136,128]{1,0:T(8,128)S(1)}, f32[136,128]{1,0:T(8,128)S(1)}, u32[]{:S(2)}, u32[]{:S(2)}) collective-permute-start(f32[136,128]{1,0:T(8,128)S(1)} %get-tuple-element.17), channel_id=1, source_target_pairs={{0,9},{1,8},{2,11},{3,10},{4,13},{5,12},{6,15},{7,14},{8,1},{9,0},... | collective-permute-start | bytes 208904 | tf_op jit(solution)/shard_map/ppermute | solution.py:372
  32.8 5.1 %collective-permute-start.4 = (f32[136,128]{1,0:T(8,128)S(1)}, f32[136,128]{1,0:T(8,128)S(1)}, u32[]{:S(2)}, u32[]{:S(2)}) collective-permute-start(f32[136,128]{1,0:T(8,128)S(1)} %fusion), channel_id=1, source_target_pairs={{0,24},{1,25},{2,26},{3,27},{4,28},{5,29},{6,30},{7,31},{8,16},{9,... | collective-permute-start | bytes 208904 | tf_op jit(solution)/shard_map/ppermute | solution.py:374
  37.8 5.4 %collective-permute-start.5 = (f32[136,128]{1,0:T(8,128)S(1)}, f32[136,128]{1,0:T(8,128)S(1)}, u32[]{:S(2)}, u32[]{:S(2)}) collective-permute-start(f32[136,128]{1,0:T(8,128)S(1)} %add.48), channel_id=1, source_target_pairs={{0,2},{1,3},{2,0},{3,1},{4,6},{5,7},{6,4},{7,5},{8,10},{9,11},{10,... | collective-permute-start | bytes 208904 | tf_op jit(solution)/shard_map/ppermute | solution.py:375
  43.2 5.4 %collective-permute-start.6 = (f32[136,128]{1,0:T(8,128)S(1)}, f32[136,128]{1,0:T(8,128)S(1)}, u32[]{:S(2)}, u32[]{:S(2)}) collective-permute-start(f32[136,128]{1,0:T(8,128)S(1)} %add.49), channel_id=1, source_target_pairs={{0,6},{1,7},{2,4},{3,5},{4,2},{5,3},{6,0},{7,1},{8,14},{9,15},{10,... | collective-permute-start | bytes 208904 | tf_op jit(solution)/shard_map/ppermute | solution.py:376
  48.6 4.7 %collective-permute-start.7 = (f32[136,128]{1,0:T(8,128)S(1)}, f32[136,128]{1,0:T(8,128)S(1)}, u32[]{:S(2)}, u32[]{:S(2)}) collective-permute-start(f32[136,128]{1,0:T(8,128)S(1)} %add.50), channel_id=1, source_target_pairs={{0,8},{1,9},{2,10},{3,11},{4,12},{5,13},{6,14},{7,15},{8,0},{9,1},... | collective-permute-start | bytes 208904 | tf_op jit(solution)/shard_map/ppermute | solution.py:377
  48.7 7.5 %collective-permute-start.9 = (f32[136,128]{1,0:T(8,128)S(1)}, f32[136,128]{1,0:T(8,128)S(1)}, u32[]{:S(2)}, u32[]{:S(2)}) collective-permute-start(f32[136,128]{1,0:T(8,128)S(1)} %add.50), channel_id=1, source_target_pairs={{0,9},{1,8},{2,11},{3,10},{4,13},{5,12},{6,15},{7,14},{8,1},{9,0},... | collective-permute-start | bytes 208904 | tf_op jit(solution)/shard_map/ppermute | solution.py:377
  53.2 3.0 %collective-permute-start.8 = (f32[136,128]{1,0:T(8,128)S(1)}, f32[136,128]{1,0:T(8,128)S(1)}, u32[]{:S(2)}, u32[]{:S(2)}) collective-permute-start(f32[136,128]{1,0:T(8,128)S(1)} %add.50), channel_id=1, source_target_pairs={{0,1},{1,0},{2,3},{3,2},{4,5},{5,4},{6,7},{7,6},{8,9},{9,8},{10,11... | collective-permute-start | bytes 208904 | tf_op jit(solution)/shard_map/ppermute | solution.py:377
